TPU v7x, 32 devices: a whole 2x2x4 slice. The times are simulated.
32 devices in a mesh: pipe: 4 (over y, core), expert: 8 (over z, x).
Axes of the slice: x: 2, y: 2, z: 4, core: 2. Of those that a mesh axis runs over, the one named last changes fastest.
Arguments:
- grad_sent: bfloat16 [4, 1024, 2048], P('pipe', 'expert'), may hold values from -6 to 6
- routes: int32 [4, 1024, 2], P('pipe', 'expert'), may hold values from 0 to 7, all different within a row; in each aligned block of 64 rows (0 to 63, 64 to 127, ..., all dimensions but the last counted through in order) at most 24 rows name the same one
- router_probs: float32 [4, 1024, 8], P('pipe', 'expert'), may hold values from 0.025 to 0.625
- saved_hidden: bfloat16 [4, 3072, 768], P('pipe', 'expert'), may hold values from -6 to 6
- w_down: bfloat16 [8, 768, 2048], P('expert'), may hold values from -0.21875 to 0.21875
- w_router: bfloat16 [2048, 8], replicated, may hold values from -0.125 to 0.125
Outputs:
- d_hidden: bfloat16 [4, 3072, 768], P('pipe', 'expert')
- grad_router_in: bfloat16 [4, 1024, 2048], P('pipe', 'expert')
Inputs may be any that keep to these rules, and one draw needn't show every extreme that they name: `routes`: each token names 2 different experts. In each micro-batch of one device (an aligned block of 64 rows) no expert is named by more than 24 tokens, a bound that some block reaches.
All inputs are finite; a program needn't handle non-finite values.
Results may differ from a plain program's by a relative error of at most 0.0046.
Values may be sent and summed in bfloat16 or wider, within the bound.
No kernel may reach another device: no remote copies, remote signals or barrier semaphores. Data moves between devices by JAX's collectives and lax.ppermute only.
A program may use at most 64 MiB of HBM per device.

v0:
```python
import jax
import jax.numpy as jnp
from jax import lax
from jax.sharding import PartitionSpec as P

TOP = 2
MICRO = 2
MB_TOK = 64


def from_behind(block, axis, distance):
    devices = range(lax.axis_size(axis))
    route = [((i - distance) % len(devices), i) for i in devices]
    return lax.ppermute(block, axis, route)


def route_slots(route_rows, peer_count, capacity):
    onehot = (route_rows[..., None] == jnp.arange(peer_count, dtype=jnp.int32)).astype(jnp.int32)
    rank_of = jnp.sum((jnp.cumsum(onehot, axis=1) - onehot) * onehot, axis=2)
    return route_rows * capacity + rank_of


def on_device(grad_sent, routes, router_probs, saved_hidden, w_down, w_router):
    peer_count = lax.axis_size("expert")
    slot_count = saved_hidden.shape[1]
    capacity = slot_count // (MICRO * peer_count)
    send_width = peer_count * capacity
    model_width = grad_sent.shape[2]
    hidden_width = saved_hidden.shape[2]
    tokens = routes.shape[1]
    incoming = from_behind(grad_sent, "pipe", -1)[0]
    route_rows = routes[0].reshape(MICRO, MB_TOK * TOP)
    position = route_slots(route_rows, peer_count, capacity)
    chosen = jnp.take_along_axis(router_probs[0], routes[0], axis=1)
    weights = chosen / jnp.sum(chosen, axis=1, keepdims=True)
    rounded = weights.astype(jnp.bfloat16)
    micro_index = jnp.arange(MICRO, dtype=jnp.int32)[:, None]
    token_index = jnp.broadcast_to(
        jnp.arange(MB_TOK * TOP, dtype=jnp.int32)[None, :] // TOP, (MICRO, MB_TOK * TOP)
    )
    slot_token = (
        jnp.zeros((MICRO, send_width), jnp.int32).at[micro_index, position].set(token_index)
    )
    slot_used = jnp.zeros((MICRO, send_width), jnp.bool_).at[micro_index, position].set(True)
    send_scale = (
        jnp.zeros((MICRO, send_width), jnp.bfloat16)
        .at[micro_index, position]
        .set(rounded.reshape(MICRO, MB_TOK * TOP))
    )
    micro_grad = incoming.reshape(MICRO, MB_TOK, model_width)
    picked = jnp.take_along_axis(micro_grad, slot_token[..., None], axis=1)
    send_rows = jnp.where(slot_used[..., None], picked, jnp.zeros((), jnp.bfloat16))
    hidden = saved_hidden[0].reshape(MICRO, send_width, hidden_width)
    weight = w_down[0]
    arrived, arrived_scale = (
        lax.all_to_all(send_rows, "expert", split_axis=1, concat_axis=1, tiled=True),
        lax.all_to_all(send_scale, "expert", split_axis=1, concat_axis=1, tiled=True),
    )
    flat_rows = arrived.reshape(-1, model_width)
    flat_saved = hidden.reshape(flat_rows.shape[0], hidden_width)
    grad_hidden = lax.dot_general(
        flat_rows, weight, (((1,), (1,)), ((), ())), preferred_element_type=jnp.float32
    )
    route_grad = jnp.sum(grad_hidden * flat_saved.astype(jnp.float32), axis=1)
    scaled = (arrived_scale.reshape(-1, 1).astype(jnp.float32) * grad_hidden).astype(jnp.bfloat16)
    d_hidden, route_grad = (scaled, route_grad.reshape(arrived_scale.shape))
    returned = lax.all_to_all(route_grad, "expert", split_axis=1, concat_axis=1, tiled=True)
    slot_grad = jnp.take_along_axis(returned, position, axis=1).reshape(tokens, TOP)
    centred = slot_grad - jnp.sum(weights * slot_grad, axis=1, keepdims=True)
    logit_part = weights * centred
    onehot_tok = (routes[0][..., None] == jnp.arange(peer_count, dtype=jnp.int32)).astype(
        jnp.float32
    )
    logit_grad = jnp.sum(logit_part[..., None] * onehot_tok, axis=1)
    grad_in = jnp.dot(logit_grad, w_router.astype(jnp.float32).T, precision=lax.Precision.HIGHEST)
    return (d_hidden.reshape(1, slot_count, hidden_width), grad_in.astype(jnp.bfloat16)[None])


def solution(mesh):
    placed = (
        P("pipe", "expert", None),
        P("pipe", "expert", None),
        P("pipe", "expert", None),
        P("pipe", "expert", None),
        P("expert", None, None),
        P(),
    )
    return jax.shard_map(
        on_device,
        mesh=mesh,
        in_specs=placed,
        out_specs=(P("pipe", "expert", None), P("pipe", "expert", None)),
        check_vma=False,
    )
```

profile of v0, /device:TPU:0, one launch (start us, length us, event | category | flops | bytes accessed | tf_op | source)
XLA Modules:
  0.0 135.3 jit_solution(17531967954192135465)
XLA Ops:
  0.6 0.0 copy-start
  0.6 0.0 copy-start.1
  0.7 2.5 %collective-permute-start = (bf16[1,128,2048]{2,1,0:T(8,128)(2,1)}, bf16[1,128,2048]{2,1,0:T(8,128)(2,1)}, u32[]{:S(2)}, u32[]{:S(2)}) collective-permute-start(bf16[1,128,2048]{2,1,0:T(8,128)(2,1)} %param.6), channel_id=1, source_target_pairs={{8,0},{16,8},{24,16},{0,24},{9,1},{17,9},{25,17},{1,25},{10,2},{18... | collective-permute-start | bytes 1572872 | tf_op jit(solution)/shard_map/ppermute | solution.py:14
  3.1 0.8 copy.50
  3.9 0.7 broadcast_multiply_fusion
  4.6 0.7 fusion.11
  5.3 0.1 eq.28
  5.4 0.1 fusion.5
  5.5 0.2 reduce_window_sum.11
  5.7 0.2 select_reduce_fusion
  5.9 0.1 copy.49
  6.0 0.1 mul.61
  6.1 0.1 copy.51
  6.3 0.1 reshape.232
  6.4 0.0 copy-done.1
  6.4 0.0 copy-start.2
  6.4 1.4 %gather_fusion = f32[256]{0:T(256)S(1)} fusion(f32[128,8]{0,1:T(8,128)S(1)} %bitcast.54, s32[256]{0:T(256)S(1)} %reshape.232), kind=kCustom, calls=%fused_computation | custom fusion | bytes 4096 | tf_op jit(solution)/shard_map/jit(take_along_axis)/gather | solution.py:34
  7.8 0.1 reshape.235
  7.9 0.1 copy.52
  8.0 0.0 copy-done.2
  8.0 0.1 div.27
  8.1 0.1 div.28
  8.2 0.2 div.29
  8.4 12.5 %scatter_fusion = bf16[2,192]{1,0:T(2,128)(2,1)S(1)} fusion(bf16[2,192]{1,0:T(2,128)(2,1)S(1)} %broadcast_in_dim.42, s32[256]{0:T(256)S(1)} %get-tuple-element.9, bf16[256]{0:T(256)(128)(2,1)S(1)} %fusion.14), kind=kCustom, calls=%fused_computation.3 | custom fusion | bytes 3584 | tf_op jit(solution)/shard_map/scatter | solution.py:48
  20.9 0.1 all_to_all.17
  21.0 0.6 copy.53
  21.6 5.8 %all-to-all-start = ((bf16[2,8,24]{2,0,1:T(2,128)(2,1)}), bf16[2,8,24]{2,0,1:T(2,128)(2,1)S(1)}, u32[]{:S(2)}, u32[]{:S(2)}) async-start(bf16[2,8,24]{2,0,1:T(2,128)(2,1)} %copy.53), calls=%async_computation | async-start | bytes 8192 | tf_op jit(solution)/shard_map/all_to_all | solution.py:57
  27.5 12.5 %scatter_fusion.2 = s32[2,192]{1,0:T(2,128)S(1)} fusion(s32[2,192]{1,0:T(2,128)S(1)} %broadcast_in_dim.78, s32[256]{0:T(256)S(1)} %get-tuple-element.9, s32[256]{0:T(256)S(1)} %broadcast_bitcast_fusion), kind=kCustom, calls=%fused_computation.5 | custom fusion | bytes 5120 | tf_op jit(solution)/shard_map/scatter | solution.py:42
  40.0 0.1 reshape.238
  40.1 0.2 copy.56
  40.2 12.7 %scatter_fusion.1 = pred[2,192]{1,0:T(4,128)(4,1)S(1)} fusion(pred[2,192]{1,0:T(4,128)(4,1)S(1)} %broadcast_in_dim.75, s32[256]{0:T(256)S(1)} %get-tuple-element.9, pred[256]{0:T(512)(128)(4,1)S(1)} %broadcast.292), kind=kCustom, calls=%fused_computation.4 | custom fusion | bytes 2816 | tf_op jit(solution)/shard_map/scatter | solution.py:44
  52.9 0.2 copy.55
  53.1 0.0 collective-permute-done
  53.1 16.3 %gather_fusion.1 = bf16[384,2048]{1,0:T(8,128)(2,1)} fusion(bf16[2,64,2048]{2,1,0:T(8,128)(2,1)} %bitcast.8, s32[384]{0:T(512)S(1)} %reshape.238), kind=kCustom, calls=%fused_computation.1 | custom fusion | bytes 3148800 | tf_op jit(solution)/shard_map/jit(take_along_axis)/gather | solution.py:51
  69.4 5.1 %broadcast_select_fusion.1 = bf16[2,192,2048]{2,0,1:T(2,128)(2,1)} fusion(pred[2,192]{0,1:T(8,128)(4,1)S(1)} %copy.55, pred[2,192]{0,1:T(8,128)(4,1)S(1)} %copy.56, bf16[2,192,2048]{2,1,0:T(8,128)(2,1)} %bitcast.55), kind=kLoop, calls=%fused_computation.9 | loop fusion | flops 1572864 | bytes 3146496 | tf_op jit(solution)/shard_map/jit(_where)/select_n | solution.py:52
  74.5 0.0 all-to-all-done
  74.5 6.0 %all-to-all-start.1 = ((bf16[2,192,2048]{2,0,1:T(2,128)(2,1)}), bf16[2,192,2048]{2,0,1:T(2,128)(2,1)}, u32[]{:S(2)}, u32[]{:S(2)}) async-start(bf16[2,192,2048]{2,0,1:T(2,128)(2,1)} %broadcast_select_fusion.1), calls=%async_computation.1 | async-start | bytes 3145728 | tf_op jit(solution)/shard_map/all_to_all | solution.py:56
  80.5 0.1 reshape.230
  80.6 35.4 %all-to-all-done.1 = bf16[2,192,2048]{2,0,1:T(2,128)(2,1)} async-done(((bf16[2,192,2048]{2,0,1:T(2,128)(2,1)}), bf16[2,192,2048]{2,0,1:T(2,128)(2,1)}, u32[]{:S(2)}, u32[]{:S(2)}) %all-to-all-start.1) | async-done | bytes 1572896 | tf_op jit(solution)/shard_map/all_to_all | solution.py:56
  116.0 0.0 copy-start.4
  116.0 2.1 %copy.58 = bf16[2,192,2048]{2,1,0:T(8,128)(2,1)S(1)} copy(bf16[2,192,2048]{2,0,1:T(2,128)(2,1)} %all-to-all-done.1) | data formatting | bytes 3145728 | tf_op jit(solution)/shard_map/all_to_all | solution.py:56
  118.1 0.0 copy-done
  118.1 0.0 copy-done.4
  118.1 0.0 copy-start.3
  118.2 2.3 %fusion.3 = (f32[384]{0:T(512)S(1)}, bf16[1,384,768]{2,1,0:T(8,128)(2,1)}) fusion(bf16[1,384,768]{2,1,0:T(8,128)(2,1)S(1)} %copy-done.4, f32[384]{0:T(512)S(1)} %reshape.230, bf16[384,2048]{1,0:T(8,128)(2,1)S(1)} %bitcast.56, bf16[1,768,2048]{2,1,0:T(8,128)(2,1)S(1)} %copy-done), kind=kOutput, calls=%fused_computation.13 | convolution fusion | flops 1209433728 | bytes 5901312 | tf_op jit(solution)/shard_map/dot_general | solution.py:61
  120.4 0.1 all_to_all.20
  120.5 0.6 copy.60
  121.1 3.4 %all-to-all-start.2 = ((f32[2,8,24]{2,0,1:T(2,128)}), f32[2,8,24]{2,0,1:T(2,128)S(1)}, u32[]{:S(2)}, u32[]{:S(2)}) async-start(f32[2,8,24]{2,0,1:T(2,128)} %copy.60), calls=%async_computation.2 | async-start | bytes 16384 | tf_op jit(solution)/shard_map/all_to_all | solution.py:67
  124.5 0.1 reduce_sum.52
  124.7 0.1 copy.59
  124.7 6.3 %all-to-all-done.2 = f32[2,8,24]{2,0,1:T(2,128)S(1)} async-done(((f32[2,8,24]{2,0,1:T(2,128)}), f32[2,8,24]{2,0,1:T(2,128)S(1)}, u32[]{:S(2)}, u32[]{:S(2)}) %all-to-all-start.2) | async-done | bytes 1568 | tf_op jit(solution)/shard_map/all_to_all | solution.py:67
  131.1 0.1 all_to_all.22
  131.1 2.5 %gather_fusion.2 = f32[256]{0:T(256)S(1)} fusion(f32[2,192]{1,0:T(2,128)S(1)} %all_to_all.22, s32[256]{0:T(256)S(1)} %get-tuple-element.8), kind=kCustom, calls=%fused_computation.2 | custom fusion | bytes 4096 | tf_op jit(solution)/shard_map/jit(take_along_axis)/gather | solution.py:68
  133.6 0.1 gather.20
  133.8 0.1 copy.62
  133.9 0.0 copy-done.3
  133.9 1.4 %fusion.2 = bf16[1,128,2048]{2,1,0:T(8,128)(2,1)} fusion(f32[128,8]{0,1:T(8,128)S(1)} %select_reduce_fusion.1, bf16[2048,8]{0,1:T(8,128)(2,1)S(1)} %copy-done.3), kind=kOutput, calls=%fused_computation.11 | convolution fusion | flops 25427968 | bytes 561152 | tf_op jit(solution)/shard_map/dot_general | solution.py:75
  (16 shorter events, 0.2 us)
Async XLA Ops:
  0.6 117.5 %copy-start = (bf16[1,768,2048]{2,1,0:T(8,128)(2,1)S(1)}, bf16[1,768,2048]{2,1,0:T(8,128)(2,1)}, u32[]{:S(2)}) copy-start(bf16[1,768,2048]{2,1,0:T(8,128)(2,1)} %param.10) | copy-start | bytes 9437188
  0.6 5.8 %copy-start.1 = (f32[1,128,8]{1,2,0:T(8,128)S(1)}, f32[1,128,8]{1,2,0:T(8,128)}, u32[]{:S(2)}) copy-start(f32[1,128,8]{1,2,0:T(8,128)} %param.8) | copy-start | bytes 12292
  0.7 52.4 %collective-permute-start = (bf16[1,128,2048]{2,1,0:T(8,128)(2,1)}, bf16[1,128,2048]{2,1,0:T(8,128)(2,1)}, u32[]{:S(2)}, u32[]{:S(2)}) collective-permute-start(bf16[1,128,2048]{2,1,0:T(8,128)(2,1)} %param.6), channel_id=1, source_target_pairs={{8,0},{16,8},{24,16},{0,24},{9,1},{17,9},{25,17},{1,25},{10,2},{18... | collective-permute-start | bytes 1572872 | tf_op jit(solution)/shard_map/ppermute | solution.py:14
  6.4 1.6 %copy-start.2 = (s32[1,128,2]{1,2,0:T(2,128)S(1)}, s32[1,128,2]{1,2,0:T(2,128)}, u32[]{:S(2)}) copy-start(s32[1,128,2]{1,2,0:T(2,128)} %param.7) | copy-start | bytes 3076
  21.6 52.9 %all-to-all-start = ((bf16[2,8,24]{2,0,1:T(2,128)(2,1)}), bf16[2,8,24]{2,0,1:T(2,128)(2,1)S(1)}, u32[]{:S(2)}, u32[]{:S(2)}) async-start(bf16[2,8,24]{2,0,1:T(2,128)(2,1)} %copy.53), calls=%async_computation | async-start | bytes 8192 | tf_op jit(solution)/shard_map/all_to_all | solution.py:57
  74.5 41.5 %all-to-all-start.1 = ((bf16[2,192,2048]{2,0,1:T(2,128)(2,1)}), bf16[2,192,2048]{2,0,1:T(2,128)(2,1)}, u32[]{:S(2)}, u32[]{:S(2)}) async-start(bf16[2,192,2048]{2,0,1:T(2,128)(2,1)} %broadcast_select_fusion.1), calls=%async_computation.1 | async-start | bytes 3145728 | tf_op jit(solution)/shard_map/all_to_all | solution.py:56
  116.0 2.1 %copy-start.4 = (bf16[1,384,768]{2,1,0:T(8,128)(2,1)S(1)}, bf16[1,384,768]{2,1,0:T(8,128)(2,1)}, u32[]{:S(2)}) copy-start(bf16[1,384,768]{2,1,0:T(8,128)(2,1)} %param.9) | copy-start | bytes 1769476
  118.1 15.8 %copy-start.3 = (bf16[2048,8]{0,1:T(8,128)(2,1)S(1)}, bf16[2048,8]{0,1:T(8,128)(2,1)}, u32[]{:S(2)}) copy-start(bf16[2048,8]{0,1:T(8,128)(2,1)} %param.11) | copy-start | bytes 98308
  121.1 9.9 %all-to-all-start.2 = ((f32[2,8,24]{2,0,1:T(2,128)}), f32[2,8,24]{2,0,1:T(2,128)S(1)}, u32[]{:S(2)}, u32[]{:S(2)}) async-start(f32[2,8,24]{2,0,1:T(2,128)} %copy.60), calls=%async_computation.2 | async-start | bytes 16384 | tf_op jit(solution)/shard_map/all_to_all | solution.py:67
where the time goes:
time: 136 us; the launch traced here: 135 us
  local copies, waits for them, and re-layouts  64.2 us (47%)
  waiting for transfers between devices  41.8 us (31%)
  starting transfers between devices  17.6 us (13%)
  other arithmetic  7.1 us (5%)
  matrix products  3.69 us (3%)
    all_to_all x1, waiting for transfers between devices, on_device(): lax.all_to_all(send_rows, 'expert', split_axis=1, concat_axis=1, tiled=True)  35.4 us
    gather x2, local copies, waits for them, and re-layouts, on_device(): picked = jnp.take_along_axis(micro_grad, slot_token[..., None], axis=1)  16.4 us
    scatter x2, local copies, waits for them, and re-layouts, on_device(): jnp.zeros((MICRO, send_width), jnp.bool_).at[micro_index, position]  12.8 us
    scatter x1, local copies, waits for them, and re-layouts, on_device(): send_scale = jnp.zeros((MICRO, send_width), jnp.bfloat16).at[micro_index,...  12.5 us
    scatter x1, local copies, waits for them, and re-layouts, on_device(): jnp.zeros((MICRO, send_width), jnp.int32).at[micro_index, position]  12.5 us
    all_to_all x1, waiting for transfers between devices, on_device(): lax.all_to_all(route_grad, 'expert', split_axis=1, concat_axis=1, tiled=T...  6.32 us
    all_to_all x1, starting transfers between devices, on_device(): lax.all_to_all(send_rows, 'expert', split_axis=1, concat_axis=1, tiled=True)  5.99 us
    all_to_all x1, starting transfers between devices, on_device(): lax.all_to_all(send_scale, 'expert', split_axis=1, concat_axis=1, tiled=T...  5.8 us
  transfers between devices with their start and end apart: 4, of which 2 were waited for; matrix products, arithmetic and copies ran while one was open for 49% of the time, Pallas kernels for 0%

commit v1 on v0

--- a/solution.py
+++ b/solution.py
@@ -1,11 +1,261 @@
+import functools
+
 import jax
 import jax.numpy as jnp
 from jax import lax
+from jax.experimental import pallas as pl
+from jax.experimental.pallas import tpu as pltpu
 from jax.sharding import PartitionSpec as P
 
 TOP = 2
 MICRO = 2
 MB_TOK = 64
+LANES = 128
+F32, BF16 = jnp.float32, jnp.bfloat16
+VMEM_LIMIT = 40 * 1024 * 1024
+
+
+def iota(shape, axis):
+    return lax.broadcasted_iota(jnp.int32, shape, axis)
+
+
+def info_kernel(routes_ref, probs_ref, info_ref):
+    routes = routes_ref[...]
+    probs = probs_ref[...]
+    expert = iota(probs.shape, 1)
+    first, second = routes[:, 0:1], routes[:, 1:2]
+    p_first = jnp.sum(jnp.where(expert == first, probs, 0.0), axis=1, keepdims=True)
+    p_second = jnp.sum(jnp.where(expert == second, probs, 0.0), axis=1, keepdims=True)
+    total = p_first + p_second
+    lane = iota((routes.shape[0], LANES), 1)
+    table = jnp.where(lane == 0, first.astype(F32), 0.0)
+    table = jnp.where(lane == 1, second.astype(F32), table)
+    table = jnp.where(lane == 2, p_first / total, table)
+    table = jnp.where(lane == 3, p_second / total, table)
+    info_ref[...] = table.T[0:8, :]
+
+
+def ranks(info, expert_rows):
+    first, second = info[0:1, :].astype(jnp.int32), info[1:2, :].astype(jnp.int32)
+    on_first, on_second = expert_rows == first, expert_rows == second
+    named = on_first | on_second
+    before = iota((LANES, LANES), 0)
+    after = iota((LANES, LANES), 1)
+    earlier = ((before < after) & (before // MB_TOK == after // MB_TOK)).astype(F32).astype(BF16)
+    rank = jnp.dot(named.astype(F32).astype(BF16), earlier, preferred_element_type=F32)
+    rank = jnp.where(named, rank.astype(jnp.int32), -1)
+    weight = jnp.where(on_first, info[2:3, :], 0.0) + jnp.where(on_second, info[3:4, :], 0.0)
+    return rank, weight.astype(BF16).astype(F32)
+
+
+def pick(rank_row, weight_row, micro, capacity):
+    slot = iota((capacity, LANES), 0)
+    token = iota((capacity, LANES), 1)
+    hit = (slot == rank_row) & (token // MB_TOK == micro)
+    onehot = jnp.where(hit, 1.0, 0.0)
+    scale = jnp.sum(jnp.where(hit, weight_row, 0.0), axis=1, keepdims=True)
+    return onehot, jnp.broadcast_to(scale, (capacity, LANES))
+
+
+def pack_kernel(half, capacity, plan, me_ref, *refs):
+    n_info = 1 + max(which for which, _ in plan)
+    infos, tokens, outs = refs[:n_info], refs[n_info : n_info + len(plan)], refs[n_info + len(plan) :]
+    me = me_ref[0]
+    rows = jnp.bitwise_xor(me, iota((8, LANES), 0))
+    tables = [ranks(info[...], rows) for info in infos]
+    at = 0
+    for (which, micros), token in zip(plan, tokens):
+        rank, weight = tables[which]
+        pieces, scales = [], []
+        for j in range(half):
+            for micro in micros:
+                onehot, scale = pick(rank[j : j + 1, :], weight[j : j + 1, :], micro, capacity)
+                pieces.append(onehot)
+                scales.append(scale)
+        width = token.shape[0]
+        lead = micros[0] * MB_TOK
+        chosen = jnp.concatenate(pieces, axis=0)[:, lead : lead + width].astype(BF16)
+        packed = jnp.dot(chosen, token[...], preferred_element_type=F32).astype(BF16)
+        size = capacity * len(micros)
+        for j in range(half):
+            outs[j][at : at + size, 0 : token.shape[1]] = packed[j * size : (j + 1) * size]
+            for i in range(len(micros)):
+                outs[j][at + i * capacity : at + (i + 1) * capacity, token.shape[1] :] = scales[
+                    j * len(micros) + i
+                ].astype(BF16)
+        at += size
+
+
+def pack(me, infos, tokens, plan, half, capacity):
+    rows = capacity * sum(len(micros) for _, micros in plan)
+    width = tokens[0].shape[1]
+    block = jax.ShapeDtypeStruct((rows, width + LANES), BF16)
+    vmem = pl.BlockSpec(memory_space=pltpu.VMEM)
+    return pl.pallas_call(
+        functools.partial(pack_kernel, half, capacity, plan),
+        out_shape=[block] * half,
+        in_specs=[pl.BlockSpec(memory_space=pltpu.SMEM)] + [vmem] * (len(infos) + len(tokens)),
+        out_specs=[vmem] * half,
+        compiler_params=pltpu.CompilerParams(vmem_limit_bytes=VMEM_LIMIT),
+    )(me, *infos, *tokens)
+
+
+def expert_kernel(half, capacity, plans, me_ref, *refs):
+    n_blocks = len(plans) * half
+    blocks, (w_ref, saved_ref, d_ref, grad_ref) = refs[:n_blocks], refs[n_blocks : n_blocks + 4]
+    lhs, product, scale, partial = refs[n_blocks + 4 :]
+    me = me_ref[0]
+    peers = 2 * half
+    width = w_ref.shape[1]
+    step = pl.program_id(0)
+
+    places = []
+    at = 0
+    for group, plan in enumerate(plans):
+        for j in range(half):
+            for i, (far, micro) in enumerate(plan):
+                source = jnp.bitwise_xor(me, j + (half if far else 0))
+                places.append((at, group * half + j, i * capacity, source, micro))
+                at += capacity
+
+    @pl.when(step == 0)
+    def _():
+        partial[...] = jnp.zeros_like(partial)
+        start = 0
+        for block in blocks:
+            lhs[start : start + block.shape[0], :] = block[:, 0:width]
+            start += block.shape[0]
+        for _, which, row, source, micro in places:
+            slot = pl.multiple_of((micro * peers + source) * capacity, 8)
+            scale[pl.ds(slot, capacity), :] = blocks[which][row : row + capacity, width:].astype(F32)
+
+    got = lax.dot_general(lhs[...], w_ref[...], (((1,), (1,)), ((), ())), preferred_element_type=F32)
+    for begin, _, _, source, micro in places:
+        slot = pl.multiple_of((micro * peers + source) * capacity, 8)
+        product[pl.ds(slot, capacity), :] = got[begin : begin + capacity, :]
+    total = jnp.zeros((product.shape[0], LANES), F32)
+    for lane in range(0, product.shape[1], LANES):
+        part = product[:, lane : lane + LANES]
+        total = total + part * saved_ref[:, lane : lane + LANES].astype(F32)
+        d_ref[:, lane : lane + LANES] = (scale[...] * part).astype(BF16)
+    for micro in range(MICRO):
+        for source in range(peers):
+            slot, row = (micro * peers + source) * capacity, source * MB_TOK + micro * (MB_TOK // 2)
+            partial[row : row + capacity, :] += total[slot : slot + capacity, :]
+
+    @pl.when(step == pl.num_programs(0) - 1)
+    def _():
+        for pair in range(peers // 2):
+            line = jnp.sum(partial[pair * LANES : (pair + 1) * LANES, :].T, axis=0, keepdims=True)
+            grad_ref[2 * pair : 2 * pair + 2, :] = jnp.broadcast_to(line, (2, LANES))
+
+
+def expert(me, groups, plans, weight, saved, half, capacity):
+    slots, hidden_width = saved.shape
+    width = weight.shape[1]
+    column = 256 if hidden_width % 256 == 0 else hidden_width
+    whole = pl.BlockSpec(memory_space=pltpu.VMEM)
+    return pl.pallas_call(
+        functools.partial(expert_kernel, half, capacity, plans),
+        grid=(hidden_width // column,),
+        out_shape=[
+            jax.ShapeDtypeStruct((slots, hidden_width), BF16),
+            jax.ShapeDtypeStruct((2 * half, LANES), F32),
+        ],
+        in_specs=[pl.BlockSpec(memory_space=pltpu.SMEM)]
+        + [whole] * (len(plans) * half)
+        + [
+            pl.BlockSpec((column, width), lambda i: (i, 0)),
+            pl.BlockSpec((slots, column), lambda i: (0, i)),
+        ],
+        out_specs=[
+            pl.BlockSpec((slots, column), lambda i: (0, i)),
+            pl.BlockSpec((2 * half, LANES), lambda i: (0, 0)),
+        ],
+        scratch_shapes=[
+            pltpu.VMEM((slots, width), BF16),
+            pltpu.VMEM((slots, column), F32),
+            pltpu.VMEM((slots, LANES), F32),
+            pltpu.VMEM((2 * half * MB_TOK, LANES), F32),
+        ],
+        compiler_params=pltpu.CompilerParams(vmem_limit_bytes=VMEM_LIMIT),
+    )(me, *[block for group in groups for block in group], weight, saved)
+
+
+def router_kernel(capacity, me_ref, info_ref, grads_ref, router_ref, out_ref):
+    me = me_ref[0]
+    info = info_ref[...]
+    expert_rows = iota((8, LANES), 0)
+    rank, _ = ranks(info, expert_rows)
+    columns = jnp.concatenate([grads_ref[...], jnp.zeros((LANES - 8, LANES), F32)], axis=0).T
+    columns = jnp.where(lax.rem(me, 2) == 0, columns[0:MB_TOK], columns[MB_TOK:])
+    slot = iota((capacity, LANES), 0)
+    token = iota((capacity, LANES), 1)
+    half = MB_TOK // 2
+    rows = []
+    for e in range(8):
+        here = jnp.where(
+            token // MB_TOK == 0, columns[0:capacity, e : e + 1], columns[half : half + capacity, e : e + 1]
+        )
+        rows.append(jnp.sum(jnp.where(slot == rank[e : e + 1, :], here, 0.0), axis=0, keepdims=True))
+    grads = jnp.concatenate(rows, axis=0)
+    on_first = expert_rows == info[0:1, :].astype(jnp.int32)
+    on_second = expert_rows == info[1:2, :].astype(jnp.int32)
+    w_first, w_second = info[2:3, :], info[3:4, :]
+    g_first = jnp.sum(jnp.where(on_first, grads, 0.0), axis=0, keepdims=True)
+    g_second = jnp.sum(jnp.where(on_second, grads, 0.0), axis=0, keepdims=True)
+    mean = w_first * g_first + w_second * g_second
+    logit = jnp.where(on_first, w_first * (g_first - mean), 0.0)
+    logit = logit + jnp.where(on_second, w_second * (g_second - mean), 0.0)
+    high = logit.astype(BF16).astype(F32)
+    middle = (logit - high).astype(BF16).astype(F32)
+    low = logit - high - middle
+    parts = jnp.concatenate([high, middle, low, jnp.zeros((LANES - 24, LANES), F32)], axis=0).T
+    router = router_ref[...].astype(F32)
+    router = jnp.concatenate([router, router, router, jnp.zeros((LANES - 24, router.shape[1]), F32)], axis=0)
+    out_ref[...] = jnp.dot(parts.astype(BF16), router.astype(BF16), preferred_element_type=F32).astype(BF16)
+
+
+def joint(block, flip, back):
+    sections, peers = lax.axis_size("pipe"), lax.axis_size("expert")
+    route = [
+        (p * peers + e, ((p - back) % sections) * peers + (e ^ flip)) for p in range(sections) for e in range(peers)
+    ]
+    return lax.ppermute(block, ("pipe", "expert"), route)
+
+
+def by_halves(grad_sent, routes, router_probs, saved_hidden, w_down, w_router):
+    peers = lax.axis_size("expert")
+    half = peers // 2
+    capacity = saved_hidden.shape[1] // (MICRO * peers)
+    me = lax.axis_index("expert").astype(jnp.int32).reshape(1)
+    tokens = grad_sent[0]
+    vmem = pl.BlockSpec(memory_space=pltpu.VMEM)
+    far = [joint(tokens[m * MB_TOK : (m + 1) * MB_TOK], half, 1) for m in range(MICRO)]
+    own = joint(tokens, 0, 1)
+    info = pl.pallas_call(
+        info_kernel,
+        out_shape=jax.ShapeDtypeStruct((8, LANES), F32),
+        in_specs=[vmem, vmem],
+        out_specs=vmem,
+    )(routes[0], router_probs[0])
+    far_info = joint(info, half, 0)
+    router = w_router.T
+    early = pack(me, [info, far_info], [own, far[0]], ((0, (0, 1)), (1, (0,))), half, capacity)
+    early = [early[0]] + [joint(early[j], j, 0) for j in range(1, half)]
+    late = pack(me, [far_info], [far[1]], ((0, (1,)),), half, capacity)
+    late = [late[0]] + [joint(late[j], j, 0) for j in range(1, half)]
+    plans = (((False, 0), (False, 1), (True, 0)), ((True, 1),))
+    d_hidden, slot_grad = expert(me, [early, late], plans, w_down[0], saved_hidden[0], half, capacity)
+    returned = lax.all_to_all(slot_grad, "expert", split_axis=0, concat_axis=0, tiled=True)
+    grad_in = pl.pallas_call(
+        functools.partial(router_kernel, capacity),
+        out_shape=jax.ShapeDtypeStruct(tokens.shape, BF16),
+        in_specs=[pl.BlockSpec(memory_space=pltpu.SMEM), vmem, vmem, vmem],
+        out_specs=vmem,
+        compiler_params=pltpu.CompilerParams(vmem_limit_bytes=VMEM_LIMIT),
+    )(me, info, returned, router)
+    return d_hidden[None], grad_in[None]
 
 
 def from_behind(block, axis, distance):
@@ -20,7 +270,7 @@
     return route_rows * capacity + rank_of
 
 
-def on_device(grad_sent, routes, router_probs, saved_hidden, w_down, w_router):
+def by_slots(grad_sent, routes, router_probs, saved_hidden, w_down, w_router):
     peer_count = lax.axis_size("expert")
     slot_count = saved_hidden.shape[1]
     capacity = slot_count // (MICRO * peer_count)
@@ -76,6 +326,14 @@
     return (d_hidden.reshape(1, slot_count, hidden_width), grad_in.astype(jnp.bfloat16)[None])
 
 
+def on_device(*blocks):
+    peers, slots = lax.axis_size("expert"), blocks[3].shape[1]
+    capacity = slots // (MICRO * peers)
+    if peers == 8 and capacity % 8 == 0 and capacity <= MB_TOK // 2:
+        return by_halves(*blocks)
+    return by_slots(*blocks)
+
+
 def solution(mesh):
     placed = (
         P("pipe", "expert", None),

time: 136 us -> 75.6 us (0.56)
  local copies, waits for them, and re-layouts: 64.2 us -> 7.52 us
  blocking collectives: 0 us -> 13.1 us
  waiting for transfers between devices: 41.8 us -> 29.9 us
  Pallas kernels: 0 us -> 7.52 us
  other arithmetic: 7.1 us -> 0 us
  matrix products: 3.69 us -> 0 us
    all_to_all x3 -> x0, waiting for transfers between devices: 41.7 us -> none  [the longest x1 35.4 us: on_device(): lax.all_to_all(send_rows, 'expert', split_axis=1, concat_axis=1, tiled=True)]
    scatter x4 -> x0, local copies, waits for them, and re-layouts: 37.8 us -> none  [the longest x2 12.8 us: on_device(): jnp.zeros((MICRO, send_width), jnp.bool_).at[micro_index, position]]
    ppermute x1 -> x10, waiting for transfers between devices: 0.01 us -> 29.9 us  [joint(): return lax.ppermute(block, ('pipe', 'expert'), route)]
    gather x10 -> x0, local copies, waits for them, and re-layouts: 20.9 us -> none  [the longest x2 16.4 us: on_device(): picked = jnp.take_along_axis(micro_grad, slot_token[..., None], axis=1)]
    all_to_all x3 -> x0, starting transfers between devices: 15.2 us -> none  [the longest x1 5.99 us: on_device(): lax.all_to_all(send_rows, 'expert', split_axis=1, concat_axis=1, tiled=True)]
    ppermute x1 -> x10, starting transfers between devices: 2.46 us -> 16.5 us  [joint(): return lax.ppermute(block, ('pipe', 'expert'), route)]
    all_to_all x0 -> x1, blocking collectives: none -> 13.1 us  [by_halves(): lax.all_to_all(slot_grad, 'expert', split_axis=0, concat_axis=0, tiled=True)]
    pallas_call x0 -> x5, Pallas kernels: none -> 7.52 us  [the longest x1 3.23 us: expert(): pl.pallas_call(functools.partial(expert_kernel, half, capacity, plans), g...]
  transfers between devices with their start and end apart: 4 -> 10, of which waited for: 2 -> 4; matrix products, arithmetic and copies ran while one was open for 49% -> 5% of each run, Pallas kernels for 0% -> 4%
where the time goes in v1:
time: 75.6 us; the launch traced here: 75.2 us
  waiting for transfers between devices  29.9 us (40%)
  starting transfers between devices  16.5 us (22%)
  blocking collectives  13.1 us (17%)
  local copies, waits for them, and re-layouts  7.52 us (10%)
  Pallas kernels  7.52 us (10%)
    ppermute x10, waiting for transfers between devices, joint(): return lax.ppermute(block, ('pipe', 'expert'), route)  29.9 us
    ppermute x10, starting transfers between devices, joint(): return lax.ppermute(block, ('pipe', 'expert'), route)  16.5 us
    all_to_all x1, blocking collectives, by_halves(): lax.all_to_all(slot_grad, 'expert', split_axis=0, concat_axis=0, tiled=True)  13.1 us
    unnamed x12, local copies, waits for them, and re-layouts  6.46 us
    pallas_call x1, Pallas kernels, expert(): pl.pallas_call(functools.partial(expert_kernel, half, capacity, plans), g...  3.23 us
    pallas_call x1, Pallas kernels, by_halves(): pl.pallas_call(info_kernel, out_shape=jax.ShapeDtypeStruct((8, LANES), F3...  1.8 us
  transfers between devices with their start and end apart: 10, of which 4 were waited for; matrix products, arithmetic and copies ran while one was open for 5% of the time, Pallas kernels for 4%

profile of v1, /device:TPU:0, one launch (start us, length us, event | category | flops | bytes accessed | tf_op | source)
XLA Modules:
  0.0 75.2 jit_solution(7693507036378067484)
XLA Ops:
  0.6 2.5 %collective-permute-start.1 = (bf16[128,2048]{1,0:T(8,128)(2,1)}, bf16[128,2048]{1,0:T(8,128)(2,1)S(1)}, u32[]{:S(2)}, u32[]{:S(2)}) collective-permute-start(bf16[128,2048]{1,0:T(8,128)(2,1)} %bitcast.23), channel_id=1, source_target_pairs={{0,24},{1,25},{2,26},{3,27},{4,28},{5,29},{6,30},{7,31},{8,0},{9,1... | collective-permute-start | bytes 1572872 | tf_op jit(solution)/shard_map/ppermute | solution.py:224
  3.1 1.1 %slice_bitcast_fusion = (bf16[64,2048]{1,0:T(8,128)(2,1)S(1)}, bf16[64,2048]{1,0:T(8,128)(2,1)S(1)}) fusion(bf16[1,128,2048]{2,1,0:T(8,128)(2,1)} %param.6), kind=kLoop, calls=%fused_computation | loop fusion | bytes 1048576 | tf_op jit(solution)/shard_map/slice | solution.py:234
  4.2 2.8 %collective-permute-start.2 = (bf16[64,2048]{1,0:T(8,128)(2,1)S(1)}, bf16[64,2048]{1,0:T(8,128)(2,1)S(1)}, u32[]{:S(2)}, u32[]{:S(2)}) collective-permute-start(bf16[64,2048]{1,0:T(8,128)(2,1)S(1)} %get-tuple-element.23), channel_id=1, source_target_pairs={{0,28},{1,29},{2,30},{3,31},{4,24},{5,25},{6,26},{7,27},{8,4},{9,5... | collective-permute-start | bytes 786440 | tf_op jit(solution)/shard_map/ppermute | solution.py:224
  6.9 0.1 collective-permute-start.6
  7.0 1.4 %copy.10 = s32[1,128,2]{2,1,0:T(8,128)} copy(s32[1,128,2]{1,2,0:T(2,128)} %param.7) | data formatting | bytes 2048 | tf_op args[1]
  8.4 1.4 %copy.11 = f32[1,128,8]{2,1,0:T(8,128)} copy(f32[1,128,8]{1,2,0:T(8,128)} %param.8) | data formatting | bytes 8192 | tf_op args[2]
  9.8 1.8 %shard_map.77.refs_0_.info_ref = f32[8,128]{1,0:T(8,128)} custom-call(s32[128,2]{1,0:T(8,128)} %bitcast.24, f32[128,8]{1,0:T(8,128)} %bitcast.25), custom_call_target="tpu_custom_call" | custom-call | tf_op jit(solution)/shard_map/pallas_call | solution.py:236
  11.6 2.5 %collective-permute-start = (f32[8,128]{1,0:T(8,128)}, f32[8,128]{1,0:T(8,128)S(1)}, u32[]{:S(2)}, u32[]{:S(2)}) collective-permute-start(f32[8,128]{1,0:T(8,128)} %shard_map.77.refs_0_.info_ref), channel_id=1, source_target_pairs={{0,4},{1,5},{2,6},{3,7},{4,0},{5,1},{6,2},{7,3},{8,12},{9,13},{10,... | collective-permute-start | bytes 12296 | tf_op jit(solution)/shard_map/ppermute | solution.py:224
  14.1 16.7 %collective-permute-done.refs_1_.refs_0_ = f32[8,128]{1,0:T(8,128)S(1)} collective-permute-done((f32[8,128]{1,0:T(8,128)}, f32[8,128]{1,0:T(8,128)S(1)}, u32[]{:S(2)}, u32[]{:S(2)}) %collective-permute-start) | collective-permute-done | bytes 4128 | tf_op jit(solution)/shard_map/ppermute | solution.py:224
  30.7 0.0 collective-permute-done.2.refs_3_
  30.7 0.0 collective-permute-done.1.refs_2_
  30.7 0.0 copy-start.2
  30.8 0.7 copy-done.2
  31.4 0.0 copy-start.3
  31.4 0.0 copy-start.4
  31.4 0.6 shard_map.78
  32.0 1.6 %collective-permute-start.3 = (bf16[72,2176]{1,0:T(8,128)(2,1)S(1)}, bf16[72,2176]{1,0:T(8,128)(2,1)S(1)}, u32[]{:S(2)}, u32[]{:S(2)}) collective-permute-start(bf16[72,2176]{1,0:T(8,128)(2,1)S(1)} %get-tuple-element.13), channel_id=1, source_target_pairs={{0,1},{1,0},{2,3},{3,2},{4,5},{5,4},{6,7},{7,6},{8,9},{9,8},{10,11... | collective-permute-start | bytes 940040 | tf_op jit(solution)/shard_map/ppermute | solution.py:224
  33.6 0.7 collective-permute-start.4
  34.3 1.3 %collective-permute-start.5 = (bf16[72,2176]{1,0:T(8,128)(2,1)S(1)}, bf16[72,2176]{1,0:T(8,128)(2,1)S(1)}, u32[]{:S(2)}, u32[]{:S(2)}) collective-permute-start(bf16[72,2176]{1,0:T(8,128)(2,1)S(1)} %get-tuple-element.15), channel_id=1, source_target_pairs={{0,3},{1,2},{2,1},{3,0},{4,7},{5,6},{6,5},{7,4},{8,11},{9,10},{10,... | collective-permute-start | bytes 940040 | tf_op jit(solution)/shard_map/ppermute | solution.py:224
  35.6 0.0 collective-permute-done.6.refs_1_
  35.6 0.5 shard_map.79
  36.1 1.6 %collective-permute-start.7 = (bf16[24,2176]{1,0:T(8,128)(2,1)S(1)}, bf16[24,2176]{1,0:T(8,128)(2,1)S(1)}, u32[]{:S(2)}, u32[]{:S(2)}) collective-permute-start(bf16[24,2176]{1,0:T(8,128)(2,1)S(1)} %get-tuple-element.17), channel_id=1, source_target_pairs={{0,1},{1,0},{2,3},{3,2},{4,5},{5,4},{6,7},{7,6},{8,9},{9,8},{10,11... | collective-permute-start | bytes 313352 | tf_op jit(solution)/shard_map/ppermute | solution.py:224
  37.6 0.7 collective-permute-start.8
  38.3 10.5 %collective-permute-done.7.refs_5_ = bf16[24,2176]{1,0:T(8,128)(2,1)S(1)} collective-permute-done((bf16[24,2176]{1,0:T(8,128)(2,1)S(1)}, bf16[24,2176]{1,0:T(8,128)(2,1)S(1)}, u32[]{:S(2)}, u32[]{:S(2)}) %collective-permute-start.7) | collective-permute-done | bytes 104480 | tf_op jit(solution)/shard_map/ppermute | solution.py:224
  48.8 3.0 %collective-permute-start.9 = (bf16[24,2176]{1,0:T(8,128)(2,1)S(1)}, bf16[24,2176]{1,0:T(8,128)(2,1)S(1)}, u32[]{:S(2)}, u32[]{:S(2)}) collective-permute-start(bf16[24,2176]{1,0:T(8,128)(2,1)S(1)} %get-tuple-element.19), channel_id=1, source_target_pairs={{0,3},{1,2},{2,1},{3,0},{4,7},{5,6},{6,5},{7,4},{8,11},{9,10},{10,... | collective-permute-start | bytes 313352 | tf_op jit(solution)/shard_map/ppermute | solution.py:224
  51.8 0.2 collective-permute-done.8.refs_6_
  52.0 2.5 %collective-permute-done.9.refs_7_ = bf16[24,2176]{1,0:T(8,128)(2,1)S(1)} collective-permute-done((bf16[24,2176]{1,0:T(8,128)(2,1)S(1)}, bf16[24,2176]{1,0:T(8,128)(2,1)S(1)}, u32[]{:S(2)}, u32[]{:S(2)}) %collective-permute-start.9) | collective-permute-done | bytes 104480 | tf_op jit(solution)/shard_map/ppermute | solution.py:224
  54.4 0.0 collective-permute-done.3.refs_1_
  54.4 0.0 collective-permute-done.4.refs_2_
  54.4 0.0 collective-permute-done.5.refs_3_
  54.5 0.0 copy-start
  54.5 1.9 %copy-done = bf16[1,768,2048]{2,1,0:T(8,128)(2,1)S(1)} copy-done((bf16[1,768,2048]{2,1,0:T(8,128)(2,1)S(1)}, bf16[1,768,2048]{2,1,0:T(8,128)(2,1)}, u32[]{:S(2)}) %copy-start) | copy-done | bytes 3145752
  56.3 0.0 copy-start.1
  56.3 1.1 %copy-done.1 = bf16[1,384,768]{2,1,0:T(8,128)(2,1)S(1)} copy-done((bf16[1,384,768]{2,1,0:T(8,128)(2,1)S(1)}, bf16[1,384,768]{2,1,0:T(8,128)(2,1)}, u32[]{:S(2)}) %copy-start.1) | copy-done | bytes 589848
  57.4 3.2 %shard_map.80 = (bf16[384,768]{1,0:T(8,128)(2,1)}, f32[8,128]{1,0:T(8,128)S(1)}) custom-call(s32[1]{0:T(128)} %bitcast.me_ref, bf16[72,2176]{1,0:T(8,128)(2,1)S(1)} %get-tuple-element.12.refs_0_, bf16[72,2176]{1,0:T(8,128)(2,1)S(1)} %collective-permute-done.3.refs_1_, bf16[72,2176]{1,0:T(8,128)(2,1)S(1)} %collective-permute-done.4.refs_2_, ...), custom_call_target="tpu_custom_call" | custom-call | tf_op jit(solution)/shard_map/pallas_call | solution.py:158
  60.6 13.1 %all_to_all.11 = f32[8,1,128]{2,1,0:T(1,128)S(1)} all-to-all(f32[8,1,128]{2,1,0:T(1,128)S(1)} %bitcast.21), channel_id=1, replica_groups=mesh['pipe'=4,'expert'=8] {'expert'}, dimensions={0} | all-to-all | bytes 8192 | tf_op jit(solution)/shard_map/all_to_all | solution.py:250
  73.7 0.0 copy-done.3
  73.7 0.0 copy-done.4
  73.7 1.5 %shard_map.81 = bf16[128,2048]{1,0:T(8,128)(2,1)} custom-call(s32[1]{0:T(128)} %bitcast.me_ref, f32[8,128]{1,0:T(8,128)S(1)} %copy-done.3, f32[8,128]{1,0:T(8,128)S(1)} %bitcast.20, bf16[8,2048]{1,0:T(8,128)(2,1)S(1)} %bitcast.19), custom_call_target="tpu_custom_call" | custom-call | tf_op jit(solution)/shard_map/pallas_call | solution.py:251
Async XLA Ops:
  0.6 30.1 %collective-permute-start.1 = (bf16[128,2048]{1,0:T(8,128)(2,1)}, bf16[128,2048]{1,0:T(8,128)(2,1)S(1)}, u32[]{:S(2)}, u32[]{:S(2)}) collective-permute-start(bf16[128,2048]{1,0:T(8,128)(2,1)} %bitcast.23), channel_id=1, source_target_pairs={{0,24},{1,25},{2,26},{3,27},{4,28},{5,29},{6,30},{7,31},{8,0},{9,1... | collective-permute-start | bytes 1572872 | tf_op jit(solution)/shard_map/ppermute | solution.py:224
  4.2 26.6 %collective-permute-start.2 = (bf16[64,2048]{1,0:T(8,128)(2,1)S(1)}, bf16[64,2048]{1,0:T(8,128)(2,1)S(1)}, u32[]{:S(2)}, u32[]{:S(2)}) collective-permute-start(bf16[64,2048]{1,0:T(8,128)(2,1)S(1)} %get-tuple-element.23), channel_id=1, source_target_pairs={{0,28},{1,29},{2,30},{3,31},{4,24},{5,25},{6,26},{7,27},{8,4},{9,5... | collective-permute-start | bytes 786440 | tf_op jit(solution)/shard_map/ppermute | solution.py:224
  6.9 28.7 %collective-permute-start.6 = (bf16[64,2048]{1,0:T(8,128)(2,1)S(1)}, bf16[64,2048]{1,0:T(8,128)(2,1)S(1)}, u32[]{:S(2)}, u32[]{:S(2)}) collective-permute-start(bf16[64,2048]{1,0:T(8,128)(2,1)S(1)} %get-tuple-element.22), channel_id=1, source_target_pairs={{0,28},{1,29},{2,30},{3,31},{4,24},{5,25},{6,26},{7,27},{8,4},{9,5... | collective-permute-start | bytes 786440 | tf_op jit(solution)/shard_map/ppermute | solution.py:224
  11.6 19.1 %collective-permute-start = (f32[8,128]{1,0:T(8,128)}, f32[8,128]{1,0:T(8,128)S(1)}, u32[]{:S(2)}, u32[]{:S(2)}) collective-permute-start(f32[8,128]{1,0:T(8,128)} %shard_map.77.refs_0_.info_ref), channel_id=1, source_target_pairs={{0,4},{1,5},{2,6},{3,7},{4,0},{5,1},{6,2},{7,3},{8,12},{9,13},{10,... | collective-permute-start | bytes 12296 | tf_op jit(solution)/shard_map/ppermute | solution.py:224
  30.7 0.7 copy-start.2
  31.4 42.3 %copy-start.3 = (f32[8,128]{1,0:T(8,128)S(1)}, f32[8,128]{1,0:T(8,128)}, u32[]{:S(2)}) copy-start(f32[8,128]{1,0:T(8,128)} %shard_map.77.refs_0_.info_ref) | copy-start | bytes 12292
  31.4 42.3 %copy-start.4 = (bf16[2048,8]{0,1:T(8,128)(2,1)S(1)}, bf16[2048,8]{0,1:T(8,128)(2,1)}, u32[]{:S(2)}) copy-start(bf16[2048,8]{0,1:T(8,128)(2,1)} %param.11) | copy-start | bytes 98308
  32.0 22.4 %collective-permute-start.3 = (bf16[72,2176]{1,0:T(8,128)(2,1)S(1)}, bf16[72,2176]{1,0:T(8,128)(2,1)S(1)}, u32[]{:S(2)}, u32[]{:S(2)}) collective-permute-start(bf16[72,2176]{1,0:T(8,128)(2,1)S(1)} %get-tuple-element.13), channel_id=1, source_target_pairs={{0,1},{1,0},{2,3},{3,2},{4,5},{5,4},{6,7},{7,6},{8,9},{9,8},{10,11... | collective-permute-start | bytes 940040 | tf_op jit(solution)/shard_map/ppermute | solution.py:224
  33.6 20.9 %collective-permute-start.4 = (bf16[72,2176]{1,0:T(8,128)(2,1)S(1)}, bf16[72,2176]{1,0:T(8,128)(2,1)S(1)}, u32[]{:S(2)}, u32[]{:S(2)}) collective-permute-start(bf16[72,2176]{1,0:T(8,128)(2,1)S(1)} %get-tuple-element.14), channel_id=1, source_target_pairs={{0,2},{1,3},{2,0},{3,1},{4,6},{5,7},{6,4},{7,5},{8,10},{9,11},{10,... | collective-permute-start | bytes 940040 | tf_op jit(solution)/shard_map/ppermute | solution.py:224
  34.3 20.2 %collective-permute-start.5 = (bf16[72,2176]{1,0:T(8,128)(2,1)S(1)}, bf16[72,2176]{1,0:T(8,128)(2,1)S(1)}, u32[]{:S(2)}, u32[]{:S(2)}) collective-permute-start(bf16[72,2176]{1,0:T(8,128)(2,1)S(1)} %get-tuple-element.15), channel_id=1, source_target_pairs={{0,3},{1,2},{2,1},{3,0},{4,7},{5,6},{6,5},{7,4},{8,11},{9,10},{10,... | collective-permute-start | bytes 940040 | tf_op jit(solution)/shard_map/ppermute | solution.py:224
  36.1 12.8 %collective-permute-start.7 = (bf16[24,2176]{1,0:T(8,128)(2,1)S(1)}, bf16[24,2176]{1,0:T(8,128)(2,1)S(1)}, u32[]{:S(2)}, u32[]{:S(2)}) collective-permute-start(bf16[24,2176]{1,0:T(8,128)(2,1)S(1)} %get-tuple-element.17), channel_id=1, source_target_pairs={{0,1},{1,0},{2,3},{3,2},{4,5},{5,4},{6,7},{7,6},{8,9},{9,8},{10,11... | collective-permute-start | bytes 313352 | tf_op jit(solution)/shard_map/ppermute | solution.py:224
  37.6 14.3 %collective-permute-start.8 = (bf16[24,2176]{1,0:T(8,128)(2,1)S(1)}, bf16[24,2176]{1,0:T(8,128)(2,1)S(1)}, u32[]{:S(2)}, u32[]{:S(2)}) collective-permute-start(bf16[24,2176]{1,0:T(8,128)(2,1)S(1)} %get-tuple-element.18), channel_id=1, source_target_pairs={{0,2},{1,3},{2,0},{3,1},{4,6},{5,7},{6,4},{7,5},{8,10},{9,11},{10,... | collective-permute-start | bytes 313352 | tf_op jit(solution)/shard_map/ppermute | solution.py:224
  48.8 5.6 %collective-permute-start.9 = (bf16[24,2176]{1,0:T(8,128)(2,1)S(1)}, bf16[24,2176]{1,0:T(8,128)(2,1)S(1)}, u32[]{:S(2)}, u32[]{:S(2)}) collective-permute-start(bf16[24,2176]{1,0:T(8,128)(2,1)S(1)} %get-tuple-element.19), channel_id=1, source_target_pairs={{0,3},{1,2},{2,1},{3,0},{4,7},{5,6},{6,5},{7,4},{8,11},{9,10},{10,... | collective-permute-start | bytes 313352 | tf_op jit(solution)/shard_map/ppermute | solution.py:224
  54.5 1.9 %copy-start = (bf16[1,768,2048]{2,1,0:T(8,128)(2,1)S(1)}, bf16[1,768,2048]{2,1,0:T(8,128)(2,1)}, u32[]{:S(2)}) copy-start(bf16[1,768,2048]{2,1,0:T(8,128)(2,1)} %param.10) | copy-start | bytes 9437188
  56.3 1.1 %copy-start.1 = (bf16[1,384,768]{2,1,0:T(8,128)(2,1)S(1)}, bf16[1,384,768]{2,1,0:T(8,128)(2,1)}, u32[]{:S(2)}) copy-start(bf16[1,384,768]{2,1,0:T(8,128)(2,1)} %param.9) | copy-start | bytes 1769476

commit v2 on v0

--- a/solution.py
+++ b/solution.py
@@ -1,11 +1,359 @@
+import functools
+
 import jax
 import jax.numpy as jnp
 from jax import lax
+from jax.experimental import pallas as pl
+from jax.experimental.pallas import tpu as pltpu
 from jax.sharding import PartitionSpec as P
 
 TOP = 2
 MICRO = 2
 MB_TOK = 64
+LANES = 128
+F32, BF16 = jnp.float32, jnp.bfloat16
+VMEM_LIMIT = 16 * 1024 * 1024
+
+
+def iota(shape, axis):
+    return lax.broadcasted_iota(jnp.int32, shape, axis)
+
+
+def first_kernel(routes_ref, probs_ref, tokens_ref, info_ref, copy_ref):
+    probs = probs_ref[...]
+    expert = iota(probs.shape, 0)
+    first, second = routes_ref[0:1, :], routes_ref[1:2, :]
+    p_first = jnp.sum(jnp.where(expert == first, probs, 0.0), axis=0, keepdims=True)
+    p_second = jnp.sum(jnp.where(expert == second, probs, 0.0), axis=0, keepdims=True)
+    total = p_first + p_second
+    info_ref[0:1, :] = first.astype(F32)
+    info_ref[1:2, :] = second.astype(F32)
+    info_ref[2:3, :] = p_first / total
+    info_ref[3:4, :] = p_second / total
+    info_ref[4:8, :] = jnp.zeros((4, LANES), F32)
+    copy_ref[...] = tokens_ref[...]
+
+
+def first(routes, probs, tokens):
+    width = tokens.shape[1]
+    return pl.pallas_call(
+        first_kernel,
+        grid=(1,),
+        out_shape=[jax.ShapeDtypeStruct((8, LANES), F32), jax.ShapeDtypeStruct((MB_TOK, width), BF16)],
+        in_specs=[
+            pl.BlockSpec(routes.shape, lambda i: (0, 0)),
+            pl.BlockSpec(probs.shape, lambda i: (0, 0)),
+            pl.BlockSpec((MB_TOK, width), lambda i: (0, 0)),
+        ],
+        out_specs=[pl.BlockSpec((8, LANES), lambda i: (0, 0)), pl.BlockSpec((MB_TOK, width), lambda i: (0, 0))],
+        name="first",
+    )(routes, probs, tokens)
+
+
+def ranks(info, expert_rows):
+    first, second = info[0:1, :].astype(jnp.int32), info[1:2, :].astype(jnp.int32)
+    on_first, on_second = expert_rows == first, expert_rows == second
+    named = on_first | on_second
+    before = iota((LANES, LANES), 0)
+    after = iota((LANES, LANES), 1)
+    earlier = ((before < after) & (before // MB_TOK == after // MB_TOK)).astype(F32).astype(BF16)
+    rank = jnp.dot(named.astype(F32).astype(BF16), earlier, preferred_element_type=F32)
+    rank = jnp.where(named, rank.astype(jnp.int32), -1)
+    weight = jnp.where(on_first, info[2:3, :], 0.0) + jnp.where(on_second, info[3:4, :], 0.0)
+    return rank, weight.astype(BF16).astype(F32)
+
+
+def pick(rank_row, weight_row, micro, capacity):
+    slot = iota((capacity, LANES), 0)
+    token = iota((capacity, LANES), 1)
+    hit = (slot == rank_row) & (token // MB_TOK == micro)
+    onehot = jnp.where(hit, 1.0, 0.0)
+    scale = jnp.sum(jnp.where(hit, weight_row, 0.0), axis=1, keepdims=True)
+    return onehot, jnp.broadcast_to(scale, (capacity, LANES))
+
+
+def pack_kernel(half, capacity, micros, me_ref, info_ref, token_ref, *outs):
+    rows = jnp.bitwise_xor(me_ref[0], iota((8, LANES), 0))
+    rank, weight = ranks(info_ref[...], rows)
+    pieces, scales = [], []
+    for j in range(half):
+        for micro in micros:
+            onehot, scale = pick(rank[j : j + 1, :], weight[j : j + 1, :], micro, capacity)
+            pieces.append(onehot)
+            scales.append(scale)
+    lead, width = micros[0] * MB_TOK, token_ref.shape[1]
+    chosen = jnp.concatenate(pieces, axis=0)[:, lead : lead + token_ref.shape[0]].astype(BF16)
+    packed = jnp.dot(chosen, token_ref[...], preferred_element_type=F32).astype(BF16)
+    size = capacity * len(micros)
+    for j in range(half):
+        outs[j][:, 0:width] = packed[j * size : (j + 1) * size]
+        outs[j][:, width:] = jnp.concatenate(scales[j * len(micros) : (j + 1) * len(micros)], axis=0).astype(BF16)
+
+
+def pack(me, info, tokens, micros, half, capacity, name):
+    block = jax.ShapeDtypeStruct((capacity * len(micros), tokens.shape[1] + LANES), BF16)
+    vmem = pl.BlockSpec(memory_space=pltpu.VMEM)
+    return pl.pallas_call(
+        functools.partial(pack_kernel, half, capacity, micros),
+        out_shape=[block] * half,
+        in_specs=[pl.BlockSpec(memory_space=pltpu.SMEM), vmem, vmem],
+        out_specs=[vmem] * half,
+        compiler_params=pltpu.CompilerParams(vmem_limit_bytes=VMEM_LIMIT),
+        name=name,
+    )(me, info, tokens)
+
+
+def back_kernel(half, capacity, me_ref, saved_ref, w_ref, tokens_ref, *refs):
+    outs, copy_ref, product = refs[:half], refs[half], refs[half + 1]
+    copy_ref[...] = tokens_ref[...]
+    run = half * capacity
+    saved = jnp.concatenate([saved_ref[m, 0] for m in range(MICRO)], axis=0)
+    product[...] = jnp.dot(saved, w_ref[...], preferred_element_type=F32)
+    here = lax.rem(me_ref[0], half)
+    for j in range(half):
+        for m in range(MICRO):
+            slot = pl.multiple_of(m * run + jnp.bitwise_xor(here, j) * capacity, 8)
+            outs[j][m * capacity : (m + 1) * capacity, :] = product[pl.ds(slot, capacity), :].astype(BF16)
+
+
+def back(me, saved, weight, tokens, half, capacity):
+    hidden_width, width = weight.shape
+    column = 512 if width % 512 == 0 else width
+    run = half * capacity
+    block = jax.ShapeDtypeStruct((MICRO * capacity, width), BF16)
+    return pl.pallas_call(
+        functools.partial(back_kernel, half, capacity),
+        grid_spec=pltpu.PrefetchScalarGridSpec(
+            num_scalar_prefetch=1,
+            grid=(width // column,),
+            in_specs=[
+                pl.BlockSpec((MICRO, 1, run, hidden_width), lambda i, me: (0, 1 - me[0] // half, 0, 0)),
+                pl.BlockSpec((hidden_width, column), lambda i, me: (0, i)),
+                pl.BlockSpec((MB_TOK, column), lambda i, me: (1, i)),
+            ],
+            out_specs=[pl.BlockSpec((MICRO * capacity, column), lambda i, me: (0, i))] * half
+            + [pl.BlockSpec((MB_TOK, column), lambda i, me: (0, i))],
+            scratch_shapes=[pltpu.VMEM((MICRO * run, column), F32)],
+        ),
+        out_shape=[block] * half + [jax.ShapeDtypeStruct((MB_TOK, width), BF16)],
+        compiler_params=pltpu.CompilerParams(vmem_limit_bytes=VMEM_LIMIT),
+        name="back",
+    )(me, saved, weight, tokens)
+
+
+def lines(spread):
+    out = []
+    for pair in range(spread.shape[0] // LANES):
+        line = jnp.sum(spread[pair * LANES : (pair + 1) * LANES, :].T, axis=0, keepdims=True)
+        out += [line, line]
+    return jnp.concatenate(out + [jnp.zeros((8 - len(out), LANES), F32)], axis=0)
+
+
+def far_grad_kernel(half, capacity, *refs):
+    blocks, backs = refs[: MICRO * half], refs[MICRO * half : (MICRO + 1) * half]
+    grad_ref, spread = refs[(MICRO + 1) * half :]
+    width = backs[0].shape[1]
+    spread[...] = jnp.zeros_like(spread)
+    for j in range(half):
+        for m in range(MICRO):
+            total = jnp.zeros((capacity, LANES), F32)
+            for lane in range(0, width, LANES):
+                sent = blocks[m * half + j][:, lane : lane + LANES].astype(F32)
+                held = backs[j][m * capacity : (m + 1) * capacity, lane : lane + LANES].astype(F32)
+                total = total + sent * held
+            at = j * MB_TOK + m * (MB_TOK // 2)
+            spread[at : at + capacity, :] = total
+    grad_ref[...] = lines(spread[...])
+
+
+def far_grad(blocks, backs, half, capacity):
+    vmem = pl.BlockSpec(memory_space=pltpu.VMEM)
+    return pl.pallas_call(
+        functools.partial(far_grad_kernel, half, capacity),
+        out_shape=jax.ShapeDtypeStruct((8, LANES), F32),
+        in_specs=[vmem] * (len(blocks) + len(backs)),
+        out_specs=vmem,
+        scratch_shapes=[pltpu.VMEM((half * MB_TOK, LANES), F32)],
+        compiler_params=pltpu.CompilerParams(vmem_limit_bytes=VMEM_LIMIT),
+        name="far_grad",
+    )(*blocks, *backs)
+
+
+def expert_kernel(half, capacity, plans, graded, me_ref, *refs):
+    n_blocks = len(plans) * half
+    blocks, (w_ref, saved_ref), refs = refs[:n_blocks], refs[n_blocks : n_blocks + 2], refs[n_blocks + 2 :]
+    if graded:
+        d_ref, grad_ref, lhs, product, scale, partial = refs
+    else:
+        _, d_ref, lhs, product, scale = refs
+    width = w_ref.shape[1]
+    run = half * capacity
+    here = lax.rem(me_ref[0], half)
+    step = pl.program_id(0)
+    places = []
+    at = 0
+    for group, plan in enumerate(plans):
+        for j in range(half):
+            for i, micro in enumerate(plan):
+                slot = pl.multiple_of(micro * run + jnp.bitwise_xor(here, j) * capacity, 8)
+                places.append((at, group * half + j, i * capacity, slot, j, micro))
+                at += capacity
+
+    @pl.when(step == 0)
+    def _():
+        start = 0
+        for block in blocks:
+            lhs[start : start + block.shape[0], :] = block[:, 0:width]
+            start += block.shape[0]
+        for _, which, row, slot, _, _ in places:
+            scale[pl.ds(slot, capacity), :] = blocks[which][row : row + capacity, width:].astype(F32)
+        if graded:
+            partial[...] = jnp.zeros_like(partial)
+
+    got = lax.dot_general(lhs[...], w_ref[...], (((1,), (1,)), ((), ())), preferred_element_type=F32)
+    for begin, _, _, slot, _, _ in places:
+        product[pl.ds(slot, capacity), :] = got[begin : begin + capacity, :]
+    for lane in range(0, product.shape[1], LANES):
+        part = (scale[...] * product[:, lane : lane + LANES]).astype(BF16)
+        for micro in range(MICRO):
+            d_ref[micro, 0, :, lane : lane + LANES] = part[micro * run : (micro + 1) * run]
+    if graded:
+        total = jnp.zeros((MICRO * run, LANES), F32)
+        for lane in range(0, product.shape[1], LANES):
+            held = jnp.concatenate([saved_ref[m, 0, :, lane : lane + LANES] for m in range(MICRO)], axis=0)
+            total = total + product[:, lane : lane + LANES] * held.astype(F32)
+        product[:, 0:LANES] = total
+        for _, _, _, slot, j, micro in places:
+            row = j * MB_TOK + micro * (MB_TOK // 2)
+            partial[row : row + capacity, :] += product[pl.ds(slot, capacity), 0:LANES]
+
+        @pl.when(step == pl.num_programs(0) - 1)
+        def _():
+            grad_ref[...] = lines(partial[...])
+
+
+def expert(me, groups, plans, weight, saved, half, capacity, held=None):
+    hidden_width, width = weight.shape
+    column = 256 if hidden_width % 256 == 0 else hidden_width
+    run = half * capacity
+    graded = held is None
+    whole = pl.BlockSpec(memory_space=pltpu.VMEM)
+    side = (lambda me: me[0] // half) if graded else (lambda me: 1 - me[0] // half)
+    slots = pl.BlockSpec((MICRO, 1, run, column), lambda i, me: (0, side(me), 0, i))
+    operands = [block for group in groups for block in group] + [weight, saved]
+    in_specs = [whole] * (len(plans) * half) + [pl.BlockSpec((column, width), lambda i, me: (i, 0)), slots]
+    out_shape, out_specs = [jax.ShapeDtypeStruct(saved.shape, BF16)], [slots]
+    scratch = [
+        pltpu.VMEM((MICRO * run, width), BF16),
+        pltpu.VMEM((MICRO * run, column), F32),
+        pltpu.VMEM((MICRO * run, LANES), F32),
+    ]
+    aliases = {}
+    if graded:
+        out_shape.append(jax.ShapeDtypeStruct((8, LANES), F32))
+        out_specs.append(pl.BlockSpec((8, LANES), lambda i, me: (0, 0)))
+        scratch.append(pltpu.VMEM((half * MB_TOK, LANES), F32))
+    else:
+        operands.append(held)
+        in_specs.append(pl.BlockSpec(memory_space=pl.ANY))
+        aliases = {len(operands): 0}
+    return pl.pallas_call(
+        functools.partial(expert_kernel, half, capacity, plans, graded),
+        grid_spec=pltpu.PrefetchScalarGridSpec(
+            num_scalar_prefetch=1,
+            grid=(hidden_width // column,),
+            in_specs=in_specs,
+            out_specs=out_specs,
+            scratch_shapes=scratch,
+        ),
+        out_shape=out_shape,
+        input_output_aliases=aliases,
+        compiler_params=pltpu.CompilerParams(vmem_limit_bytes=VMEM_LIMIT),
+        name="expert_own" if graded else "expert_far",
+    )(me, *operands)
+
+
+def router_kernel(half, capacity, me_ref, info_ref, *refs):
+    own, (far_ref, router_ref, out_ref) = refs[:half], refs[half:]
+    info = info_ref[...]
+    rank, _ = ranks(info, jnp.bitwise_xor(me_ref[0], iota((8, LANES), 0)))
+    grads = [own[j][j : j + 1, :] for j in range(half)] + [far_ref[0:half, :]]
+    columns = jnp.concatenate(grads + [jnp.zeros((LANES - 2 * half, LANES), F32)], axis=0).T
+    slot = iota((capacity, LANES), 0)
+    token = iota((capacity, LANES), 1)
+    rows = []
+    for j in range(2 * half):
+        at = (j % 2) * MB_TOK
+        second = at + MB_TOK // 2
+        here = jnp.where(
+            token // MB_TOK == 0, columns[at : at + capacity, j : j + 1], columns[second : second + capacity, j : j + 1]
+        )
+        rows.append(jnp.sum(jnp.where(slot == rank[j : j + 1, :], here, 0.0), axis=0, keepdims=True))
+    grads = jnp.concatenate(rows, axis=0)
+    first, second = info[0:1, :].astype(jnp.int32), info[1:2, :].astype(jnp.int32)
+    w_first, w_second = info[2:3, :], info[3:4, :]
+    relative = jnp.bitwise_xor(me_ref[0], iota((8, LANES), 0))
+    g_first = jnp.sum(jnp.where(relative == first, grads, 0.0), axis=0, keepdims=True)
+    g_second = jnp.sum(jnp.where(relative == second, grads, 0.0), axis=0, keepdims=True)
+    mean = w_first * g_first + w_second * g_second
+    expert_rows = iota((8, LANES), 0)
+    logit = jnp.where(expert_rows == first, w_first * (g_first - mean), 0.0)
+    logit = logit + jnp.where(expert_rows == second, w_second * (g_second - mean), 0.0)
+    high = logit.astype(BF16).astype(F32)
+    middle = (logit - high).astype(BF16).astype(F32)
+    low = logit - high - middle
+    parts = jnp.concatenate([high, middle, low, jnp.zeros((LANES - 24, LANES), F32)], axis=0).T
+    router = router_ref[...].astype(F32)
+    router = jnp.concatenate([router, router, router, jnp.zeros((LANES - 24, router.shape[1]), F32)], axis=0)
+    out_ref[...] = jnp.dot(parts.astype(BF16), router.astype(BF16), preferred_element_type=F32).astype(BF16)
+
+
+def route(block, flip, back):
+    sections, peers = lax.axis_size("pipe"), lax.axis_size("expert")
+    pairs = [
+        (p * peers + e, ((p - back) % sections) * peers + (e ^ flip)) for p in range(sections) for e in range(peers)
+    ]
+    return lax.ppermute(block, ("pipe", "expert"), pairs)
+
+
+def by_halves(grad_sent, routes, router_probs, saved_hidden, w_down, w_router):
+    peers = lax.axis_size("expert")
+    half = peers // 2
+    slots, hidden_width = saved_hidden.shape[1:]
+    capacity = slots // (MICRO * peers)
+    me = lax.axis_index("expert").astype(jnp.int32).reshape(1)
+    tokens, weight = grad_sent[0], w_down[0]
+    saved = saved_hidden.reshape(MICRO, 2, half * capacity, hidden_width)
+    vmem = pl.BlockSpec(memory_space=pltpu.VMEM)
+
+    def spread(blocks):
+        return [blocks[0]] + [route(blocks[j], j, 0) for j in range(1, half)]
+
+    info, first_tokens = first(routes[0].T, router_probs[0].T, tokens)
+    far_first = route(first_tokens, half, 1)
+    own = route(tokens, 0, 1)
+    far_info = route(info, half, 0)
+    *backs, second_tokens = back(me, saved, weight, tokens, half, capacity)
+    far_second = route(second_tokens, half, 1)
+    backs = spread(backs)
+    own_blocks = spread(pack(me, info, own, (0, 1), half, capacity, "pack_own"))
+    early = pack(me, far_info, far_first, (0,), half, capacity, "pack_early")
+    early_blocks = spread(early)
+    held, own_grad = expert(me, [own_blocks], ((0, 1),), weight, saved, half, capacity)
+    own_grads = [own_grad] + [route(own_grad, j, 0) for j in range(1, half)]
+    late = pack(me, far_info, far_second, (1,), half, capacity, "pack_late")
+    late_blocks = spread(late)
+    far_grads = route(far_grad([*early, *late], backs, half, capacity), half, 0)
+    (d_hidden,) = expert(me, [early_blocks, late_blocks], ((0,), (1,)), weight, saved, half, capacity, held)
+    grad_in = pl.pallas_call(
+        functools.partial(router_kernel, half, capacity),
+        out_shape=jax.ShapeDtypeStruct(tokens.shape, BF16),
+        in_specs=[pl.BlockSpec(memory_space=pltpu.SMEM)] + [vmem] * (half + 3),
+        out_specs=vmem,
+        compiler_params=pltpu.CompilerParams(vmem_limit_bytes=VMEM_LIMIT),
+        name="router",
+    )(me, info, *own_grads, far_grads, w_router.T)
+    return d_hidden.reshape(saved_hidden.shape), grad_in[None]
 
 
 def from_behind(block, axis, distance):
@@ -20,7 +368,7 @@
     return route_rows * capacity + rank_of
 
 
-def on_device(grad_sent, routes, router_probs, saved_hidden, w_down, w_router):
+def by_slots(grad_sent, routes, router_probs, saved_hidden, w_down, w_router):
     peer_count = lax.axis_size("expert")
     slot_count = saved_hidden.shape[1]
     capacity = slot_count // (MICRO * peer_count)
@@ -76,6 +424,14 @@
     return (d_hidden.reshape(1, slot_count, hidden_width), grad_in.astype(jnp.bfloat16)[None])
 
 
+def on_device(*blocks):
+    peers, slots = lax.axis_size("expert"), blocks[3].shape[1]
+    capacity = slots // (MICRO * peers)
+    if peers == 8 and capacity % 8 == 0 and capacity <= MB_TOK // 2:
+        return by_halves(*blocks)
+    return by_slots(*blocks)
+
+
 def solution(mesh):
     placed = (
         P("pipe", "expert", None),

time: 136 us -> 78.5 us (0.58)
  local copies, waits for them, and re-layouts: 64.2 us -> 8.08 us
  waiting for transfers between devices: 41.8 us -> 25.1 us
  Pallas kernels: 0 us -> 14.6 us
  starting transfers between devices: 17.6 us -> 29.5 us
  other arithmetic: 7.1 us -> 0 us
  matrix products: 3.69 us -> 0 us
    all_to_all x3 -> x0, waiting for transfers between devices: 41.7 us -> none  [the longest x1 35.4 us: on_device(): lax.all_to_all(send_rows, 'expert', split_axis=1, concat_axis=1, tiled=True)]
    scatter x4 -> x0, local copies, waits for them, and re-layouts: 37.8 us -> none  [the longest x2 12.8 us: on_device(): jnp.zeros((MICRO, send_width), jnp.bool_).at[micro_index, position]]
    ppermute x1 -> x20, starting transfers between devices: 2.46 us -> 29.5 us  [route(): return lax.ppermute(block, ('pipe', 'expert'), pairs)]
    ppermute x1 -> x20, waiting for transfers between devices: 0.01 us -> 25.1 us  [route(): return lax.ppermute(block, ('pipe', 'expert'), pairs)]
    gather x10 -> x0, local copies, waits for them, and re-layouts: 20.9 us -> none  [the longest x2 16.4 us: on_device(): picked = jnp.take_along_axis(micro_grad, slot_token[..., None], axis=1)]
    all_to_all x3 -> x0, starting transfers between devices: 15.2 us -> none  [the longest x1 5.99 us: on_device(): lax.all_to_all(send_rows, 'expert', split_axis=1, concat_axis=1, tiled=True)]
    pallas_call x0 -> x9, Pallas kernels: none -> 14.6 us  [the longest x2 5.05 us: expert(): pl.pallas_call(functools.partial(expert_kernel, half, capacity, plans, gr...]
    unnamed x11 -> x24, local copies, waits for them, and re-layouts: 0.81 us -> 8.08 us
  transfers between devices with their start and end apart: 4 -> 20, of which waited for: 2 -> 3; matrix products, arithmetic and copies ran while one was open for 49% -> 0% of each run, Pallas kernels for 0% -> 17%
where the time goes in v2:
time: 78.5 us; the launch traced here: 78.1 us
  starting transfers between devices  29.5 us (38%)
  waiting for transfers between devices  25.1 us (32%)
  Pallas kernels  14.6 us (19%)
  local copies, waits for them, and re-layouts  8.08 us (10%)
    ppermute x20, starting transfers between devices, route(): return lax.ppermute(block, ('pipe', 'expert'), pairs)  29.5 us
    ppermute x20, waiting for transfers between devices, route(): return lax.ppermute(block, ('pipe', 'expert'), pairs)  25.1 us
    unnamed x24, local copies, waits for them, and re-layouts  8.08 us
    pallas_call x2, Pallas kernels, expert(): pl.pallas_call(functools.partial(expert_kernel, half, capacity, plans, gr...  5.05 us
    pallas_call x1, Pallas kernels, back(): pl.pallas_call(functools.partial(back_kernel, half, capacity), grid_spec=...  2.75 us
    pallas_call x3, Pallas kernels, pack(): pl.pallas_call(functools.partial(pack_kernel, half, capacity, micros), ou...  2.35 us
    pallas_call x1, Pallas kernels, first(): pl.pallas_call(first_kernel, grid=(1,), out_shape=[jax.ShapeDtypeStruct((...  1.7 us
  transfers between devices with their start and end apart: 20, of which 3 were waited for; matrix products, arithmetic and copies ran while one was open for 0% of the time, Pallas kernels for 17%

profile of v2, /device:TPU:0, one launch (start us, length us, event | category | flops | bytes accessed | tf_op | source)
XLA Modules:
  0.0 78.1 jit_solution(13901116901746815391)
XLA Ops:
  0.6 2.5 %collective-permute-start.9 = (bf16[128,2048]{1,0:T(8,128)(2,1)}, bf16[128,2048]{1,0:T(8,128)(2,1)}, u32[]{:S(2)}, u32[]{:S(2)}) collective-permute-start(bf16[128,2048]{1,0:T(8,128)(2,1)} %bitcast.19), channel_id=1, source_target_pairs={{0,24},{1,25},{2,26},{3,27},{4,28},{5,29},{6,30},{7,31},{8,0},{9,1... | collective-permute-start | bytes 1572872 | tf_op jit(solution)/shard_map/ppermute | solution.py:316
  3.1 0.0 copy-start
  3.1 1.9 %copy-done = bf16[1,768,2048]{2,1,0:T(8,128)(2,1)S(1)} copy-done((bf16[1,768,2048]{2,1,0:T(8,128)(2,1)S(1)}, bf16[1,768,2048]{2,1,0:T(8,128)(2,1)}, u32[]{:S(2)}) %copy-start) | copy-done | bytes 3145752
  5.0 1.1 %copy-done.2 = bf16[1,384,768]{2,1,0:T(8,128)(2,1)S(1)} copy-done((bf16[1,384,768]{2,1,0:T(8,128)(2,1)S(1)}, bf16[1,384,768]{2,1,0:T(8,128)(2,1)}, u32[]{:S(2)}) %copy-start.2) | copy-done | bytes 589848
  6.0 1.0 %copy-done.5 = bf16[1,128,2048]{2,1,0:T(8,128)(2,1)S(1)} copy-done((bf16[1,128,2048]{2,1,0:T(8,128)(2,1)S(1)}, bf16[1,128,2048]{2,1,0:T(8,128)(2,1)}, u32[]{:S(2)}) %copy-start.5) | copy-done | bytes 524312
  7.1 2.7 %back.1 = (bf16[48,2048]{1,0:T(8,128)(2,1)S(1)}, bf16[48,2048]{1,0:T(8,128)(2,1)}, bf16[48,2048]{1,0:T(8,128)(2,1)}, bf16[48,2048]{1,0:T(8,128)(2,1)S(1)}, bf16[64,2048]{1,0:T(8,128)(2,1)}) custom-call(s32[1]{0:T(128)} %bitcast.me_ref, bf16[2,2,96,768]{3,2,1,0:T(8,128)(2,1)S(1)} %bitcast.16, bf16[768,2048]{1,0:T(8,128)(2,1)S(1)} %bitcast.13, ...), custom_call_target="tpu_custom_call" | custom-call | tf_op jit(solution)/shard_map/back/pallas_call | solution.py:124
  9.8 0.7 copy-done.6
  10.5 0.7 copy-done.11
  11.2 2.7 %collective-permute-start.5 = (bf16[64,2048]{1,0:T(8,128)(2,1)}, bf16[64,2048]{1,0:T(8,128)(2,1)S(1)}, u32[]{:S(2)}, u32[]{:S(2)}) collective-permute-start(bf16[64,2048]{1,0:T(8,128)(2,1)} %get-tuple-element.29), channel_id=1, source_target_pairs={{0,28},{1,29},{2,30},{3,31},{4,24},{5,25},{6,26},{7,27},{8,4},{9,5... | collective-permute-start | bytes 786440 | tf_op jit(solution)/shard_map/ppermute | solution.py:316
  13.9 1.5 %collective-permute-start.16 = (bf16[48,2048]{1,0:T(8,128)(2,1)}, bf16[48,2048]{1,0:T(8,128)(2,1)}, u32[]{:S(2)}, u32[]{:S(2)}) collective-permute-start(bf16[48,2048]{1,0:T(8,128)(2,1)} %get-tuple-element.41), channel_id=1, source_target_pairs={{0,1},{1,0},{2,3},{3,2},{4,5},{5,4},{6,7},{7,6},{8,9},{9,8},{10,11... | collective-permute-start | bytes 589832 | tf_op jit(solution)/shard_map/ppermute | solution.py:316
  15.4 1.6 %collective-permute-start.17 = (bf16[48,2048]{1,0:T(8,128)(2,1)}, bf16[48,2048]{1,0:T(8,128)(2,1)}, u32[]{:S(2)}, u32[]{:S(2)}) collective-permute-start(bf16[48,2048]{1,0:T(8,128)(2,1)} %get-tuple-element.42), channel_id=1, source_target_pairs={{0,2},{1,3},{2,0},{3,1},{4,6},{5,7},{6,4},{7,5},{8,10},{9,11},{10,... | collective-permute-start | bytes 589832 | tf_op jit(solution)/shard_map/ppermute | solution.py:316
  17.0 1.7 %first.1 = (f32[8,128]{1,0:T(8,128)}, bf16[64,2048]{1,0:T(8,128)(2,1)}) custom-call(s32[2,128]{1,0:T(2,128)} %bitcast.26, f32[8,128]{1,0:T(8,128)} %bitcast.25, bf16[128,2048]{1,0:T(8,128)(2,1)} %bitcast.20), custom_call_target="tpu_custom_call" | custom-call | tf_op jit(solution)/shard_map/first/pallas_call | solution.py:39
  18.7 0.0 collective-permute-start.1
  18.7 0.0 collective-permute-done.9.token_ref
  18.7 2.0 %collective-permute-start = (f32[8,128]{1,0:T(8,128)}, f32[8,128]{1,0:T(8,128)S(1)}, u32[]{:S(2)}, u32[]{:S(2)}) collective-permute-start(f32[8,128]{1,0:T(8,128)} %get-tuple-element.23.info_ref), channel_id=1, source_target_pairs={{0,4},{1,5},{2,6},{3,7},{4,0},{5,1},{6,2},{7,3},{8,12},{9,13},{10,... | collective-permute-start | bytes 12296 | tf_op jit(solution)/shard_map/ppermute | solution.py:316
  20.7 0.7 copy-done.9
  21.4 1.5 %pack_own.1 = (bf16[48,2176]{1,0:T(8,128)(2,1)S(1)}, bf16[48,2176]{1,0:T(8,128)(2,1)S(1)}, bf16[48,2176]{1,0:T(8,128)(2,1)S(1)}, bf16[48,2176]{1,0:T(8,128)(2,1)S(1)}) custom-call(s32[1]{0:T(128)} %bitcast.me_ref, f32[8,128]{1,0:T(8,128)S(1)} %copy-done.9, bf16[128,2048]{1,0:T(8,128)(2,1)} %collective-permute-done.9.token_ref), custom_call_target="tpu_custom_call" | custom-call | tf_op jit(solution)/shard_map/pack_own/pallas_call | solution.py:96
  22.9 15.1 %collective-permute-done.info_ref = f32[8,128]{1,0:T(8,128)S(1)} collective-permute-done((f32[8,128]{1,0:T(8,128)}, f32[8,128]{1,0:T(8,128)S(1)}, u32[]{:S(2)}, u32[]{:S(2)}) %collective-permute-start) | collective-permute-done | bytes 4128 | tf_op jit(solution)/shard_map/ppermute | solution.py:316
  38.0 1.5 %collective-permute-start.10 = (bf16[48,2176]{1,0:T(8,128)(2,1)S(1)}, bf16[48,2176]{1,0:T(8,128)(2,1)S(1)}, u32[]{:S(2)}, u32[]{:S(2)}) collective-permute-start(bf16[48,2176]{1,0:T(8,128)(2,1)S(1)} %get-tuple-element.35), channel_id=1, source_target_pairs={{0,1},{1,0},{2,3},{3,2},{4,5},{5,4},{6,7},{7,6},{8,9},{9,8},{10,11... | collective-permute-start | bytes 626696 | tf_op jit(solution)/shard_map/ppermute | solution.py:316
  39.5 0.0 collective-permute-done.16.refs_9_
  39.5 0.7 collective-permute-start.11
  40.2 0.0 collective-permute-done.17.refs_10_
  40.2 1.3 %collective-permute-start.12 = (bf16[48,2176]{1,0:T(8,128)(2,1)S(1)}, bf16[48,2176]{1,0:T(8,128)(2,1)S(1)}, u32[]{:S(2)}, u32[]{:S(2)}) collective-permute-start(bf16[48,2176]{1,0:T(8,128)(2,1)S(1)} %get-tuple-element.37), channel_id=1, source_target_pairs={{0,3},{1,2},{2,1},{3,0},{4,7},{5,6},{6,5},{7,4},{8,11},{9,10},{10,... | collective-permute-start | bytes 626696 | tf_op jit(solution)/shard_map/ppermute | solution.py:316
  41.5 0.0 collective-permute-done.5.token_ref
  41.5 1.6 %collective-permute-start.18 = (bf16[48,2048]{1,0:T(8,128)(2,1)}, bf16[48,2048]{1,0:T(8,128)(2,1)S(1)}, u32[]{:S(2)}, u32[]{:S(2)}) collective-permute-start(bf16[48,2048]{1,0:T(8,128)(2,1)} %copy-done.11), channel_id=1, source_target_pairs={{0,3},{1,2},{2,1},{3,0},{4,7},{5,6},{6,5},{7,4},{8,11},{9,10},{10,... | collective-permute-start | bytes 589832 | tf_op jit(solution)/shard_map/ppermute | solution.py:316
  43.1 0.5 pack_late.1
  43.6 0.0 collective-permute-done.1.token_ref
  43.6 0.6 collective-permute-start.6
  44.2 0.4 pack_early.1
  44.6 0.0 copy-start.4
  44.6 9.8 %collective-permute-done.18.refs_11_ = bf16[48,2048]{1,0:T(8,128)(2,1)S(1)} collective-permute-done((bf16[48,2048]{1,0:T(8,128)(2,1)}, bf16[48,2048]{1,0:T(8,128)(2,1)S(1)}, u32[]{:S(2)}, u32[]{:S(2)}) %collective-permute-start.18) | collective-permute-done | bytes 196640 | tf_op jit(solution)/shard_map/ppermute | solution.py:316
  54.4 1.3 %collective-permute-start.7 = (bf16[24,2176]{1,0:T(8,128)(2,1)S(1)}, bf16[24,2176]{1,0:T(8,128)(2,1)S(1)}, u32[]{:S(2)}, u32[]{:S(2)}) collective-permute-start(bf16[24,2176]{1,0:T(8,128)(2,1)S(1)} %get-tuple-element.32.refs_6_), channel_id=1, source_target_pairs={{0,2},{1,3},{2,0},{3,1},{4,6},{5,7},{6,4},{7,5},{8,10},{9,11},{10,... | collective-permute-start | bytes 313352 | tf_op jit(solution)/shard_map/ppermute | solution.py:316
  55.8 0.0 collective-permute-done.6.refs_5_
  55.8 1.9 %collective-permute-start.8 = (bf16[24,2176]{1,0:T(8,128)(2,1)S(1)}, bf16[24,2176]{1,0:T(8,128)(2,1)S(1)}, u32[]{:S(2)}, u32[]{:S(2)}) collective-permute-start(bf16[24,2176]{1,0:T(8,128)(2,1)S(1)} %get-tuple-element.33.refs_7_), channel_id=1, source_target_pairs={{0,3},{1,2},{2,1},{3,0},{4,7},{5,6},{6,5},{7,4},{8,11},{9,10},{10,... | collective-permute-start | bytes 313352 | tf_op jit(solution)/shard_map/ppermute | solution.py:316
  57.6 0.0 collective-permute-done.10.refs_1_
  57.6 0.6 collective-permute-start.2
  58.2 0.0 collective-permute-done.11.refs_2_
  58.2 1.0 %collective-permute-start.3 = (bf16[24,2176]{1,0:T(8,128)(2,1)S(1)}, bf16[24,2176]{1,0:T(8,128)(2,1)S(1)}, u32[]{:S(2)}, u32[]{:S(2)}) collective-permute-start(bf16[24,2176]{1,0:T(8,128)(2,1)S(1)} %get-tuple-element.27.refs_2_), channel_id=1, source_target_pairs={{0,2},{1,3},{2,0},{3,1},{4,6},{5,7},{6,4},{7,5},{8,10},{9,11},{10,... | collective-permute-start | bytes 313352 | tf_op jit(solution)/shard_map/ppermute | solution.py:316
  59.3 0.0 collective-permute-done.12.refs_3_
  59.3 1.9 %collective-permute-start.4 = (bf16[24,2176]{1,0:T(8,128)(2,1)S(1)}, bf16[24,2176]{1,0:T(8,128)(2,1)S(1)}, u32[]{:S(2)}, u32[]{:S(2)}) collective-permute-start(bf16[24,2176]{1,0:T(8,128)(2,1)S(1)} %get-tuple-element.28.refs_3_), channel_id=1, source_target_pairs={{0,3},{1,2},{2,1},{3,0},{4,7},{5,6},{6,5},{7,4},{8,11},{9,10},{10,... | collective-permute-start | bytes 313352 | tf_op jit(solution)/shard_map/ppermute | solution.py:316
  61.1 0.9 %copy-done.7 = bf16[48,2048]{1,0:T(8,128)(2,1)S(1)} copy-done((bf16[48,2048]{1,0:T(8,128)(2,1)S(1)}, bf16[48,2048]{1,0:T(8,128)(2,1)}, u32[]{:S(2)}) %copy-start.7) | copy-done | bytes 196632
  62.1 1.3 %far_grad.1 = f32[8,128]{1,0:T(8,128)S(1)} custom-call(bf16[24,2176]{1,0:T(8,128)(2,1)S(1)} %get-tuple-element.25.refs_0_, bf16[24,2176]{1,0:T(8,128)(2,1)S(1)} %get-tuple-element.26.refs_1_, bf16[24,2176]{1,0:T(8,128)(2,1)S(1)} %get-tuple-element.27.refs_2_, bf16[24,2176]{1,0:T(8,128)(2,1)S(1)} %get-tuple-element.28.refs_3_, ...), custom_call_target="tpu_custom_call" | custom-call | tf_op jit(solution)/shard_map/far_grad/pallas_call | solution.py:171
  63.4 0.0 copy-done.1
  63.4 0.0 copy-start.3
  63.4 1.1 %copy-done.3 = bf16[1,384,768]{2,1,0:T(8,128)(2,1)S(1)} copy-done((bf16[1,384,768]{2,1,0:T(8,128)(2,1)S(1)}, bf16[1,384,768]{2,1,0:T(8,128)(2,1)}, u32[]{:S(2)}) %copy-start.3) | copy-done | bytes 589848
  64.5 2.6 %expert_own.1 = (bf16[2,2,96,768]{3,2,1,0:T(8,128)(2,1)}, f32[8,128]{1,0:T(8,128)S(1)}) custom-call(s32[1]{0:T(128)} %bitcast.me_ref, bf16[48,2176]{1,0:T(8,128)(2,1)S(1)} %get-tuple-element.34.refs_0_, bf16[48,2176]{1,0:T(8,128)(2,1)S(1)} %collective-permute-done.10.refs_1_, bf16[48,2176]{1,0:T(8,128)(2,1)S(1)} %collective-permute-done.11.refs_2_, ...), custom_call_target="tpu_custom_call" | custom-call | tf_op jit(solution)/shard_map/expert_own/pallas_call | solution.py:260
  67.1 0.0 collective-permute-done.7.refs_6_
  67.1 3.3 %collective-permute-start.19 = (f32[8,128]{1,0:T(8,128)S(1)}, f32[8,128]{1,0:T(8,128)S(1)}, u32[]{:S(2)}, u32[]{:S(2)}) collective-permute-start(f32[8,128]{1,0:T(8,128)S(1)} %far_grad.1), channel_id=1, source_target_pairs={{0,4},{1,5},{2,6},{3,7},{4,0},{5,1},{6,2},{7,3},{8,12},{9,13},{10,... | collective-permute-start | bytes 12296 | tf_op jit(solution)/shard_map/ppermute | solution.py:316
  70.5 0.0 collective-permute-done.8.refs_7_
  70.5 0.5 collective-permute-start.13
  71.0 0.0 collective-permute-done.2.refs_1_
  71.0 1.1 %collective-permute-start.14 = (f32[8,128]{1,0:T(8,128)S(1)}, f32[8,128]{1,0:T(8,128)S(1)}, u32[]{:S(2)}, u32[]{:S(2)}) collective-permute-start(f32[8,128]{1,0:T(8,128)S(1)} %get-tuple-element.39.refs_0_), channel_id=1, source_target_pairs={{0,2},{1,3},{2,0},{3,1},{4,6},{5,7},{6,4},{7,5},{8,10},{9,11},{10,... | collective-permute-start | bytes 12296 | tf_op jit(solution)/shard_map/ppermute | solution.py:316
  72.1 0.0 collective-permute-done.3.refs_2_
  72.1 1.9 %collective-permute-start.15 = (f32[8,128]{1,0:T(8,128)S(1)}, f32[8,128]{1,0:T(8,128)S(1)}, u32[]{:S(2)}, u32[]{:S(2)}) collective-permute-start(f32[8,128]{1,0:T(8,128)S(1)} %get-tuple-element.39.refs_0_), channel_id=1, source_target_pairs={{0,3},{1,2},{2,1},{3,0},{4,7},{5,6},{6,5},{7,4},{8,11},{9,10},{10,... | collective-permute-start | bytes 12296 | tf_op jit(solution)/shard_map/ppermute | solution.py:316
  74.0 0.0 collective-permute-done.4.refs_3_
  74.0 0.0 copy-done.4
  74.0 2.4 %expert_far.1 = bf16[2,2,96,768]{3,2,1,0:T(8,128)(2,1)} custom-call(s32[1]{0:T(128)} %bitcast.me_ref, bf16[24,2176]{1,0:T(8,128)(2,1)S(1)} %get-tuple-element.25.refs_0_, bf16[24,2176]{1,0:T(8,128)(2,1)S(1)} %collective-permute-done.2.refs_1_, bf16[24,2176]{1,0:T(8,128)(2,1)S(1)} %collective-permute-done.3.refs_2_, ...), custom_call_target="tpu_custom_call", output_to_operand_aliasing={{}: (11, {})} | custom-call | tf_op jit(solution)/shard_map/expert_far/pallas_call | solution.py:260
  76.4 0.0 collective-permute-done.19.refs_4_
  76.4 0.0 collective-permute-done.13.refs_1_
  76.4 0.0 collective-permute-done.14.refs_2_
  76.4 0.2 collective-permute-done.15.refs_3_
  76.6 0.0 copy-done.8
  76.6 0.0 copy-done.10
  76.6 1.5 %router.1 = bf16[128,2048]{1,0:T(8,128)(2,1)} custom-call(s32[1]{0:T(128)} %bitcast.me_ref, f32[8,128]{1,0:T(8,128)S(1)} %copy-done.10, f32[8,128]{1,0:T(8,128)S(1)} %get-tuple-element.39.refs_0_, f32[8,128]{1,0:T(8,128)S(1)} %collective-permute-done.13.refs_1_, f32[8,128]{1,0:T(8,128)S(1)} %collective-permute-done.14.refs_2_, ...), custom_call_target="tpu_custom_call" | custom-call | tf_op jit(solution)/shard_map/router/pallas_call | solution.py:348
  (9 shorter events, 0.0 us)
Async XLA Ops:
  0.6 18.1 %collective-permute-start.9 = (bf16[128,2048]{1,0:T(8,128)(2,1)}, bf16[128,2048]{1,0:T(8,128)(2,1)}, u32[]{:S(2)}, u32[]{:S(2)}) collective-permute-start(bf16[128,2048]{1,0:T(8,128)(2,1)} %bitcast.19), channel_id=1, source_target_pairs={{0,24},{1,25},{2,26},{3,27},{4,28},{5,29},{6,30},{7,31},{8,0},{9,1... | collective-permute-start | bytes 1572872 | tf_op jit(solution)/shard_map/ppermute | solution.py:316
  3.1 1.9 %copy-start = (bf16[1,768,2048]{2,1,0:T(8,128)(2,1)S(1)}, bf16[1,768,2048]{2,1,0:T(8,128)(2,1)}, u32[]{:S(2)}) copy-start(bf16[1,768,2048]{2,1,0:T(8,128)(2,1)} %param.10) | copy-start | bytes 9437188
  5.0 1.1 %copy-start.2 = (bf16[1,384,768]{2,1,0:T(8,128)(2,1)S(1)}, bf16[1,384,768]{2,1,0:T(8,128)(2,1)}, u32[]{:S(2)}) copy-start(bf16[1,384,768]{2,1,0:T(8,128)(2,1)} %param.9) | copy-start | bytes 1769476
  6.0 1.0 %copy-start.5 = (bf16[1,128,2048]{2,1,0:T(8,128)(2,1)S(1)}, bf16[1,128,2048]{2,1,0:T(8,128)(2,1)}, u32[]{:S(2)}) copy-start(bf16[1,128,2048]{2,1,0:T(8,128)(2,1)} %param.6) | copy-start | bytes 1572868
  7.1 56.3 %copy-start.1 = (bf16[1,768,2048]{2,1,0:T(8,128)(2,1)S(1)}, bf16[1,768,2048]{2,1,0:T(8,128)(2,1)}, u32[]{:S(2)}) copy-start(bf16[1,768,2048]{2,1,0:T(8,128)(2,1)} %param.10) | copy-start | bytes 9437188
  9.8 0.7 copy-start.6
  10.5 0.7 copy-start.11
  11.2 30.3 %collective-permute-start.5 = (bf16[64,2048]{1,0:T(8,128)(2,1)}, bf16[64,2048]{1,0:T(8,128)(2,1)S(1)}, u32[]{:S(2)}, u32[]{:S(2)}) collective-permute-start(bf16[64,2048]{1,0:T(8,128)(2,1)} %get-tuple-element.29), channel_id=1, source_target_pairs={{0,28},{1,29},{2,30},{3,31},{4,24},{5,25},{6,26},{7,27},{8,4},{9,5... | collective-permute-start | bytes 786440 | tf_op jit(solution)/shard_map/ppermute | solution.py:316
  13.9 25.5 %collective-permute-start.16 = (bf16[48,2048]{1,0:T(8,128)(2,1)}, bf16[48,2048]{1,0:T(8,128)(2,1)}, u32[]{:S(2)}, u32[]{:S(2)}) collective-permute-start(bf16[48,2048]{1,0:T(8,128)(2,1)} %get-tuple-element.41), channel_id=1, source_target_pairs={{0,1},{1,0},{2,3},{3,2},{4,5},{5,4},{6,7},{7,6},{8,9},{9,8},{10,11... | collective-permute-start | bytes 589832 | tf_op jit(solution)/shard_map/ppermute | solution.py:316
  15.4 24.8 %collective-permute-start.17 = (bf16[48,2048]{1,0:T(8,128)(2,1)}, bf16[48,2048]{1,0:T(8,128)(2,1)}, u32[]{:S(2)}, u32[]{:S(2)}) collective-permute-start(bf16[48,2048]{1,0:T(8,128)(2,1)} %get-tuple-element.42), channel_id=1, source_target_pairs={{0,2},{1,3},{2,0},{3,1},{4,6},{5,7},{6,4},{7,5},{8,10},{9,11},{10,... | collective-permute-start | bytes 589832 | tf_op jit(solution)/shard_map/ppermute | solution.py:316
  18.7 24.9 %collective-permute-start.1 = (bf16[64,2048]{1,0:T(8,128)(2,1)}, bf16[64,2048]{1,0:T(8,128)(2,1)S(1)}, u32[]{:S(2)}, u32[]{:S(2)}) collective-permute-start(bf16[64,2048]{1,0:T(8,128)(2,1)} %get-tuple-element.24), channel_id=1, source_target_pairs={{0,28},{1,29},{2,30},{3,31},{4,24},{5,25},{6,26},{7,27},{8,4},{9,5... | collective-permute-start | bytes 786440 | tf_op jit(solution)/shard_map/ppermute | solution.py:316
  18.7 19.3 %collective-permute-start = (f32[8,128]{1,0:T(8,128)}, f32[8,128]{1,0:T(8,128)S(1)}, u32[]{:S(2)}, u32[]{:S(2)}) collective-permute-start(f32[8,128]{1,0:T(8,128)} %get-tuple-element.23.info_ref), channel_id=1, source_target_pairs={{0,4},{1,5},{2,6},{3,7},{4,0},{5,1},{6,2},{7,3},{8,12},{9,13},{10,... | collective-permute-start | bytes 12296 | tf_op jit(solution)/shard_map/ppermute | solution.py:316
  20.7 0.7 copy-start.9
  38.0 19.6 %collective-permute-start.10 = (bf16[48,2176]{1,0:T(8,128)(2,1)S(1)}, bf16[48,2176]{1,0:T(8,128)(2,1)S(1)}, u32[]{:S(2)}, u32[]{:S(2)}) collective-permute-start(bf16[48,2176]{1,0:T(8,128)(2,1)S(1)} %get-tuple-element.35), channel_id=1, source_target_pairs={{0,1},{1,0},{2,3},{3,2},{4,5},{5,4},{6,7},{7,6},{8,9},{9,8},{10,11... | collective-permute-start | bytes 626696 | tf_op jit(solution)/shard_map/ppermute | solution.py:316
  39.5 18.8 %collective-permute-start.11 = (bf16[48,2176]{1,0:T(8,128)(2,1)S(1)}, bf16[48,2176]{1,0:T(8,128)(2,1)S(1)}, u32[]{:S(2)}, u32[]{:S(2)}) collective-permute-start(bf16[48,2176]{1,0:T(8,128)(2,1)S(1)} %get-tuple-element.36), channel_id=1, source_target_pairs={{0,2},{1,3},{2,0},{3,1},{4,6},{5,7},{6,4},{7,5},{8,10},{9,11},{10,... | collective-permute-start | bytes 626696 | tf_op jit(solution)/shard_map/ppermute | solution.py:316
  40.2 19.1 %collective-permute-start.12 = (bf16[48,2176]{1,0:T(8,128)(2,1)S(1)}, bf16[48,2176]{1,0:T(8,128)(2,1)S(1)}, u32[]{:S(2)}, u32[]{:S(2)}) collective-permute-start(bf16[48,2176]{1,0:T(8,128)(2,1)S(1)} %get-tuple-element.37), channel_id=1, source_target_pairs={{0,3},{1,2},{2,1},{3,0},{4,7},{5,6},{6,5},{7,4},{8,11},{9,10},{10,... | collective-permute-start | bytes 626696 | tf_op jit(solution)/shard_map/ppermute | solution.py:316
  41.5 12.9 %collective-permute-start.18 = (bf16[48,2048]{1,0:T(8,128)(2,1)}, bf16[48,2048]{1,0:T(8,128)(2,1)S(1)}, u32[]{:S(2)}, u32[]{:S(2)}) collective-permute-start(bf16[48,2048]{1,0:T(8,128)(2,1)} %copy-done.11), channel_id=1, source_target_pairs={{0,3},{1,2},{2,1},{3,0},{4,7},{5,6},{6,5},{7,4},{8,11},{9,10},{10,... | collective-permute-start | bytes 589832 | tf_op jit(solution)/shard_map/ppermute | solution.py:316
  43.6 12.2 %collective-permute-start.6 = (bf16[24,2176]{1,0:T(8,128)(2,1)S(1)}, bf16[24,2176]{1,0:T(8,128)(2,1)S(1)}, u32[]{:S(2)}, u32[]{:S(2)}) collective-permute-start(bf16[24,2176]{1,0:T(8,128)(2,1)S(1)} %get-tuple-element.31.refs_5_), channel_id=1, source_target_pairs={{0,1},{1,0},{2,3},{3,2},{4,5},{5,4},{6,7},{7,6},{8,9},{9,8},{10,11... | collective-permute-start | bytes 313352 | tf_op jit(solution)/shard_map/ppermute | solution.py:316
  44.6 29.4 %copy-start.4 = (bf16[1,384,768]{2,1,0:T(8,128)(2,1)S(1)}, bf16[1,384,768]{2,1,0:T(8,128)(2,1)}, u32[]{:S(2)}) copy-start(bf16[1,384,768]{2,1,0:T(8,128)(2,1)} %param.9) | copy-start | bytes 1769476
  54.4 12.7 %collective-permute-start.7 = (bf16[24,2176]{1,0:T(8,128)(2,1)S(1)}, bf16[24,2176]{1,0:T(8,128)(2,1)S(1)}, u32[]{:S(2)}, u32[]{:S(2)}) collective-permute-start(bf16[24,2176]{1,0:T(8,128)(2,1)S(1)} %get-tuple-element.32.refs_6_), channel_id=1, source_target_pairs={{0,2},{1,3},{2,0},{3,1},{4,6},{5,7},{6,4},{7,5},{8,10},{9,11},{10,... | collective-permute-start | bytes 313352 | tf_op jit(solution)/shard_map/ppermute | solution.py:316
  55.8 14.7 %collective-permute-start.8 = (bf16[24,2176]{1,0:T(8,128)(2,1)S(1)}, bf16[24,2176]{1,0:T(8,128)(2,1)S(1)}, u32[]{:S(2)}, u32[]{:S(2)}) collective-permute-start(bf16[24,2176]{1,0:T(8,128)(2,1)S(1)} %get-tuple-element.33.refs_7_), channel_id=1, source_target_pairs={{0,3},{1,2},{2,1},{3,0},{4,7},{5,6},{6,5},{7,4},{8,11},{9,10},{10,... | collective-permute-start | bytes 313352 | tf_op jit(solution)/shard_map/ppermute | solution.py:316
  57.6 13.4 %collective-permute-start.2 = (bf16[24,2176]{1,0:T(8,128)(2,1)S(1)}, bf16[24,2176]{1,0:T(8,128)(2,1)S(1)}, u32[]{:S(2)}, u32[]{:S(2)}) collective-permute-start(bf16[24,2176]{1,0:T(8,128)(2,1)S(1)} %get-tuple-element.26.refs_1_), channel_id=1, source_target_pairs={{0,1},{1,0},{2,3},{3,2},{4,5},{5,4},{6,7},{7,6},{8,9},{9,8},{10,11... | collective-permute-start | bytes 313352 | tf_op jit(solution)/shard_map/ppermute | solution.py:316
  58.2 13.8 %collective-permute-start.3 = (bf16[24,2176]{1,0:T(8,128)(2,1)S(1)}, bf16[24,2176]{1,0:T(8,128)(2,1)S(1)}, u32[]{:S(2)}, u32[]{:S(2)}) collective-permute-start(bf16[24,2176]{1,0:T(8,128)(2,1)S(1)} %get-tuple-element.27.refs_2_), channel_id=1, source_target_pairs={{0,2},{1,3},{2,0},{3,1},{4,6},{5,7},{6,4},{7,5},{8,10},{9,11},{10,... | collective-permute-start | bytes 313352 | tf_op jit(solution)/shard_map/ppermute | solution.py:316
  59.3 14.7 %collective-permute-start.4 = (bf16[24,2176]{1,0:T(8,128)(2,1)S(1)}, bf16[24,2176]{1,0:T(8,128)(2,1)S(1)}, u32[]{:S(2)}, u32[]{:S(2)}) collective-permute-start(bf16[24,2176]{1,0:T(8,128)(2,1)S(1)} %get-tuple-element.28.refs_3_), channel_id=1, source_target_pairs={{0,3},{1,2},{2,1},{3,0},{4,7},{5,6},{6,5},{7,4},{8,11},{9,10},{10,... | collective-permute-start | bytes 313352 | tf_op jit(solution)/shard_map/ppermute | solution.py:316
  61.1 0.9 %copy-start.7 = (bf16[48,2048]{1,0:T(8,128)(2,1)S(1)}, bf16[48,2048]{1,0:T(8,128)(2,1)}, u32[]{:S(2)}) copy-start(bf16[48,2048]{1,0:T(8,128)(2,1)} %copy-done.6) | copy-start | bytes 589828
  63.4 1.1 %copy-start.3 = (bf16[1,384,768]{2,1,0:T(8,128)(2,1)S(1)}, bf16[1,384,768]{2,1,0:T(8,128)(2,1)}, u32[]{:S(2)}) copy-start(bf16[1,384,768]{2,1,0:T(8,128)(2,1)} %param.9) | copy-start | bytes 1769476
  67.1 9.5 %copy-start.8 = (bf16[2048,8]{0,1:T(8,128)(2,1)S(1)}, bf16[2048,8]{0,1:T(8,128)(2,1)}, u32[]{:S(2)}) copy-start(bf16[2048,8]{0,1:T(8,128)(2,1)} %param.11) | copy-start | bytes 98308
  67.1 9.5 %copy-start.10 = (f32[8,128]{1,0:T(8,128)S(1)}, f32[8,128]{1,0:T(8,128)}, u32[]{:S(2)}) copy-start(f32[8,128]{1,0:T(8,128)} %get-tuple-element.23.info_ref) | copy-start | bytes 12292
  67.1 9.3 %collective-permute-start.19 = (f32[8,128]{1,0:T(8,128)S(1)}, f32[8,128]{1,0:T(8,128)S(1)}, u32[]{:S(2)}, u32[]{:S(2)}) collective-permute-start(f32[8,128]{1,0:T(8,128)S(1)} %far_grad.1), channel_id=1, source_target_pairs={{0,4},{1,5},{2,6},{3,7},{4,0},{5,1},{6,2},{7,3},{8,12},{9,13},{10,... | collective-permute-start | bytes 12296 | tf_op jit(solution)/shard_map/ppermute | solution.py:316
  70.5 5.9 %collective-permute-start.13 = (f32[8,128]{1,0:T(8,128)S(1)}, f32[8,128]{1,0:T(8,128)S(1)}, u32[]{:S(2)}, u32[]{:S(2)}) collective-permute-start(f32[8,128]{1,0:T(8,128)S(1)} %get-tuple-element.39.refs_0_), channel_id=1, source_target_pairs={{0,1},{1,0},{2,3},{3,2},{4,5},{5,4},{6,7},{7,6},{8,9},{9,8},{10,11... | collective-permute-start | bytes 12296 | tf_op jit(solution)/shard_map/ppermute | solution.py:316
  71.0 5.4 %collective-permute-start.14 = (f32[8,128]{1,0:T(8,128)S(1)}, f32[8,128]{1,0:T(8,128)S(1)}, u32[]{:S(2)}, u32[]{:S(2)}) collective-permute-start(f32[8,128]{1,0:T(8,128)S(1)} %get-tuple-element.39.refs_0_), channel_id=1, source_target_pairs={{0,2},{1,3},{2,0},{3,1},{4,6},{5,7},{6,4},{7,5},{8,10},{9,11},{10,... | collective-permute-start | bytes 12296 | tf_op jit(solution)/shard_map/ppermute | solution.py:316
  72.1 4.5 %collective-permute-start.15 = (f32[8,128]{1,0:T(8,128)S(1)}, f32[8,128]{1,0:T(8,128)S(1)}, u32[]{:S(2)}, u32[]{:S(2)}) collective-permute-start(f32[8,128]{1,0:T(8,128)S(1)} %get-tuple-element.39.refs_0_), channel_id=1, source_target_pairs={{0,3},{1,2},{2,1},{3,0},{4,7},{5,6},{6,5},{7,4},{8,11},{9,10},{10,... | collective-permute-start | bytes 12296 | tf_op jit(solution)/shard_map/ppermute | solution.py:316

commit v3 on v0

--- a/solution.py
+++ b/solution.py
@@ -1,11 +1,340 @@
+import functools
+
 import jax
 import jax.numpy as jnp
 from jax import lax
+from jax.experimental import pallas as pl
+from jax.experimental.pallas import tpu as pltpu
 from jax.sharding import PartitionSpec as P
 
 TOP = 2
 MICRO = 2
 MB_TOK = 64
+LANES = 128
+F32, BF16 = jnp.float32, jnp.bfloat16
+VMEM_LIMIT = 16 * 1024 * 1024
+COLUMN = 256
+
+
+def iota(shape, axis):
+    return lax.broadcasted_iota(jnp.int32, shape, axis)
+
+
+def info_kernel(routes_ref, probs_ref, info_ref):
+    probs = probs_ref[...]
+    expert = iota(probs.shape, 0)
+    first, second = routes_ref[0:1, :], routes_ref[1:2, :]
+    p_first = jnp.sum(jnp.where(expert == first, probs, 0.0), axis=0, keepdims=True)
+    p_second = jnp.sum(jnp.where(expert == second, probs, 0.0), axis=0, keepdims=True)
+    total = p_first + p_second
+    info_ref[0:1, :] = first.astype(F32)
+    info_ref[1:2, :] = second.astype(F32)
+    info_ref[2:3, :] = p_first / total
+    info_ref[3:4, :] = p_second / total
+    info_ref[4:8, :] = jnp.zeros((4, LANES), F32)
+
+
+def split(column):
+    high = column.astype(BF16).astype(F32)
+    middle = (column - high).astype(BF16).astype(F32)
+    return high, middle, column - high - middle
+
+
+def ranks(info, expert_rows):
+    first, second = info[0:1, :].astype(jnp.int32), info[1:2, :].astype(jnp.int32)
+    on_first, on_second = expert_rows == first, expert_rows == second
+    named = on_first | on_second
+    before = iota((LANES, LANES), 0)
+    after = iota((LANES, LANES), 1)
+    earlier = ((before < after) & (before // MB_TOK == after // MB_TOK)).astype(F32).astype(BF16)
+    rank = jnp.dot(named.astype(F32).astype(BF16), earlier, preferred_element_type=F32)
+    rank = jnp.where(named, rank.astype(jnp.int32), -1)
+    weight = jnp.where(on_first, info[2:3, :], 0.0) + jnp.where(on_second, info[3:4, :], 0.0)
+    return rank, weight.astype(BF16).astype(F32)
+
+
+def pick(rank_row, weight_row, micro, capacity):
+    slot = iota((capacity, LANES), 0)
+    token = iota((capacity, LANES), 1)
+    hit = (slot == rank_row) & (token // MB_TOK == micro)
+    onehot = jnp.where(hit, 1.0, 0.0)
+    scale = jnp.sum(jnp.where(hit, weight_row, 0.0), axis=1, keepdims=True)
+    return onehot, jnp.broadcast_to(scale, (capacity, LANES))
+
+
+def pack_kernel(half, capacity, me_ref, info_ref, token_ref, *refs):
+    outs = refs[-half:]
+    rows = jnp.bitwise_xor(me_ref[0], iota((8, LANES), 0))
+    rank, weight = ranks(info_ref[...], rows)
+    pieces, scales = [], []
+    for j in range(half):
+        for micro in range(MICRO):
+            onehot, scale = pick(rank[j : j + 1, :], weight[j : j + 1, :], micro, capacity)
+            pieces.append(onehot)
+            scales.append(scale)
+    width = token_ref.shape[1]
+    chosen = jnp.concatenate(pieces, axis=0).astype(BF16)
+    packed = jnp.dot(chosen, token_ref[...], preferred_element_type=F32).astype(BF16)
+    size = MICRO * capacity
+    for j in range(half):
+        outs[j][:, 0:width] = packed[j * size : (j + 1) * size]
+        outs[j][:, width:] = jnp.concatenate(scales[j * MICRO : (j + 1) * MICRO], axis=0).astype(BF16)
+
+
+def pack(me, info, tokens, half, capacity, name, into=()):
+    rows, width = MICRO * capacity, tokens.shape[1] + LANES
+    at = 1 if into else 0
+    return pl.pallas_call(
+        functools.partial(pack_kernel, half, capacity),
+        grid=(1,),
+        out_shape=[jax.ShapeDtypeStruct(((1 + at) * rows, width), BF16)] * half,
+        in_specs=[
+            pl.BlockSpec(memory_space=pltpu.SMEM),
+            pl.BlockSpec(info.shape, lambda i: (0, 0)),
+            pl.BlockSpec(tokens.shape, lambda i: (0, 0)),
+        ]
+        + [pl.BlockSpec(memory_space=pl.ANY)] * len(into),
+        out_specs=[pl.BlockSpec((rows, width), lambda i: (at, 0))] * half,
+        input_output_aliases={3 + j: j for j in range(len(into))},
+        compiler_params=pltpu.CompilerParams(vmem_limit_bytes=VMEM_LIMIT),
+        name=name,
+    )(me, info, tokens, *into)
+
+
+def chunks(width):
+    step = COLUMN if width % COLUMN == 0 else width
+    return [pl.ds(start, step) for start in range(0, width, step)]
+
+
+def back_kernel(half, capacity, turn, me_ref, saved_ref, w_ref, *refs):
+    outs, product = refs[:half], refs[half]
+    run = half * capacity
+    saved = jnp.concatenate([saved_ref[m, 0] for m in range(MICRO)], axis=0)
+    here = jnp.bitwise_xor(lax.rem(me_ref[0], half), turn)
+    for columns in chunks(w_ref.shape[1]):
+        product[:, columns] = jnp.dot(saved, w_ref[:, columns], preferred_element_type=F32)
+    for j in range(half):
+        for m in range(MICRO):
+            slot = pl.multiple_of(m * run + jnp.bitwise_xor(here, j) * capacity, 8)
+            outs[j][m * capacity : (m + 1) * capacity, :] = product[pl.ds(slot, capacity), :].astype(BF16)
+
+
+def back(me, saved, weight, half, capacity, turn):
+    hidden_width, width = weight.shape
+    run, rows = half * capacity, MICRO * capacity
+    return pl.pallas_call(
+        functools.partial(back_kernel, half, capacity, turn),
+        grid_spec=pltpu.PrefetchScalarGridSpec(
+            num_scalar_prefetch=1,
+            grid=(1,),
+            in_specs=[
+                pl.BlockSpec((MICRO, 1, run, hidden_width), lambda i, me: (0, 1 - me[0] // half, 0, 0)),
+                pl.BlockSpec(memory_space=pltpu.VMEM),
+            ],
+            out_specs=[pl.BlockSpec((rows, width), lambda i, me: (0, 0))] * half,
+            scratch_shapes=[pltpu.VMEM((MICRO * run, width), F32)],
+        ),
+        out_shape=[jax.ShapeDtypeStruct((2 * rows, width + LANES), BF16)] * half,
+        compiler_params=pltpu.CompilerParams(vmem_limit_bytes=VMEM_LIMIT),
+        name="back",
+    )(me, saved, weight)
+
+
+def far_grad_kernel(half, capacity, *refs):
+    blocks, backs, (grad_ref,) = refs[:half], refs[half : 2 * half], refs[2 * half :]
+    width = blocks[0].shape[1] - LANES
+    rows = MICRO * capacity
+    where = iota((rows, LANES), 1)
+    table = jnp.zeros((rows, LANES), F32)
+    for j in range(half):
+        total = jnp.zeros((rows, LANES), F32)
+        for lane in range(0, width, LANES):
+            sent = blocks[j][:, lane : lane + LANES].astype(F32)
+            total = total + sent * backs[j][:, lane : lane + LANES].astype(F32)
+        for i, part in enumerate(split(jnp.sum(total, axis=1, keepdims=True))):
+            table = jnp.where(where == 3 * j + i, part, table)
+    grad_ref[...] = table.astype(BF16)
+
+
+def far_grad(blocks, backs, half, capacity):
+    vmem = pl.BlockSpec(memory_space=pltpu.VMEM)
+    rows, width = blocks[0].shape
+    return pl.pallas_call(
+        functools.partial(far_grad_kernel, half, capacity),
+        grid=(1,),
+        out_shape=jax.ShapeDtypeStruct((rows, LANES), BF16),
+        in_specs=[vmem] * half + [pl.BlockSpec((rows, width), lambda i: (0, 0))] * half,
+        out_specs=vmem,
+        compiler_params=pltpu.CompilerParams(vmem_limit_bytes=VMEM_LIMIT),
+        name="far_grad",
+    )(*blocks, *backs)
+
+
+def expert_kernel(half, capacity, turn, graded, me_ref, *refs):
+    blocks, w_ref, refs = refs[:half], refs[half], refs[half + 1 :]
+    if graded:
+        saved_ref, _, d_ref, *grads, lhs, product, scale, partial = refs
+    else:
+        _, d_ref, lhs, product, scale = refs
+    hidden_width, width = w_ref.shape
+    run = half * capacity
+    here = jnp.bitwise_xor(lax.rem(me_ref[0], half), turn)
+    places = []
+    for j in range(half):
+        for m in range(MICRO):
+            slot = pl.multiple_of(m * run + jnp.bitwise_xor(here, j) * capacity, 8)
+            places.append((j, m * capacity, (j * MICRO + m) * capacity, slot))
+    for j in range(half):
+        lhs[j * MICRO * capacity : (j + 1) * MICRO * capacity, :] = blocks[j][:, 0:width]
+    for j, row, _, slot in places:
+        scale[pl.ds(slot, capacity), :] = blocks[j][row : row + capacity, width:].astype(F32)
+    for columns in chunks(hidden_width):
+        got = lax.dot_general(lhs[...], w_ref[columns, :], (((1,), (1,)), ((), ())), preferred_element_type=F32)
+        for _, _, begin, slot in places:
+            product[pl.ds(slot, capacity), columns] = got[begin : begin + capacity, :]
+    total = jnp.zeros((MICRO * run, LANES), F32)
+    for lane in range(0, hidden_width, LANES):
+        part = product[:, lane : lane + LANES]
+        scaled = (scale[...] * part).astype(BF16)
+        for m in range(MICRO):
+            d_ref[m, 0, :, lane : lane + LANES] = scaled[m * run : (m + 1) * run]
+        if graded:
+            held = jnp.concatenate([saved_ref[m, 0, :, lane : lane + LANES] for m in range(MICRO)], axis=0)
+            total = total + part * held.astype(F32)
+    if graded:
+        partial[...] = total
+        lane = iota((capacity, LANES), 1)
+        for j, row, _, slot in places:
+            parts = split(jnp.sum(partial[pl.ds(slot, capacity), :], axis=1, keepdims=True))
+            table = jnp.where(lane == 0, parts[0], jnp.where(lane == 1, parts[1], parts[2]))
+            grads[j][row : row + capacity, :] = table.astype(BF16)
+
+
+def expert(me, blocks, weight, half, capacity, turn, saved=None, wait=None, held=None):
+    hidden_width, width = weight.shape
+    run, rows = half * capacity, MICRO * capacity
+    graded = held is None
+    row_block = 1 if graded else 0
+    anywhere = pl.BlockSpec(memory_space=pl.ANY)
+    side = (lambda me: me[0] // half) if graded else (lambda me: 1 - me[0] // half)
+    slots = pl.BlockSpec((MICRO, 1, run, hidden_width), lambda i, me: (0, side(me), 0, 0))
+    in_specs = [pl.BlockSpec((rows, width + LANES), lambda i, me: (row_block, 0))] * half
+    in_specs += [pl.BlockSpec(memory_space=pltpu.VMEM)]
+    scratch = [
+        pltpu.VMEM((MICRO * run, width), BF16),
+        pltpu.VMEM((MICRO * run, hidden_width), F32),
+        pltpu.VMEM((MICRO * run, LANES), F32),
+    ]
+    if graded:
+        out_shape = [jax.ShapeDtypeStruct(saved.shape, BF16)] + [jax.ShapeDtypeStruct((rows, LANES), BF16)] * half
+        out_specs = [slots] + [pl.BlockSpec((rows, LANES), lambda i, me: (0, 0))] * half
+        scratch.append(pltpu.VMEM((MICRO * run, LANES), F32))
+        operands, in_specs, aliases = [saved, wait], in_specs + [slots, anywhere], {}
+    else:
+        out_shape, out_specs = [jax.ShapeDtypeStruct(held.shape, BF16)], [slots]
+        operands, in_specs, aliases = [held], in_specs + [anywhere], {half + 2: 0}
+    return pl.pallas_call(
+        functools.partial(expert_kernel, half, capacity, turn, graded),
+        grid_spec=pltpu.PrefetchScalarGridSpec(
+            num_scalar_prefetch=1,
+            grid=(1,),
+            in_specs=in_specs,
+            out_specs=out_specs,
+            scratch_shapes=scratch,
+        ),
+        out_shape=out_shape,
+        input_output_aliases=aliases,
+        compiler_params=pltpu.CompilerParams(vmem_limit_bytes=VMEM_LIMIT),
+        name="expert_own" if graded else "expert_far",
+    )(me, *blocks, weight, *operands)
+
+
+def router_kernel(half, capacity, turn, me_ref, info_ref, *refs):
+    own, (far_ref, router_ref, out_ref) = refs[:half], refs[half:]
+    info = info_ref[...]
+    relative = jnp.bitwise_xor(me_ref[0], iota((8, LANES), 0))
+    rank, _ = ranks(info, relative)
+    slot = iota((capacity, LANES), 0)
+    token = iota((capacity, LANES), 1)
+    far = far_ref[...].astype(F32)
+    rows = []
+    for j in range(2 * half):
+        if j < half:
+            table, lane = own[j][...].astype(F32), 0
+        else:
+            table, lane = far, 3 * ((j - half) ^ turn)
+        column = table[:, lane : lane + 1] + table[:, lane + 1 : lane + 2] + table[:, lane + 2 : lane + 3]
+        here = jnp.where(token // MB_TOK == 0, column[0:capacity], column[capacity : 2 * capacity])
+        rows.append(jnp.sum(jnp.where(slot == rank[j : j + 1, :], here, 0.0), axis=0, keepdims=True))
+    grads = jnp.concatenate(rows, axis=0)
+    first, second = info[0:1, :].astype(jnp.int32), info[1:2, :].astype(jnp.int32)
+    w_first, w_second = info[2:3, :], info[3:4, :]
+    g_first = jnp.sum(jnp.where(relative == first, grads, 0.0), axis=0, keepdims=True)
+    g_second = jnp.sum(jnp.where(relative == second, grads, 0.0), axis=0, keepdims=True)
+    mean = w_first * g_first + w_second * g_second
+    expert_rows = iota((8, LANES), 0)
+    logit = jnp.where(expert_rows == first, w_first * (g_first - mean), 0.0)
+    logit = logit + jnp.where(expert_rows == second, w_second * (g_second - mean), 0.0)
+    parts = jnp.concatenate([*split(logit), jnp.zeros((LANES - 24, LANES), F32)], axis=0).T
+    router = router_ref[...].astype(F32)
+    router = jnp.concatenate([router, router, router, jnp.zeros((LANES - 24, router.shape[1]), F32)], axis=0)
+    out_ref[...] = jnp.dot(parts.astype(BF16), router.astype(BF16), preferred_element_type=F32).astype(BF16)
+
+
+def router(me, info, own, far, table, tokens, half, capacity, turn):
+    vmem = pl.BlockSpec(memory_space=pltpu.VMEM)
+    return pl.pallas_call(
+        functools.partial(router_kernel, half, capacity, turn),
+        out_shape=jax.ShapeDtypeStruct(tokens.shape, BF16),
+        in_specs=[pl.BlockSpec(memory_space=pltpu.SMEM)] + [vmem] * (half + 3),
+        out_specs=vmem,
+        compiler_params=pltpu.CompilerParams(vmem_limit_bytes=VMEM_LIMIT),
+        name="router",
+    )(me, info, *own, far, table)
+
+
+def route(block, flip, back):
+    sections, peers = lax.axis_size("pipe"), lax.axis_size("expert")
+    pairs = [
+        (p * peers + e, ((p - back) % sections) * peers + (e ^ flip)) for p in range(sections) for e in range(peers)
+    ]
+    return lax.ppermute(block, ("pipe", "expert"), pairs)
+
+
+def by_halves(grad_sent, routes, router_probs, saved_hidden, w_down, w_router):
+    peers = lax.axis_size("expert")
+    half, turn = peers // 2, 2
+    slots, hidden_width = saved_hidden.shape[1:]
+    capacity = slots // (MICRO * peers)
+    me = lax.axis_index("expert").astype(jnp.int32).reshape(1)
+    tokens, weight = grad_sent[0], w_down[0]
+    saved = saved_hidden.reshape(MICRO, 2, half * capacity, hidden_width)
+    vmem = pl.BlockSpec(memory_space=pltpu.VMEM)
+
+    def spread(blocks):
+        return [blocks[0]] + [route(blocks[j], j, 0) for j in range(1, half)]
+
+    own_tokens = route(tokens, 0, 1)
+    info = pl.pallas_call(
+        info_kernel,
+        out_shape=jax.ShapeDtypeStruct((8, LANES), F32),
+        in_specs=[vmem, vmem],
+        out_specs=vmem,
+        name="info",
+    )(routes[0].T, router_probs[0].T)
+    far_info = route(info, half + turn, 0)
+    far_tokens = route(lax.optimization_barrier((tokens, info))[0], half + turn, 1)
+    backs = back(me, saved, weight, half, capacity, turn)
+    near = spread(pack(me, info, own_tokens, half, capacity, "pack_own", backs))
+    far = pack(me, far_info, far_tokens, half, capacity, "pack_far")
+    far_own = far_grad(far, near, half, capacity)
+    far_grads = route(far_own, half + turn, 0)
+    far = spread(far)
+    held, *own_grads = expert(me, near, weight, half, capacity, 0, saved=saved, wait=far_own)
+    own_grads = spread(own_grads)
+    (d_hidden,) = expert(me, far, weight, half, capacity, turn, held=held)
+    grad_in = router(me, info, own_grads, far_grads, w_router.T, tokens, half, capacity, turn)
+    return d_hidden.reshape(saved_hidden.shape), grad_in[None]
 
 
 def from_behind(block, axis, distance):
@@ -20,7 +349,7 @@
     return route_rows * capacity + rank_of
 
 
-def on_device(grad_sent, routes, router_probs, saved_hidden, w_down, w_router):
+def by_slots(grad_sent, routes, router_probs, saved_hidden, w_down, w_router):
     peer_count = lax.axis_size("expert")
     slot_count = saved_hidden.shape[1]
     capacity = slot_count // (MICRO * peer_count)
@@ -76,6 +405,14 @@
     return (d_hidden.reshape(1, slot_count, hidden_width), grad_in.astype(jnp.bfloat16)[None])
 
 
+def on_device(*blocks):
+    peers, slots = lax.axis_size("expert"), blocks[3].shape[1]
+    capacity = slots // (MICRO * peers)
+    if peers == 8 and capacity % 8 == 0 and capacity <= MB_TOK // 2:
+        return by_halves(*blocks)
+    return by_slots(*blocks)
+
+
 def solution(mesh):
     placed = (
         P("pipe", "expert", None),

time: 136 us -> 56.2 us (0.41)
  local copies, waits for them, and re-layouts: 64.2 us -> 2.97 us
  waiting for transfers between devices: 41.8 us -> 20.4 us
  Pallas kernels: 0 us -> 9 us
  other arithmetic: 7.1 us -> 0 us
  starting transfers between devices: 17.6 us -> 22.8 us
  matrix products: 3.69 us -> 0 us
    all_to_all x3 -> x0, waiting for transfers between devices: 41.7 us -> none  [the longest x1 35.4 us: on_device(): lax.all_to_all(send_rows, 'expert', split_axis=1, concat_axis=1, tiled=True)]
    scatter x4 -> x0, local copies, waits for them, and re-layouts: 37.8 us -> none  [the longest x2 12.8 us: on_device(): jnp.zeros((MICRO, send_width), jnp.bool_).at[micro_index, position]]
    gather x10 -> x0, local copies, waits for them, and re-layouts: 20.9 us -> none  [the longest x2 16.4 us: on_device(): picked = jnp.take_along_axis(micro_grad, slot_token[..., None], axis=1)]
    ppermute x1 -> x13, waiting for transfers between devices: 0.01 us -> 20.4 us  [route(): return lax.ppermute(block, ('pipe', 'expert'), pairs)]
    ppermute x1 -> x13, starting transfers between devices: 2.46 us -> 22.8 us  [route(): return lax.ppermute(block, ('pipe', 'expert'), pairs)]
    all_to_all x3 -> x0, starting transfers between devices: 15.2 us -> none  [the longest x1 5.99 us: on_device(): lax.all_to_all(send_rows, 'expert', split_axis=1, concat_axis=1, tiled=True)]
    pallas_call x0 -> x8, Pallas kernels: none -> 9 us  [the longest x2 4.14 us: expert(): pl.pallas_call(functools.partial(expert_kernel, half, capacity, turn, gra...]
    select_n x2 -> x0, other arithmetic: 5.12 us -> none  [the longest x1 5.12 us: on_device(): jnp.where(slot_used[..., None], picked, jnp.zeros((), jnp.bfloat16))]
  transfers between devices with their start and end apart: 4 -> 13, of which waited for: 2 -> 2; matrix products, arithmetic and copies ran while one was open for 49% -> 0% of each run, Pallas kernels for 0% -> 14%
where the time goes in v3:
time: 56.2 us; the launch traced here: 55.9 us
  starting transfers between devices  22.8 us (41%)
  waiting for transfers between devices  20.4 us (36%)
  Pallas kernels  9 us (16%)
  local copies, waits for them, and re-layouts  2.97 us (5%)
  between operations  0.73 us (1%)
    ppermute x13, starting transfers between devices, route(): return lax.ppermute(block, ('pipe', 'expert'), pairs)  22.8 us
    ppermute x13, waiting for transfers between devices, route(): return lax.ppermute(block, ('pipe', 'expert'), pairs)  20.4 us
    pallas_call x2, Pallas kernels, expert(): pl.pallas_call(functools.partial(expert_kernel, half, capacity, turn, gra...  4.14 us
    unnamed x12, local copies, waits for them, and re-layouts  2.97 us
    pallas_call x1, Pallas kernels, router(): pl.pallas_call(functools.partial(router_kernel, half, capacity, turn), ou...  1.38 us
    pallas_call x1, Pallas kernels, by_halves(): pl.pallas_call(info_kernel, out_shape=jax.ShapeDtypeStruct((8, LANES), F3...  1.31 us
  transfers between devices with their start and end apart: 13, of which 2 were waited for; matrix products, arithmetic and copies ran while one was open for 0% of the time, Pallas kernels for 14%

profile of v3, /device:TPU:0, one launch (start us, length us, event | category | flops | bytes accessed | tf_op | source)
XLA Modules:
  0.0 55.9 jit_solution(16667728096229502819)
XLA Ops:
  0.6 2.5 %collective-permute-start.5 = (bf16[128,2048]{1,0:T(8,128)(2,1)}, bf16[128,2048]{1,0:T(8,128)(2,1)S(1)}, u32[]{:S(2)}, u32[]{:S(2)}) collective-permute-start(bf16[128,2048]{1,0:T(8,128)(2,1)} %bitcast.23), channel_id=1, source_target_pairs={{0,24},{1,25},{2,26},{3,27},{4,28},{5,29},{6,30},{7,31},{8,0},{9,1... | collective-permute-start | bytes 1572872 | tf_op jit(solution)/shard_map/ppermute | solution.py:301
  3.1 1.3 %info.1.info_ref = f32[8,128]{1,0:T(8,128)} custom-call(s32[2,128]{1,0:T(2,128)} %bitcast.22, f32[8,128]{1,0:T(8,128)} %bitcast.21), custom_call_target="tpu_custom_call" | custom-call | tf_op jit(solution)/shard_map/info/pallas_call | solution.py:318
  4.4 0.0 copy-start.4
  4.4 3.7 %collective-permute-start.1 = (bf16[128,2048]{1,0:T(8,128)(2,1)}, bf16[128,2048]{1,0:T(8,128)(2,1)S(1)}, u32[]{:S(2)}, u32[]{:S(2)}) collective-permute-start(bf16[128,2048]{1,0:T(8,128)(2,1)} %bitcast.24), channel_id=1, source_target_pairs={{0,30},{1,31},{2,28},{3,29},{4,26},{5,27},{6,24},{7,25},{8,6},{9,7... | collective-permute-start | bytes 1572872 | tf_op jit(solution)/shard_map/ppermute | solution.py:301
  8.1 0.0 copy-start
  8.1 1.9 %copy-done = bf16[1,768,2048]{2,1,0:T(8,128)(2,1)S(1)} copy-done((bf16[1,768,2048]{2,1,0:T(8,128)(2,1)S(1)}, bf16[1,768,2048]{2,1,0:T(8,128)(2,1)}, u32[]{:S(2)}) %copy-start) | copy-done | bytes 3145752
  10.0 0.0 copy-start.2
  10.0 1.1 %copy-done.2 = bf16[1,384,768]{2,1,0:T(8,128)(2,1)S(1)} copy-done((bf16[1,384,768]{2,1,0:T(8,128)(2,1)S(1)}, bf16[1,384,768]{2,1,0:T(8,128)(2,1)}, u32[]{:S(2)}) %copy-start.2) | copy-done | bytes 589848
  11.1 0.9 %back.1 = (bf16[96,2176]{1,0:T(8,128)(2,1)S(1)}, bf16[96,2176]{1,0:T(8,128)(2,1)S(1)}, bf16[96,2176]{1,0:T(8,128)(2,1)S(1)}, bf16[96,2176]{1,0:T(8,128)(2,1)S(1)}) custom-call(s32[1]{0:T(128)} %bitcast.me_ref, bf16[2,2,96,768]{3,2,1,0:T(8,128)(2,1)S(1)} %bitcast.16, bf16[768,2048]{1,0:T(8,128)(2,1)S(1)} %bitcast.13), custom_call_target="tpu_custom_call" | custom-call | tf_op jit(solution)/shard_map/back/pallas_call | solution.py:125
  12.0 0.0 copy-start.1
  12.0 0.0 copy-start.3
  12.0 0.0 collective-permute-done.5.token_ref
  12.0 0.0 copy-done.4
  12.0 0.5 pack_own.1
  12.5 1.6 %collective-permute-start.6 = (bf16[96,2176]{1,0:T(8,128)(2,1)S(1)}, bf16[96,2176]{1,0:T(8,128)(2,1)S(1)}, u32[]{:S(2)}, u32[]{:S(2)}) collective-permute-start(bf16[96,2176]{1,0:T(8,128)(2,1)S(1)} %get-tuple-element.30), channel_id=1, source_target_pairs={{0,1},{1,0},{2,3},{3,2},{4,5},{5,4},{6,7},{7,6},{8,9},{9,8},{10,11... | collective-permute-start | bytes 1253384 | tf_op jit(solution)/shard_map/ppermute | solution.py:301
  14.1 0.0 collective-permute-start.7
  14.1 2.0 %collective-permute-start.8 = (bf16[96,2176]{1,0:T(8,128)(2,1)S(1)}, bf16[96,2176]{1,0:T(8,128)(2,1)S(1)}, u32[]{:S(2)}, u32[]{:S(2)}) collective-permute-start(bf16[96,2176]{1,0:T(8,128)(2,1)S(1)} %get-tuple-element.32), channel_id=1, source_target_pairs={{0,3},{1,2},{2,1},{3,0},{4,7},{5,6},{6,5},{7,4},{8,11},{9,10},{10,... | collective-permute-start | bytes 1253384 | tf_op jit(solution)/shard_map/ppermute | solution.py:301
  16.1 2.4 %collective-permute-start = (f32[8,128]{1,0:T(8,128)S(1)}, f32[8,128]{1,0:T(8,128)S(1)}, u32[]{:S(2)}, u32[]{:S(2)}) collective-permute-start(f32[8,128]{1,0:T(8,128)S(1)} %copy-done.4), channel_id=1, source_target_pairs={{0,6},{1,7},{2,4},{3,5},{4,2},{5,3},{6,0},{7,1},{8,14},{9,15},{10,... | collective-permute-start | bytes 12296 | tf_op jit(solution)/shard_map/ppermute | solution.py:301
  18.5 20.3 %collective-permute-done.info_ref = f32[8,128]{1,0:T(8,128)S(1)} collective-permute-done((f32[8,128]{1,0:T(8,128)S(1)}, f32[8,128]{1,0:T(8,128)S(1)}, u32[]{:S(2)}, u32[]{:S(2)}) %collective-permute-start) | collective-permute-done | bytes 4128 | tf_op jit(solution)/shard_map/ppermute | solution.py:301
  38.8 0.0 collective-permute-done.1.token_ref
  38.8 0.5 pack_far.1
  39.3 1.5 %collective-permute-start.2 = (bf16[48,2176]{1,0:T(8,128)(2,1)S(1)}, bf16[48,2176]{1,0:T(8,128)(2,1)S(1)}, u32[]{:S(2)}, u32[]{:S(2)}) collective-permute-start(bf16[48,2176]{1,0:T(8,128)(2,1)S(1)} %get-tuple-element.22.refs_1_), channel_id=1, source_target_pairs={{0,1},{1,0},{2,3},{3,2},{4,5},{5,4},{6,7},{7,6},{8,9},{9,8},{10,11... | collective-permute-start | bytes 626696 | tf_op jit(solution)/shard_map/ppermute | solution.py:301
  40.8 0.0 collective-permute-start.3
  40.8 0.0 collective-permute-done.6.refs_5_.refs_1_
  40.8 2.0 %collective-permute-start.4 = (bf16[48,2176]{1,0:T(8,128)(2,1)S(1)}, bf16[48,2176]{1,0:T(8,128)(2,1)S(1)}, u32[]{:S(2)}, u32[]{:S(2)}) collective-permute-start(bf16[48,2176]{1,0:T(8,128)(2,1)S(1)} %get-tuple-element.24.refs_3_), channel_id=1, source_target_pairs={{0,3},{1,2},{2,1},{3,0},{4,7},{5,6},{6,5},{7,4},{8,11},{9,10},{10,... | collective-permute-start | bytes 626696 | tf_op jit(solution)/shard_map/ppermute | solution.py:301
  42.8 0.0 collective-permute-done.7.refs_6_.refs_2_
  42.8 0.0 collective-permute-done.8.refs_7_.refs_3_
  42.8 0.3 far_grad.1.refs_6_
  43.1 0.0 copy-done.1
  43.1 0.0 copy-done.3
  43.1 2.2 %expert_own.1 = (bf16[2,2,96,768]{3,2,1,0:T(8,128)(2,1)}, bf16[48,128]{1,0:T(8,128)(2,1)S(1)}, bf16[48,128]{1,0:T(8,128)(2,1)S(1)}, bf16[48,128]{1,0:T(8,128)(2,1)S(1)}, bf16[48,128]{1,0:T(8,128)(2,1)S(1)}) custom-call(s32[1]{0:T(128)} %bitcast.me_ref, bf16[96,2176]{1,0:T(8,128)(2,1)S(1)} %get-tuple-element.29.refs_4_.refs_0_, ...), custom_call_target="tpu_custom_call" | custom-call | tf_op jit(solution)/shard_map/expert_own/pallas_call | solution.py:236
  45.3 0.0 copy-start.5
  45.3 0.0 collective-permute-start.10
  45.3 2.9 %collective-permute-start.11 = (bf16[48,128]{1,0:T(8,128)(2,1)S(1)}, bf16[48,128]{1,0:T(8,128)(2,1)S(1)}, u32[]{:S(2)}, u32[]{:S(2)}) collective-permute-start(bf16[48,128]{1,0:T(8,128)(2,1)S(1)} %get-tuple-element.37), channel_id=1, source_target_pairs={{0,3},{1,2},{2,1},{3,0},{4,7},{5,6},{6,5},{7,4},{8,11},{9,10},{10,... | collective-permute-start | bytes 36872 | tf_op jit(solution)/shard_map/ppermute | solution.py:301
  48.2 0.0 collective-permute-done.2.refs_1_
  48.2 0.5 collective-permute-start.9
  48.8 0.1 collective-permute-done.3.refs_2_
  48.9 3.6 %collective-permute-start.12 = (bf16[48,128]{1,0:T(8,128)(2,1)S(1)}, bf16[48,128]{1,0:T(8,128)(2,1)S(1)}, u32[]{:S(2)}, u32[]{:S(2)}) collective-permute-start(bf16[48,128]{1,0:T(8,128)(2,1)S(1)} %far_grad.1.refs_6_), channel_id=1, source_target_pairs={{0,6},{1,7},{2,4},{3,5},{4,2},{5,3},{6,0},{7,1},{8,14},{9,15},{10,... | collective-permute-start | bytes 36872 | tf_op jit(solution)/shard_map/ppermute | solution.py:301
  52.5 0.0 collective-permute-done.4.refs_3_
  52.5 2.0 %expert_far.1 = bf16[2,2,96,768]{3,2,1,0:T(8,128)(2,1)} custom-call(s32[1]{0:T(128)} %bitcast.me_ref, bf16[48,2176]{1,0:T(8,128)(2,1)S(1)} %get-tuple-element.21.refs_0_, bf16[48,2176]{1,0:T(8,128)(2,1)S(1)} %collective-permute-done.2.refs_1_, bf16[48,2176]{1,0:T(8,128)(2,1)S(1)} %collective-permute-done.3.refs_2_, ...), custom_call_target="tpu_custom_call", output_to_operand_aliasing={{}: (6, {})} | custom-call | tf_op jit(solution)/shard_map/expert_far/pallas_call | solution.py:236
  54.5 0.0 collective-permute-done.10.refs_2_
  54.5 0.0 collective-permute-done.11.refs_3_
  54.5 0.0 collective-permute-done.9.refs_1_
  54.5 0.0 collective-permute-done.12.refs_4_
  54.5 0.0 copy-done.5
  54.5 1.4 %router.1 = bf16[128,2048]{1,0:T(8,128)(2,1)} custom-call(s32[1]{0:T(128)} %bitcast.me_ref, f32[8,128]{1,0:T(8,128)S(1)} %copy-done.4, bf16[48,128]{1,0:T(8,128)(2,1)S(1)} %get-tuple-element.34.refs_0_, bf16[48,128]{1,0:T(8,128)(2,1)S(1)} %collective-permute-done.9.refs_1_, bf16[48,128]{1,0:T(8,128)(2,1)S(1)} %collective-permute-done.10.refs_2_, ...), custom_call_target="tpu_custom_call" | custom-call | tf_op jit(solution)/shard_map/router/pallas_call | solution.py:286
Async XLA Ops:
  0.6 11.4 %collective-permute-start.5 = (bf16[128,2048]{1,0:T(8,128)(2,1)}, bf16[128,2048]{1,0:T(8,128)(2,1)S(1)}, u32[]{:S(2)}, u32[]{:S(2)}) collective-permute-start(bf16[128,2048]{1,0:T(8,128)(2,1)} %bitcast.23), channel_id=1, source_target_pairs={{0,24},{1,25},{2,26},{3,27},{4,28},{5,29},{6,30},{7,31},{8,0},{9,1... | collective-permute-start | bytes 1572872 | tf_op jit(solution)/shard_map/ppermute | solution.py:301
  4.4 7.6 %copy-start.4 = (f32[8,128]{1,0:T(8,128)S(1)}, f32[8,128]{1,0:T(8,128)}, u32[]{:S(2)}) copy-start(f32[8,128]{1,0:T(8,128)} %info.1.info_ref) | copy-start | bytes 12292
  4.4 34.4 %collective-permute-start.1 = (bf16[128,2048]{1,0:T(8,128)(2,1)}, bf16[128,2048]{1,0:T(8,128)(2,1)S(1)}, u32[]{:S(2)}, u32[]{:S(2)}) collective-permute-start(bf16[128,2048]{1,0:T(8,128)(2,1)} %bitcast.24), channel_id=1, source_target_pairs={{0,30},{1,31},{2,28},{3,29},{4,26},{5,27},{6,24},{7,25},{8,6},{9,7... | collective-permute-start | bytes 1572872 | tf_op jit(solution)/shard_map/ppermute | solution.py:301
  8.1 1.9 %copy-start = (bf16[1,768,2048]{2,1,0:T(8,128)(2,1)S(1)}, bf16[1,768,2048]{2,1,0:T(8,128)(2,1)}, u32[]{:S(2)}) copy-start(bf16[1,768,2048]{2,1,0:T(8,128)(2,1)} %param.10) | copy-start | bytes 9437188
  10.0 1.1 %copy-start.2 = (bf16[1,384,768]{2,1,0:T(8,128)(2,1)S(1)}, bf16[1,384,768]{2,1,0:T(8,128)(2,1)}, u32[]{:S(2)}) copy-start(bf16[1,384,768]{2,1,0:T(8,128)(2,1)} %param.9) | copy-start | bytes 1769476
  12.0 31.1 %copy-start.1 = (bf16[1,768,2048]{2,1,0:T(8,128)(2,1)S(1)}, bf16[1,768,2048]{2,1,0:T(8,128)(2,1)}, u32[]{:S(2)}) copy-start(bf16[1,768,2048]{2,1,0:T(8,128)(2,1)} %param.10) | copy-start | bytes 9437188
  12.0 31.1 %copy-start.3 = (bf16[1,384,768]{2,1,0:T(8,128)(2,1)S(1)}, bf16[1,384,768]{2,1,0:T(8,128)(2,1)}, u32[]{:S(2)}) copy-start(bf16[1,384,768]{2,1,0:T(8,128)(2,1)} %param.9) | copy-start | bytes 1769476
  12.5 28.3 %collective-permute-start.6 = (bf16[96,2176]{1,0:T(8,128)(2,1)S(1)}, bf16[96,2176]{1,0:T(8,128)(2,1)S(1)}, u32[]{:S(2)}, u32[]{:S(2)}) collective-permute-start(bf16[96,2176]{1,0:T(8,128)(2,1)S(1)} %get-tuple-element.30), channel_id=1, source_target_pairs={{0,1},{1,0},{2,3},{3,2},{4,5},{5,4},{6,7},{7,6},{8,9},{9,8},{10,11... | collective-permute-start | bytes 1253384 | tf_op jit(solution)/shard_map/ppermute | solution.py:301
  14.1 28.8 %collective-permute-start.7 = (bf16[96,2176]{1,0:T(8,128)(2,1)S(1)}, bf16[96,2176]{1,0:T(8,128)(2,1)S(1)}, u32[]{:S(2)}, u32[]{:S(2)}) collective-permute-start(bf16[96,2176]{1,0:T(8,128)(2,1)S(1)} %get-tuple-element.31), channel_id=1, source_target_pairs={{0,2},{1,3},{2,0},{3,1},{4,6},{5,7},{6,4},{7,5},{8,10},{9,11},{10,... | collective-permute-start | bytes 1253384 | tf_op jit(solution)/shard_map/ppermute | solution.py:301
  14.1 28.8 %collective-permute-start.8 = (bf16[96,2176]{1,0:T(8,128)(2,1)S(1)}, bf16[96,2176]{1,0:T(8,128)(2,1)S(1)}, u32[]{:S(2)}, u32[]{:S(2)}) collective-permute-start(bf16[96,2176]{1,0:T(8,128)(2,1)S(1)} %get-tuple-element.32), channel_id=1, source_target_pairs={{0,3},{1,2},{2,1},{3,0},{4,7},{5,6},{6,5},{7,4},{8,11},{9,10},{10,... | collective-permute-start | bytes 1253384 | tf_op jit(solution)/shard_map/ppermute | solution.py:301
  16.1 22.7 %collective-permute-start = (f32[8,128]{1,0:T(8,128)S(1)}, f32[8,128]{1,0:T(8,128)S(1)}, u32[]{:S(2)}, u32[]{:S(2)}) collective-permute-start(f32[8,128]{1,0:T(8,128)S(1)} %copy-done.4), channel_id=1, source_target_pairs={{0,6},{1,7},{2,4},{3,5},{4,2},{5,3},{6,0},{7,1},{8,14},{9,15},{10,... | collective-permute-start | bytes 12296 | tf_op jit(solution)/shard_map/ppermute | solution.py:301
  39.3 9.0 %collective-permute-start.2 = (bf16[48,2176]{1,0:T(8,128)(2,1)S(1)}, bf16[48,2176]{1,0:T(8,128)(2,1)S(1)}, u32[]{:S(2)}, u32[]{:S(2)}) collective-permute-start(bf16[48,2176]{1,0:T(8,128)(2,1)S(1)} %get-tuple-element.22.refs_1_), channel_id=1, source_target_pairs={{0,1},{1,0},{2,3},{3,2},{4,5},{5,4},{6,7},{7,6},{8,9},{9,8},{10,11... | collective-permute-start | bytes 626696 | tf_op jit(solution)/shard_map/ppermute | solution.py:301
  40.8 8.1 %collective-permute-start.3 = (bf16[48,2176]{1,0:T(8,128)(2,1)S(1)}, bf16[48,2176]{1,0:T(8,128)(2,1)S(1)}, u32[]{:S(2)}, u32[]{:S(2)}) collective-permute-start(bf16[48,2176]{1,0:T(8,128)(2,1)S(1)} %get-tuple-element.23.refs_2_), channel_id=1, source_target_pairs={{0,2},{1,3},{2,0},{3,1},{4,6},{5,7},{6,4},{7,5},{8,10},{9,11},{10,... | collective-permute-start | bytes 626696 | tf_op jit(solution)/shard_map/ppermute | solution.py:301
  40.8 11.7 %collective-permute-start.4 = (bf16[48,2176]{1,0:T(8,128)(2,1)S(1)}, bf16[48,2176]{1,0:T(8,128)(2,1)S(1)}, u32[]{:S(2)}, u32[]{:S(2)}) collective-permute-start(bf16[48,2176]{1,0:T(8,128)(2,1)S(1)} %get-tuple-element.24.refs_3_), channel_id=1, source_target_pairs={{0,3},{1,2},{2,1},{3,0},{4,7},{5,6},{6,5},{7,4},{8,11},{9,10},{10,... | collective-permute-start | bytes 626696 | tf_op jit(solution)/shard_map/ppermute | solution.py:301
  45.3 9.2 %copy-start.5 = (bf16[2048,8]{0,1:T(8,128)(2,1)S(1)}, bf16[2048,8]{0,1:T(8,128)(2,1)}, u32[]{:S(2)}) copy-start(bf16[2048,8]{0,1:T(8,128)(2,1)} %param.11) | copy-start | bytes 98308
  45.3 9.2 %collective-permute-start.10 = (bf16[48,128]{1,0:T(8,128)(2,1)S(1)}, bf16[48,128]{1,0:T(8,128)(2,1)S(1)}, u32[]{:S(2)}, u32[]{:S(2)}) collective-permute-start(bf16[48,128]{1,0:T(8,128)(2,1)S(1)} %get-tuple-element.36), channel_id=1, source_target_pairs={{0,2},{1,3},{2,0},{3,1},{4,6},{5,7},{6,4},{7,5},{8,10},{9,11},{10,... | collective-permute-start | bytes 36872 | tf_op jit(solution)/shard_map/ppermute | solution.py:301
  45.3 9.2 %collective-permute-start.11 = (bf16[48,128]{1,0:T(8,128)(2,1)S(1)}, bf16[48,128]{1,0:T(8,128)(2,1)S(1)}, u32[]{:S(2)}, u32[]{:S(2)}) collective-permute-start(bf16[48,128]{1,0:T(8,128)(2,1)S(1)} %get-tuple-element.37), channel_id=1, source_target_pairs={{0,3},{1,2},{2,1},{3,0},{4,7},{5,6},{6,5},{7,4},{8,11},{9,10},{10,... | collective-permute-start | bytes 36872 | tf_op jit(solution)/shard_map/ppermute | solution.py:301
  48.2 6.3 %collective-permute-start.9 = (bf16[48,128]{1,0:T(8,128)(2,1)S(1)}, bf16[48,128]{1,0:T(8,128)(2,1)S(1)}, u32[]{:S(2)}, u32[]{:S(2)}) collective-permute-start(bf16[48,128]{1,0:T(8,128)(2,1)S(1)} %get-tuple-element.35), channel_id=1, source_target_pairs={{0,1},{1,0},{2,3},{3,2},{4,5},{5,4},{6,7},{7,6},{8,9},{9,8},{10,11... | collective-permute-start | bytes 36872 | tf_op jit(solution)/shard_map/ppermute | solution.py:301
  48.9 5.6 %collective-permute-start.12 = (bf16[48,128]{1,0:T(8,128)(2,1)S(1)}, bf16[48,128]{1,0:T(8,128)(2,1)S(1)}, u32[]{:S(2)}, u32[]{:S(2)}) collective-permute-start(bf16[48,128]{1,0:T(8,128)(2,1)S(1)} %far_grad.1.refs_6_), channel_id=1, source_target_pairs={{0,6},{1,7},{2,4},{3,5},{4,2},{5,3},{6,0},{7,1},{8,14},{9,15},{10,... | collective-permute-start | bytes 36872 | tf_op jit(solution)/shard_map/ppermute | solution.py:301

commit v4 on v3

--- a/solution.py
+++ b/solution.py
@@ -14,6 +14,8 @@
 F32, BF16 = jnp.float32, jnp.bfloat16
 VMEM_LIMIT = 16 * 1024 * 1024
 COLUMN = 256
+SCALE = 3
+OWN_ORDER, BACK_ORDER, FAR_ORDER = (0, 1, 2, 3), (0, 3, 2, 1), (0, 3, 2, 1)
 
 
 def iota(shape, axis):
@@ -63,7 +65,7 @@
 
 
 def pack_kernel(half, capacity, me_ref, info_ref, token_ref, *refs):
-    outs = refs[-half:]
+    grads, outs = refs[:-half], refs[-half:]
     rows = jnp.bitwise_xor(me_ref[0], iota((8, LANES), 0))
     rank, weight = ranks(info_ref[...], rows)
     pieces, scales = [], []
@@ -76,29 +78,26 @@
     chosen = jnp.concatenate(pieces, axis=0).astype(BF16)
     packed = jnp.dot(chosen, token_ref[...], preferred_element_type=F32).astype(BF16)
     size = MICRO * capacity
+    lane = iota((size, LANES), 1)
     for j in range(half):
         outs[j][:, 0:width] = packed[j * size : (j + 1) * size]
-        outs[j][:, width:] = jnp.concatenate(scales[j * MICRO : (j + 1) * MICRO], axis=0).astype(BF16)
-
-
-def pack(me, info, tokens, half, capacity, name, into=()):
-    rows, width = MICRO * capacity, tokens.shape[1] + LANES
-    at = 1 if into else 0
+        tail = jnp.concatenate(scales[j * MICRO : (j + 1) * MICRO], axis=0)
+        if grads:
+            tail = jnp.where(lane < SCALE, grads[j][...].astype(F32), tail)
+        outs[j][:, width:] = tail.astype(BF16)
+
+
+def pack(me, info, tokens, half, capacity, name, grads=()):
+    block = jax.ShapeDtypeStruct((MICRO * capacity, tokens.shape[1] + LANES), BF16)
+    vmem = pl.BlockSpec(memory_space=pltpu.VMEM)
     return pl.pallas_call(
         functools.partial(pack_kernel, half, capacity),
-        grid=(1,),
-        out_shape=[jax.ShapeDtypeStruct(((1 + at) * rows, width), BF16)] * half,
-        in_specs=[
-            pl.BlockSpec(memory_space=pltpu.SMEM),
-            pl.BlockSpec(info.shape, lambda i: (0, 0)),
-            pl.BlockSpec(tokens.shape, lambda i: (0, 0)),
-        ]
-        + [pl.BlockSpec(memory_space=pl.ANY)] * len(into),
-        out_specs=[pl.BlockSpec((rows, width), lambda i: (at, 0))] * half,
-        input_output_aliases={3 + j: j for j in range(len(into))},
+        out_shape=[block] * half,
+        in_specs=[pl.BlockSpec(memory_space=pltpu.SMEM)] + [vmem] * (2 + len(grads)),
+        out_specs=[vmem] * half,
         compiler_params=pltpu.CompilerParams(vmem_limit_bytes=VMEM_LIMIT),
         name=name,
-    )(me, info, tokens, *into)
+    )(me, info, tokens, *grads)
 
 
 def chunks(width):
@@ -134,14 +133,33 @@
             out_specs=[pl.BlockSpec((rows, width), lambda i, me: (0, 0))] * half,
             scratch_shapes=[pltpu.VMEM((MICRO * run, width), F32)],
         ),
-        out_shape=[jax.ShapeDtypeStruct((2 * rows, width + LANES), BF16)] * half,
+        out_shape=[jax.ShapeDtypeStruct((rows, width), BF16)] * half,
         compiler_params=pltpu.CompilerParams(vmem_limit_bytes=VMEM_LIMIT),
         name="back",
     )(me, saved, weight)
 
 
+def turn_kernel(w_ref, after_ref, out_ref):
+    del after_ref
+    for columns in chunks(w_ref.shape[1]):
+        out_ref[columns, :] = w_ref[:, columns].T
+
+
+def turned(weight, after):
+    vmem = pl.BlockSpec(memory_space=pltpu.VMEM)
+    return pl.pallas_call(
+        turn_kernel,
+        out_shape=jax.ShapeDtypeStruct(weight.shape[::-1], BF16),
+        in_specs=[vmem, pl.BlockSpec(memory_space=pl.ANY)],
+        out_specs=vmem,
+        compiler_params=pltpu.CompilerParams(vmem_limit_bytes=VMEM_LIMIT),
+        name="turned",
+    )(weight, after)
+
+
 def far_grad_kernel(half, capacity, *refs):
-    blocks, backs, (grad_ref,) = refs[:half], refs[half : 2 * half], refs[2 * half :]
+    blocks, (grad_ref,) = refs[:half], refs[2 * half :]
+    backs = [refs[half + BACK_ORDER.index(j)] for j in range(half)]
     width = blocks[0].shape[1] - LANES
     rows = MICRO * capacity
     where = iota((rows, LANES), 1)
@@ -158,25 +176,24 @@
 
 def far_grad(blocks, backs, half, capacity):
     vmem = pl.BlockSpec(memory_space=pltpu.VMEM)
-    rows, width = blocks[0].shape
     return pl.pallas_call(
         functools.partial(far_grad_kernel, half, capacity),
-        grid=(1,),
-        out_shape=jax.ShapeDtypeStruct((rows, LANES), BF16),
-        in_specs=[vmem] * half + [pl.BlockSpec((rows, width), lambda i: (0, 0))] * half,
+        out_shape=jax.ShapeDtypeStruct((MICRO * capacity, LANES), BF16),
+        in_specs=[vmem] * (2 * half),
         out_specs=vmem,
         compiler_params=pltpu.CompilerParams(vmem_limit_bytes=VMEM_LIMIT),
         name="far_grad",
-    )(*blocks, *backs)
+    )(*blocks, *[backs[j] for j in BACK_ORDER])
 
 
 def expert_kernel(half, capacity, turn, graded, me_ref, *refs):
-    blocks, w_ref, refs = refs[:half], refs[half], refs[half + 1 :]
+    order = OWN_ORDER if graded else FAR_ORDER
+    blocks, w_ref, refs = [refs[order.index(j)] for j in range(half)], refs[half], refs[half + 1 :]
     if graded:
-        saved_ref, _, d_ref, *grads, lhs, product, scale, partial = refs
+        saved_ref, d_ref, *grads, lhs, product, scale, partial = refs
     else:
         _, d_ref, lhs, product, scale = refs
-    hidden_width, width = w_ref.shape
+    width, hidden_width = w_ref.shape
     run = half * capacity
     here = jnp.bitwise_xor(lax.rem(me_ref[0], half), turn)
     places = []
@@ -187,9 +204,10 @@
     for j in range(half):
         lhs[j * MICRO * capacity : (j + 1) * MICRO * capacity, :] = blocks[j][:, 0:width]
     for j, row, _, slot in places:
-        scale[pl.ds(slot, capacity), :] = blocks[j][row : row + capacity, width:].astype(F32)
+        tail = blocks[j][row : row + capacity, width:].astype(F32)
+        scale[pl.ds(slot, capacity), :] = jnp.broadcast_to(tail[:, SCALE : SCALE + 1], tail.shape)
     for columns in chunks(hidden_width):
-        got = lax.dot_general(lhs[...], w_ref[columns, :], (((1,), (1,)), ((), ())), preferred_element_type=F32)
+        got = jnp.dot(lhs[...], w_ref[:, columns], preferred_element_type=F32)
         for _, _, begin, slot in places:
             product[pl.ds(slot, capacity), columns] = got[begin : begin + capacity, :]
     total = jnp.zeros((MICRO * run, LANES), F32)
@@ -210,16 +228,14 @@
             grads[j][row : row + capacity, :] = table.astype(BF16)
 
 
-def expert(me, blocks, weight, half, capacity, turn, saved=None, wait=None, held=None):
-    hidden_width, width = weight.shape
+def expert(me, blocks, weight, half, capacity, turn, saved=None, held=None):
+    width, hidden_width = weight.shape
     run, rows = half * capacity, MICRO * capacity
     graded = held is None
-    row_block = 1 if graded else 0
     anywhere = pl.BlockSpec(memory_space=pl.ANY)
     side = (lambda me: me[0] // half) if graded else (lambda me: 1 - me[0] // half)
     slots = pl.BlockSpec((MICRO, 1, run, hidden_width), lambda i, me: (0, side(me), 0, 0))
-    in_specs = [pl.BlockSpec((rows, width + LANES), lambda i, me: (row_block, 0))] * half
-    in_specs += [pl.BlockSpec(memory_space=pltpu.VMEM)]
+    in_specs = [pl.BlockSpec(memory_space=pltpu.VMEM)] * (half + 1)
     scratch = [
         pltpu.VMEM((MICRO * run, width), BF16),
         pltpu.VMEM((MICRO * run, hidden_width), F32),
@@ -229,7 +245,7 @@
         out_shape = [jax.ShapeDtypeStruct(saved.shape, BF16)] + [jax.ShapeDtypeStruct((rows, LANES), BF16)] * half
         out_specs = [slots] + [pl.BlockSpec((rows, LANES), lambda i, me: (0, 0))] * half
         scratch.append(pltpu.VMEM((MICRO * run, LANES), F32))
-        operands, in_specs, aliases = [saved, wait], in_specs + [slots, anywhere], {}
+        operands, in_specs, aliases = [saved], in_specs + [slots], {}
     else:
         out_shape, out_specs = [jax.ShapeDtypeStruct(held.shape, BF16)], [slots]
         operands, in_specs, aliases = [held], in_specs + [anywhere], {half + 2: 0}
@@ -246,7 +262,7 @@
         input_output_aliases=aliases,
         compiler_params=pltpu.CompilerParams(vmem_limit_bytes=VMEM_LIMIT),
         name="expert_own" if graded else "expert_far",
-    )(me, *blocks, weight, *operands)
+    )(me, *[blocks[j] for j in (OWN_ORDER if graded else FAR_ORDER)], weight, *operands)
 
 
 def router_kernel(half, capacity, turn, me_ref, info_ref, *refs):
@@ -282,11 +298,14 @@
 
 
 def router(me, info, own, far, table, tokens, half, capacity, turn):
+    width = tokens.shape[1]
     vmem = pl.BlockSpec(memory_space=pltpu.VMEM)
+    tail = pl.BlockSpec((MICRO * capacity, LANES), lambda i: (0, width // LANES))
     return pl.pallas_call(
         functools.partial(router_kernel, half, capacity, turn),
+        grid=(1,),
         out_shape=jax.ShapeDtypeStruct(tokens.shape, BF16),
-        in_specs=[pl.BlockSpec(memory_space=pltpu.SMEM)] + [vmem] * (half + 3),
+        in_specs=[pl.BlockSpec(memory_space=pltpu.SMEM), vmem] + [tail] * half + [vmem] * 2,
         out_specs=vmem,
         compiler_params=pltpu.CompilerParams(vmem_limit_bytes=VMEM_LIMIT),
         name="router",
@@ -314,7 +333,6 @@
     def spread(blocks):
         return [blocks[0]] + [route(blocks[j], j, 0) for j in range(1, half)]
 
-    own_tokens = route(tokens, 0, 1)
     info = pl.pallas_call(
         info_kernel,
         out_shape=jax.ShapeDtypeStruct((8, LANES), F32),
@@ -322,18 +340,21 @@
         out_specs=vmem,
         name="info",
     )(routes[0].T, router_probs[0].T)
+    next_info = route(info, 0, -1)
     far_info = route(info, half + turn, 0)
-    far_tokens = route(lax.optimization_barrier((tokens, info))[0], half + turn, 1)
+    far_tokens = route(tokens, half + turn, 1)
+    packed = pack(me, next_info, tokens, half, capacity, "pack_own")
+    weight_t = turned(weight, packed[0])
+    saved, packed = lax.optimization_barrier((saved, packed))
     backs = back(me, saved, weight, half, capacity, turn)
-    near = spread(pack(me, info, own_tokens, half, capacity, "pack_own", backs))
-    far = pack(me, far_info, far_tokens, half, capacity, "pack_far")
-    far_own = far_grad(far, near, half, capacity)
-    far_grads = route(far_own, half + turn, 0)
+    own = [route(packed[j], j, 1) for j in range(half)]
+    backs = spread(backs)
+    held, *own_grads = expert(me, own, weight_t, half, capacity, 0, saved=saved)
+    far = pack(me, far_info, far_tokens, half, capacity, "pack_far", own_grads)
+    far_grads = route(far_grad(far, backs, half, capacity), half + turn, 0)
     far = spread(far)
-    held, *own_grads = expert(me, near, weight, half, capacity, 0, saved=saved, wait=far_own)
-    own_grads = spread(own_grads)
-    (d_hidden,) = expert(me, far, weight, half, capacity, turn, held=held)
-    grad_in = router(me, info, own_grads, far_grads, w_router.T, tokens, half, capacity, turn)
+    (d_hidden,) = expert(me, far, weight_t, half, capacity, turn, held=held)
+    grad_in = router(me, info, far, far_grads, w_router.T, tokens, half, capacity, turn)
     return d_hidden.reshape(saved_hidden.shape), grad_in[None]
 
 

time: 56.2 us -> 49.1 us (0.87)
  waiting for transfers between devices: 20.4 us -> 13.2 us
  starting transfers between devices: 22.8 us -> 21.7 us
  local copies, waits for them, and re-layouts: 2.97 us -> 4.01 us
    ppermute x13 -> x14, waiting for transfers between devices: 20.4 us -> 13.2 us  [route(): return lax.ppermute(block, ('pipe', 'expert'), pairs)]
    ppermute x13 -> x14, starting transfers between devices: 22.8 us -> 21.7 us  [route(): return lax.ppermute(block, ('pipe', 'expert'), pairs)]
    unnamed x12 -> x14, local copies, waits for them, and re-layouts: 2.97 us -> 4.01 us
    pallas_call x4 -> x5, Pallas kernels: 2.65 us -> 3.52 us  [the longest x1 1.41 us: router(): pl.pallas_call(functools.partial(router_kernel, half, capacity, turn), gr...]
    pallas_call x2, Pallas kernels: 4.14 us -> 3.37 us  [expert(): pl.pallas_call(functools.partial(expert_kernel, half, capacity, turn, gra...]
  transfers between devices with their start and end apart: 13 -> 14, of which waited for: 2 -> 8; matrix products, arithmetic and copies ran while one was open for 0% -> 0% of each run, Pallas kernels for 14% -> 16%
where the time goes in v4:
time: 49.1 us; the launch traced here: 48.8 us
  starting transfers between devices  21.7 us (44%)
  waiting for transfers between devices  13.2 us (27%)
  Pallas kernels  9.1 us (19%)
  local copies, waits for them, and re-layouts  4.01 us (8%)
  between operations  0.7 us (1%)
    ppermute x14, starting transfers between devices, route(): return lax.ppermute(block, ('pipe', 'expert'), pairs)  21.7 us
    ppermute x14, waiting for transfers between devices, route(): return lax.ppermute(block, ('pipe', 'expert'), pairs)  13.2 us
    unnamed x14, local copies, waits for them, and re-layouts  4.01 us
    pallas_call x2, Pallas kernels, expert(): pl.pallas_call(functools.partial(expert_kernel, half, capacity, turn, gra...  3.37 us
    pallas_call x1, Pallas kernels, router(): pl.pallas_call(functools.partial(router_kernel, half, capacity, turn), gr...  1.41 us
    pallas_call x1, Pallas kernels, by_halves(): pl.pallas_call(info_kernel, out_shape=jax.ShapeDtypeStruct((8, LANES), F3...  1.31 us
  transfers between devices with their start and end apart: 14, of which 8 were waited for; matrix products, arithmetic and copies ran while one was open for 0% of the time, Pallas kernels for 16%

profile of v4, /device:TPU:0, one launch (start us, length us, event | category | flops | bytes accessed | tf_op | source)
XLA Modules:
  0.0 48.8 jit_solution(14734819557605876087)
XLA Ops:
  0.6 5.5 %collective-permute-start.1 = (bf16[128,2048]{1,0:T(8,128)(2,1)}, bf16[128,2048]{1,0:T(8,128)(2,1)S(1)}, u32[]{:S(2)}, u32[]{:S(2)}) collective-permute-start(bf16[128,2048]{1,0:T(8,128)(2,1)} %bitcast.17), channel_id=1, source_target_pairs={{0,30},{1,31},{2,28},{3,29},{4,26},{5,27},{6,24},{7,25},{8,6},{9,7... | collective-permute-start | bytes 1572872 | tf_op jit(solution)/shard_map/ppermute | solution.py:320
  6.1 1.3 %info.1.info_ref = f32[8,128]{1,0:T(8,128)} custom-call(s32[2,128]{1,0:T(2,128)} %bitcast.23, f32[8,128]{1,0:T(8,128)} %bitcast.22), custom_call_target="tpu_custom_call" | custom-call | tf_op jit(solution)/shard_map/info/pallas_call | solution.py:336
  7.4 0.0 copy-start.6
  7.4 0.0 collective-permute-start.2
  7.4 3.3 %collective-permute-done.2.info_ref = f32[8,128]{1,0:T(8,128)S(1)} collective-permute-done((f32[8,128]{1,0:T(8,128)}, f32[8,128]{1,0:T(8,128)S(1)}, u32[]{:S(2)}, u32[]{:S(2)}) %collective-permute-start.2) | collective-permute-done | bytes 4128 | tf_op jit(solution)/shard_map/ppermute | solution.py:320
  10.7 0.0 copy-start.4
  10.7 1.0 %copy-done.4 = bf16[1,128,2048]{2,1,0:T(8,128)(2,1)S(1)} copy-done((bf16[1,128,2048]{2,1,0:T(8,128)(2,1)S(1)}, bf16[1,128,2048]{2,1,0:T(8,128)(2,1)}, u32[]{:S(2)}) %copy-start.4) | copy-done | bytes 524312
  11.8 0.5 pack_own.1
  12.3 0.1 collective-permute-start.3
  12.3 1.5 %collective-permute-start.4 = (bf16[48,2176]{1,0:T(8,128)(2,1)S(1)}, bf16[48,2176]{1,0:T(8,128)(2,1)S(1)}, u32[]{:S(2)}, u32[]{:S(2)}) collective-permute-start(bf16[48,2176]{1,0:T(8,128)(2,1)S(1)} %get-tuple-element.29), channel_id=1, source_target_pairs={{0,25},{1,24},{2,27},{3,26},{4,29},{5,28},{6,31},{7,30},{8,1},{9,0... | collective-permute-start | bytes 626696 | tf_op jit(solution)/shard_map/ppermute | solution.py:320
  13.9 0.0 collective-permute-start.5
  13.9 2.7 %collective-permute-start.6 = (bf16[48,2176]{1,0:T(8,128)(2,1)S(1)}, bf16[48,2176]{1,0:T(8,128)(2,1)S(1)}, u32[]{:S(2)}, u32[]{:S(2)}) collective-permute-start(bf16[48,2176]{1,0:T(8,128)(2,1)S(1)} %get-tuple-element.31), channel_id=1, source_target_pairs={{0,27},{1,26},{2,25},{3,24},{4,31},{5,30},{6,29},{7,28},{8,3},{9,2... | collective-permute-start | bytes 626696 | tf_op jit(solution)/shard_map/ppermute | solution.py:320
  16.5 0.0 copy-start
  16.5 1.9 %copy-done = bf16[1,768,2048]{2,1,0:T(8,128)(2,1)S(1)} copy-done((bf16[1,768,2048]{2,1,0:T(8,128)(2,1)S(1)}, bf16[1,768,2048]{2,1,0:T(8,128)(2,1)}, u32[]{:S(2)}) %copy-start) | copy-done | bytes 3145752
  18.4 0.0 copy-start.2
  18.4 1.1 %copy-done.2 = bf16[1,384,768]{2,1,0:T(8,128)(2,1)S(1)} copy-done((bf16[1,384,768]{2,1,0:T(8,128)(2,1)S(1)}, bf16[1,384,768]{2,1,0:T(8,128)(2,1)}, u32[]{:S(2)}) %copy-start.2) | copy-done | bytes 589848
  19.5 0.0 copy-start.1
  19.5 0.9 %back.1 = (bf16[48,2048]{1,0:T(8,128)(2,1)S(1)}, bf16[48,2048]{1,0:T(8,128)(2,1)S(1)}, bf16[48,2048]{1,0:T(8,128)(2,1)S(1)}, bf16[48,2048]{1,0:T(8,128)(2,1)S(1)}) custom-call(s32[1]{0:T(128)} %bitcast.me_ref, bf16[2,2,96,768]{3,2,1,0:T(8,128)(2,1)S(1)} %bitcast.15, bf16[768,2048]{1,0:T(8,128)(2,1)S(1)} %bitcast.13), custom_call_target="tpu_custom_call" | custom-call | tf_op jit(solution)/shard_map/back/pallas_call | solution.py:124
  20.4 2.2 %collective-permute-done.3.refs_0_ = bf16[48,2176]{1,0:T(8,128)(2,1)S(1)} collective-permute-done((bf16[48,2176]{1,0:T(8,128)(2,1)S(1)}, bf16[48,2176]{1,0:T(8,128)(2,1)S(1)}, u32[]{:S(2)}, u32[]{:S(2)}) %collective-permute-start.3) | collective-permute-done | bytes 208928 | tf_op jit(solution)/shard_map/ppermute | solution.py:320
  22.6 0.0 copy-start.3
  22.6 0.0 collective-permute-start.10
  22.6 0.0 collective-permute-done.4.refs_1_
  22.6 0.0 copy-done.6
  22.6 0.8 %collective-permute-start = (f32[8,128]{1,0:T(8,128)S(1)}, f32[8,128]{1,0:T(8,128)S(1)}, u32[]{:S(2)}, u32[]{:S(2)}) collective-permute-start(f32[8,128]{1,0:T(8,128)S(1)} %copy-done.6), channel_id=1, source_target_pairs={{0,6},{1,7},{2,4},{3,5},{4,2},{5,3},{6,0},{7,1},{8,14},{9,15},{10,... | collective-permute-start | bytes 12296 | tf_op jit(solution)/shard_map/ppermute | solution.py:320
  23.4 0.0 copy-done.1
  23.4 0.9 %turned.1.refs_4_ = bf16[2048,768]{1,0:T(8,128)(2,1)S(1)} custom-call(bf16[768,2048]{1,0:T(8,128)(2,1)S(1)} %bitcast.14, bf16[48,2176]{1,0:T(8,128)(2,1)S(1)} %get-tuple-element.28.after_ref), custom_call_target="tpu_custom_call" | custom-call | tf_op jit(solution)/shard_map/turned/pallas_call | solution.py:150
  24.3 0.0 collective-permute-done.5.refs_2_
  24.3 3.0 %collective-permute-start.11 = (bf16[48,2048]{1,0:T(8,128)(2,1)S(1)}, bf16[48,2048]{1,0:T(8,128)(2,1)S(1)}, u32[]{:S(2)}, u32[]{:S(2)}) collective-permute-start(bf16[48,2048]{1,0:T(8,128)(2,1)S(1)} %get-tuple-element.44), channel_id=1, source_target_pairs={{0,2},{1,3},{2,0},{3,1},{4,6},{5,7},{6,4},{7,5},{8,10},{9,11},{10,... | collective-permute-start | bytes 589832 | tf_op jit(solution)/shard_map/ppermute | solution.py:320
  27.3 1.0 %collective-permute-done.6.refs_3_ = bf16[48,2176]{1,0:T(8,128)(2,1)S(1)} collective-permute-done((bf16[48,2176]{1,0:T(8,128)(2,1)S(1)}, bf16[48,2176]{1,0:T(8,128)(2,1)S(1)}, u32[]{:S(2)}, u32[]{:S(2)}) %collective-permute-start.6) | collective-permute-done | bytes 208928 | tf_op jit(solution)/shard_map/ppermute | solution.py:320
  28.3 0.8 %collective-permute-start.12 = (bf16[48,2048]{1,0:T(8,128)(2,1)S(1)}, bf16[48,2048]{1,0:T(8,128)(2,1)S(1)}, u32[]{:S(2)}, u32[]{:S(2)}) collective-permute-start(bf16[48,2048]{1,0:T(8,128)(2,1)S(1)} %get-tuple-element.45), channel_id=1, source_target_pairs={{0,1},{1,0},{2,3},{3,2},{4,5},{5,4},{6,7},{7,6},{8,9},{9,8},{10,11... | collective-permute-start | bytes 589832 | tf_op jit(solution)/shard_map/ppermute | solution.py:320
  29.2 0.0 copy-done.3
  29.2 1.8 %expert_own.1 = (bf16[2,2,96,768]{3,2,1,0:T(8,128)(2,1)}, bf16[48,128]{1,0:T(8,128)(2,1)S(1)}, bf16[48,128]{1,0:T(8,128)(2,1)S(1)}, bf16[48,128]{1,0:T(8,128)(2,1)S(1)}, bf16[48,128]{1,0:T(8,128)(2,1)S(1)}) custom-call(s32[1]{0:T(128)} %bitcast.me_ref, bf16[48,2176]{1,0:T(8,128)(2,1)S(1)} %collective-permute-done.3.refs_0_, ...), custom_call_target="tpu_custom_call" | custom-call | tf_op jit(solution)/shard_map/expert_own/pallas_call | solution.py:252
  31.0 1.0 %collective-permute-done.info_ref = f32[8,128]{1,0:T(8,128)S(1)} collective-permute-done((f32[8,128]{1,0:T(8,128)S(1)}, f32[8,128]{1,0:T(8,128)S(1)}, u32[]{:S(2)}, u32[]{:S(2)}) %collective-permute-start) | collective-permute-done | bytes 4128 | tf_op jit(solution)/shard_map/ppermute | solution.py:320
  32.0 0.0 collective-permute-done.1.token_ref
  32.0 0.5 pack_far.1
  32.5 0.5 %collective-permute-start.7 = (bf16[48,2176]{1,0:T(8,128)(2,1)S(1)}, bf16[48,2176]{1,0:T(8,128)(2,1)S(1)}, u32[]{:S(2)}, u32[]{:S(2)}) collective-permute-start(bf16[48,2176]{1,0:T(8,128)(2,1)S(1)} %get-tuple-element.38.refs_3_), channel_id=1, source_target_pairs={{0,3},{1,2},{2,1},{3,0},{4,7},{5,6},{6,5},{7,4},{8,11},{9,10},{10,... | collective-permute-start | bytes 626696 | tf_op jit(solution)/shard_map/ppermute | solution.py:320
  33.0 3.1 %collective-permute-start.8 = (bf16[48,2176]{1,0:T(8,128)(2,1)S(1)}, bf16[48,2176]{1,0:T(8,128)(2,1)S(1)}, u32[]{:S(2)}, u32[]{:S(2)}) collective-permute-start(bf16[48,2176]{1,0:T(8,128)(2,1)S(1)} %get-tuple-element.39.refs_2_), channel_id=1, source_target_pairs={{0,2},{1,3},{2,0},{3,1},{4,6},{5,7},{6,4},{7,5},{8,10},{9,11},{10,... | collective-permute-start | bytes 626696 | tf_op jit(solution)/shard_map/ppermute | solution.py:320
  36.1 0.0 collective-permute-done.10.refs_5_
  36.1 0.0 collective-permute-start.9
  36.1 0.0 collective-permute-done.11.refs_6_
  36.1 0.7 %collective-permute-done.12.refs_7_ = bf16[48,2048]{1,0:T(8,128)(2,1)S(1)} collective-permute-done((bf16[48,2048]{1,0:T(8,128)(2,1)S(1)}, bf16[48,2048]{1,0:T(8,128)(2,1)S(1)}, u32[]{:S(2)}, u32[]{:S(2)}) %collective-permute-start.12) | collective-permute-done | bytes 196640 | tf_op jit(solution)/shard_map/ppermute | solution.py:320
  36.8 0.0 copy-start.5
  36.8 0.3 far_grad.1
  37.1 3.7 %collective-permute-start.13 = (bf16[48,128]{1,0:T(8,128)(2,1)S(1)}, bf16[48,128]{1,0:T(8,128)(2,1)S(1)}, u32[]{:S(2)}, u32[]{:S(2)}) collective-permute-start(bf16[48,128]{1,0:T(8,128)(2,1)S(1)} %far_grad.1), channel_id=1, source_target_pairs={{0,6},{1,7},{2,4},{3,5},{4,2},{5,3},{6,0},{7,1},{8,14},{9,15},{10,... | collective-permute-start | bytes 36872 | tf_op jit(solution)/shard_map/ppermute | solution.py:320
  40.8 0.8 %collective-permute-done.7.refs_1_.refs_3_ = bf16[48,2176]{1,0:T(8,128)(2,1)S(1)} collective-permute-done((bf16[48,2176]{1,0:T(8,128)(2,1)S(1)}, bf16[48,2176]{1,0:T(8,128)(2,1)S(1)}, u32[]{:S(2)}, u32[]{:S(2)}) %collective-permute-start.7) | collective-permute-done | bytes 208928 | tf_op jit(solution)/shard_map/ppermute | solution.py:320
  41.6 3.2 %collective-permute-done.8.refs_2_ = bf16[48,2176]{1,0:T(8,128)(2,1)S(1)} collective-permute-done((bf16[48,2176]{1,0:T(8,128)(2,1)S(1)}, bf16[48,2176]{1,0:T(8,128)(2,1)S(1)}, u32[]{:S(2)}, u32[]{:S(2)}) %collective-permute-start.8) | collective-permute-done | bytes 208928 | tf_op jit(solution)/shard_map/ppermute | solution.py:320
  44.8 0.9 %collective-permute-done.9.refs_3_.refs_1_ = bf16[48,2176]{1,0:T(8,128)(2,1)S(1)} collective-permute-done((bf16[48,2176]{1,0:T(8,128)(2,1)S(1)}, bf16[48,2176]{1,0:T(8,128)(2,1)S(1)}, u32[]{:S(2)}, u32[]{:S(2)}) %collective-permute-start.9) | collective-permute-done | bytes 208928 | tf_op jit(solution)/shard_map/ppermute | solution.py:320
  45.8 1.6 %expert_far.1 = bf16[2,2,96,768]{3,2,1,0:T(8,128)(2,1)} custom-call(s32[1]{0:T(128)} %bitcast.me_ref, bf16[48,2176]{1,0:T(8,128)(2,1)S(1)} %get-tuple-element.37.refs_0_, bf16[48,2176]{1,0:T(8,128)(2,1)S(1)} %collective-permute-done.7.refs_1_.refs_3_, bf16[48,2176]{1,0:T(8,128)(2,1)S(1)} %collective-permute-done.8.refs_2_, ...), custom_call_target="tpu_custom_call", output_to_operand_aliasing={{}: (6, {})} | custom-call | tf_op jit(solution)/shard_map/expert_far/pallas_call | solution.py:252
  47.4 0.0 collective-permute-done.13.refs_4_
  47.4 0.0 copy-done.5
  47.4 1.4 %router.1 = bf16[128,2048]{1,0:T(8,128)(2,1)} custom-call(s32[1]{0:T(128)} %bitcast.me_ref, f32[8,128]{1,0:T(8,128)S(1)} %copy-done.6, bf16[48,2176]{1,0:T(8,128)(2,1)S(1)} %get-tuple-element.37.refs_0_, bf16[48,2176]{1,0:T(8,128)(2,1)S(1)} %collective-permute-done.9.refs_3_.refs_1_, bf16[48,2176]{1,0:T(8,128)(2,1)S(1)} %collective-permute-done.8.refs_2_, ...), custom_call_target="tpu_custom_call" | custom-call | tf_op jit(solution)/shard_map/router/pallas_call | solution.py:304
Async XLA Ops:
  0.6 31.4 %collective-permute-start.1 = (bf16[128,2048]{1,0:T(8,128)(2,1)}, bf16[128,2048]{1,0:T(8,128)(2,1)S(1)}, u32[]{:S(2)}, u32[]{:S(2)}) collective-permute-start(bf16[128,2048]{1,0:T(8,128)(2,1)} %bitcast.17), channel_id=1, source_target_pairs={{0,30},{1,31},{2,28},{3,29},{4,26},{5,27},{6,24},{7,25},{8,6},{9,7... | collective-permute-start | bytes 1572872 | tf_op jit(solution)/shard_map/ppermute | solution.py:320
  7.4 15.2 %copy-start.6 = (f32[8,128]{1,0:T(8,128)S(1)}, f32[8,128]{1,0:T(8,128)}, u32[]{:S(2)}) copy-start(f32[8,128]{1,0:T(8,128)} %info.1.info_ref) | copy-start | bytes 12292
  7.4 3.3 %collective-permute-start.2 = (f32[8,128]{1,0:T(8,128)}, f32[8,128]{1,0:T(8,128)S(1)}, u32[]{:S(2)}, u32[]{:S(2)}) collective-permute-start(f32[8,128]{1,0:T(8,128)} %info.1.info_ref), channel_id=1, source_target_pairs={{0,8},{1,9},{2,10},{3,11},{4,12},{5,13},{6,14},{7,15},{8,16},{9,17... | collective-permute-start | bytes 12296 | tf_op jit(solution)/shard_map/ppermute | solution.py:320
  10.7 1.0 %copy-start.4 = (bf16[1,128,2048]{2,1,0:T(8,128)(2,1)S(1)}, bf16[1,128,2048]{2,1,0:T(8,128)(2,1)}, u32[]{:S(2)}) copy-start(bf16[1,128,2048]{2,1,0:T(8,128)(2,1)} %param.6) | copy-start | bytes 1572868
  12.3 10.4 %collective-permute-start.3 = (bf16[48,2176]{1,0:T(8,128)(2,1)S(1)}, bf16[48,2176]{1,0:T(8,128)(2,1)S(1)}, u32[]{:S(2)}, u32[]{:S(2)}) collective-permute-start(bf16[48,2176]{1,0:T(8,128)(2,1)S(1)} %get-tuple-element.28.after_ref), channel_id=1, source_target_pairs={{0,24},{1,25},{2,26},{3,27},{4,28},{5,29},{6,30},{7,31},{8,0},{9,1... | collective-permute-start | bytes 626696 | tf_op jit(solution)/shard_map/ppermute | solution.py:320
  12.3 10.3 %collective-permute-start.4 = (bf16[48,2176]{1,0:T(8,128)(2,1)S(1)}, bf16[48,2176]{1,0:T(8,128)(2,1)S(1)}, u32[]{:S(2)}, u32[]{:S(2)}) collective-permute-start(bf16[48,2176]{1,0:T(8,128)(2,1)S(1)} %get-tuple-element.29), channel_id=1, source_target_pairs={{0,25},{1,24},{2,27},{3,26},{4,29},{5,28},{6,31},{7,30},{8,1},{9,0... | collective-permute-start | bytes 626696 | tf_op jit(solution)/shard_map/ppermute | solution.py:320
  13.9 10.4 %collective-permute-start.5 = (bf16[48,2176]{1,0:T(8,128)(2,1)S(1)}, bf16[48,2176]{1,0:T(8,128)(2,1)S(1)}, u32[]{:S(2)}, u32[]{:S(2)}) collective-permute-start(bf16[48,2176]{1,0:T(8,128)(2,1)S(1)} %get-tuple-element.30), channel_id=1, source_target_pairs={{0,26},{1,27},{2,24},{3,25},{4,30},{5,31},{6,28},{7,29},{8,2},{9,3... | collective-permute-start | bytes 626696 | tf_op jit(solution)/shard_map/ppermute | solution.py:320
  13.9 14.5 %collective-permute-start.6 = (bf16[48,2176]{1,0:T(8,128)(2,1)S(1)}, bf16[48,2176]{1,0:T(8,128)(2,1)S(1)}, u32[]{:S(2)}, u32[]{:S(2)}) collective-permute-start(bf16[48,2176]{1,0:T(8,128)(2,1)S(1)} %get-tuple-element.31), channel_id=1, source_target_pairs={{0,27},{1,26},{2,25},{3,24},{4,31},{5,30},{6,29},{7,28},{8,3},{9,2... | collective-permute-start | bytes 626696 | tf_op jit(solution)/shard_map/ppermute | solution.py:320
  16.5 1.9 %copy-start = (bf16[1,768,2048]{2,1,0:T(8,128)(2,1)S(1)}, bf16[1,768,2048]{2,1,0:T(8,128)(2,1)}, u32[]{:S(2)}) copy-start(bf16[1,768,2048]{2,1,0:T(8,128)(2,1)} %param.10) | copy-start | bytes 9437188
  18.4 1.1 %copy-start.2 = (bf16[1,384,768]{2,1,0:T(8,128)(2,1)S(1)}, bf16[1,384,768]{2,1,0:T(8,128)(2,1)}, u32[]{:S(2)}) copy-start(bf16[1,384,768]{2,1,0:T(8,128)(2,1)} %param.9) | copy-start | bytes 1769476
  19.5 3.9 %copy-start.1 = (bf16[1,768,2048]{2,1,0:T(8,128)(2,1)S(1)}, bf16[1,768,2048]{2,1,0:T(8,128)(2,1)}, u32[]{:S(2)}) copy-start(bf16[1,768,2048]{2,1,0:T(8,128)(2,1)} %param.10) | copy-start | bytes 9437188
  22.6 6.6 %copy-start.3 = (bf16[1,384,768]{2,1,0:T(8,128)(2,1)S(1)}, bf16[1,384,768]{2,1,0:T(8,128)(2,1)}, u32[]{:S(2)}) copy-start(bf16[1,384,768]{2,1,0:T(8,128)(2,1)} %param.9) | copy-start | bytes 1769476
  22.6 13.5 %collective-permute-start.10 = (bf16[48,2048]{1,0:T(8,128)(2,1)S(1)}, bf16[48,2048]{1,0:T(8,128)(2,1)S(1)}, u32[]{:S(2)}, u32[]{:S(2)}) collective-permute-start(bf16[48,2048]{1,0:T(8,128)(2,1)S(1)} %get-tuple-element.43), channel_id=1, source_target_pairs={{0,3},{1,2},{2,1},{3,0},{4,7},{5,6},{6,5},{7,4},{8,11},{9,10},{10,... | collective-permute-start | bytes 589832 | tf_op jit(solution)/shard_map/ppermute | solution.py:320
  22.6 9.3 %collective-permute-start = (f32[8,128]{1,0:T(8,128)S(1)}, f32[8,128]{1,0:T(8,128)S(1)}, u32[]{:S(2)}, u32[]{:S(2)}) collective-permute-start(f32[8,128]{1,0:T(8,128)S(1)} %copy-done.6), channel_id=1, source_target_pairs={{0,6},{1,7},{2,4},{3,5},{4,2},{5,3},{6,0},{7,1},{8,14},{9,15},{10,... | collective-permute-start | bytes 12296 | tf_op jit(solution)/shard_map/ppermute | solution.py:320
  24.3 11.8 %collective-permute-start.11 = (bf16[48,2048]{1,0:T(8,128)(2,1)S(1)}, bf16[48,2048]{1,0:T(8,128)(2,1)S(1)}, u32[]{:S(2)}, u32[]{:S(2)}) collective-permute-start(bf16[48,2048]{1,0:T(8,128)(2,1)S(1)} %get-tuple-element.44), channel_id=1, source_target_pairs={{0,2},{1,3},{2,0},{3,1},{4,6},{5,7},{6,4},{7,5},{8,10},{9,11},{10,... | collective-permute-start | bytes 589832 | tf_op jit(solution)/shard_map/ppermute | solution.py:320
  28.3 8.5 %collective-permute-start.12 = (bf16[48,2048]{1,0:T(8,128)(2,1)S(1)}, bf16[48,2048]{1,0:T(8,128)(2,1)S(1)}, u32[]{:S(2)}, u32[]{:S(2)}) collective-permute-start(bf16[48,2048]{1,0:T(8,128)(2,1)S(1)} %get-tuple-element.45), channel_id=1, source_target_pairs={{0,1},{1,0},{2,3},{3,2},{4,5},{5,4},{6,7},{7,6},{8,9},{9,8},{10,11... | collective-permute-start | bytes 589832 | tf_op jit(solution)/shard_map/ppermute | solution.py:320
  32.5 9.1 %collective-permute-start.7 = (bf16[48,2176]{1,0:T(8,128)(2,1)S(1)}, bf16[48,2176]{1,0:T(8,128)(2,1)S(1)}, u32[]{:S(2)}, u32[]{:S(2)}) collective-permute-start(bf16[48,2176]{1,0:T(8,128)(2,1)S(1)} %get-tuple-element.38.refs_3_), channel_id=1, source_target_pairs={{0,3},{1,2},{2,1},{3,0},{4,7},{5,6},{6,5},{7,4},{8,11},{9,10},{10,... | collective-permute-start | bytes 626696 | tf_op jit(solution)/shard_map/ppermute | solution.py:320
  33.0 11.8 %collective-permute-start.8 = (bf16[48,2176]{1,0:T(8,128)(2,1)S(1)}, bf16[48,2176]{1,0:T(8,128)(2,1)S(1)}, u32[]{:S(2)}, u32[]{:S(2)}) collective-permute-start(bf16[48,2176]{1,0:T(8,128)(2,1)S(1)} %get-tuple-element.39.refs_2_), channel_id=1, source_target_pairs={{0,2},{1,3},{2,0},{3,1},{4,6},{5,7},{6,4},{7,5},{8,10},{9,11},{10,... | collective-permute-start | bytes 626696 | tf_op jit(solution)/shard_map/ppermute | solution.py:320
  36.1 9.6 %collective-permute-start.9 = (bf16[48,2176]{1,0:T(8,128)(2,1)S(1)}, bf16[48,2176]{1,0:T(8,128)(2,1)S(1)}, u32[]{:S(2)}, u32[]{:S(2)}) collective-permute-start(bf16[48,2176]{1,0:T(8,128)(2,1)S(1)} %get-tuple-element.40.refs_1_), channel_id=1, source_target_pairs={{0,1},{1,0},{2,3},{3,2},{4,5},{5,4},{6,7},{7,6},{8,9},{9,8},{10,11... | collective-permute-start | bytes 626696 | tf_op jit(solution)/shard_map/ppermute | solution.py:320
  36.8 10.5 %copy-start.5 = (bf16[2048,8]{0,1:T(8,128)(2,1)S(1)}, bf16[2048,8]{0,1:T(8,128)(2,1)}, u32[]{:S(2)}) copy-start(bf16[2048,8]{0,1:T(8,128)(2,1)} %param.11) | copy-start | bytes 98308
  37.1 10.2 %collective-permute-start.13 = (bf16[48,128]{1,0:T(8,128)(2,1)S(1)}, bf16[48,128]{1,0:T(8,128)(2,1)S(1)}, u32[]{:S(2)}, u32[]{:S(2)}) collective-permute-start(bf16[48,128]{1,0:T(8,128)(2,1)S(1)} %far_grad.1), channel_id=1, source_target_pairs={{0,6},{1,7},{2,4},{3,5},{4,2},{5,3},{6,0},{7,1},{8,14},{9,15},{10,... | collective-permute-start | bytes 36872 | tf_op jit(solution)/shard_map/ppermute | solution.py:320

commit v5 on v4

--- a/solution.py
+++ b/solution.py
@@ -265,10 +265,9 @@
     )(me, *[blocks[j] for j in (OWN_ORDER if graded else FAR_ORDER)], weight, *operands)
 
 
-def router_kernel(half, capacity, turn, me_ref, info_ref, *refs):
-    own, (far_ref, router_ref, out_ref) = refs[:half], refs[half:]
+def router_rows(half, capacity, turn, me, info_ref, own, far_ref, router_ref):
     info = info_ref[...]
-    relative = jnp.bitwise_xor(me_ref[0], iota((8, LANES), 0))
+    relative = jnp.bitwise_xor(me, iota((8, LANES), 0))
     rank, _ = ranks(info, relative)
     slot = iota((capacity, LANES), 0)
     token = iota((capacity, LANES), 1)
@@ -276,7 +275,7 @@
     rows = []
     for j in range(2 * half):
         if j < half:
-            table, lane = own[j][...].astype(F32), 0
+            table, lane = own[j].astype(F32), 0
         else:
             table, lane = far, 3 * ((j - half) ^ turn)
         column = table[:, lane : lane + 1] + table[:, lane + 1 : lane + 2] + table[:, lane + 2 : lane + 3]
@@ -294,22 +293,69 @@
     parts = jnp.concatenate([*split(logit), jnp.zeros((LANES - 24, LANES), F32)], axis=0).T
     router = router_ref[...].astype(F32)
     router = jnp.concatenate([router, router, router, jnp.zeros((LANES - 24, router.shape[1]), F32)], axis=0)
-    out_ref[...] = jnp.dot(parts.astype(BF16), router.astype(BF16), preferred_element_type=F32).astype(BF16)
-
-
-def router(me, info, own, far, table, tokens, half, capacity, turn):
-    width = tokens.shape[1]
-    vmem = pl.BlockSpec(memory_space=pltpu.VMEM)
-    tail = pl.BlockSpec((MICRO * capacity, LANES), lambda i: (0, width // LANES))
-    return pl.pallas_call(
-        functools.partial(router_kernel, half, capacity, turn),
-        grid=(1,),
-        out_shape=jax.ShapeDtypeStruct(tokens.shape, BF16),
-        in_specs=[pl.BlockSpec(memory_space=pltpu.SMEM), vmem] + [tail] * half + [vmem] * 2,
-        out_specs=vmem,
-        compiler_params=pltpu.CompilerParams(vmem_limit_bytes=VMEM_LIMIT),
-        name="router",
-    )(me, info, *own, far, table)
+    return jnp.dot(parts.astype(BF16), router.astype(BF16), preferred_element_type=F32).astype(BF16)
+
+
+def last_kernel(half, capacity, turn, me_ref, *refs):
+    blocks, refs = [refs[FAR_ORDER.index(j)] for j in range(half)], refs[half:]
+    w_ref, info_ref, far_ref, router_ref, _, d_ref, out_ref = refs[:7]
+    lhs, product, scale, rows, hidden, row_sem, hidden_sem = refs[7:]
+    width, hidden_width = w_ref.shape
+    run, size = half * capacity, MICRO * capacity
+    me = me_ref[0]
+    here = jnp.bitwise_xor(lax.rem(me, half), turn)
+    side = 1 - me // half
+    own = [block[:, width:] for block in blocks]
+    rows[...] = router_rows(half, capacity, turn, me, info_ref, own, far_ref, router_ref)
+    row_copy = pltpu.make_async_copy(rows, out_ref, row_sem)
+    row_copy.start()
+    places = []
+    for j in range(half):
+        lhs[j * size : (j + 1) * size, :] = blocks[j][:, 0:width]
+        for m in range(MICRO):
+            slot = pl.multiple_of(m * run + jnp.bitwise_xor(here, j) * capacity, 8)
+            places.append((j * size + m * capacity, slot))
+            tail = own[j][m * capacity : (m + 1) * capacity].astype(F32)
+            scale[pl.ds(slot, capacity), :] = jnp.broadcast_to(tail[:, SCALE : SCALE + 1], tail.shape)
+    for columns in chunks(hidden_width):
+        got = jnp.dot(lhs[...], w_ref[:, columns], preferred_element_type=F32)
+        for begin, slot in places:
+            product[pl.ds(slot, capacity), columns] = got[begin : begin + capacity, :]
+    copies = []
+    for m in range(MICRO):
+        at = slice(m * run, (m + 1) * run)
+        for lane in range(0, hidden_width, LANES):
+            lanes = slice(lane, lane + LANES)
+            hidden[m, :, lanes] = (scale[at, :] * product[at, lanes]).astype(BF16)
+        copies.append(pltpu.make_async_copy(hidden.at[m], d_ref.at[m, side], hidden_sem.at[m]))
+        copies[m].start()
+    for copy in copies:
+        copy.wait()
+    row_copy.wait()
+
+
+def last(me, blocks, weight, info, far, table, held, tokens, half, capacity, turn):
+    width, hidden_width = weight.shape
+    run = half * capacity
+    vmem, anywhere = pl.BlockSpec(memory_space=pltpu.VMEM), pl.BlockSpec(memory_space=pl.ANY)
+    return pl.pallas_call(
+        functools.partial(last_kernel, half, capacity, turn),
+        out_shape=[jax.ShapeDtypeStruct(held.shape, BF16), jax.ShapeDtypeStruct(tokens.shape, BF16)],
+        in_specs=[pl.BlockSpec(memory_space=pltpu.SMEM)] + [vmem] * (half + 4) + [anywhere],
+        out_specs=[anywhere, anywhere],
+        scratch_shapes=[
+            pltpu.VMEM((MICRO * run, width), BF16),
+            pltpu.VMEM((MICRO * run, hidden_width), F32),
+            pltpu.VMEM((MICRO * run, LANES), F32),
+            pltpu.VMEM(tokens.shape, BF16),
+            pltpu.VMEM((MICRO, run, hidden_width), BF16),
+            pltpu.SemaphoreType.DMA,
+            pltpu.SemaphoreType.DMA((MICRO,)),
+        ],
+        input_output_aliases={half + 5: 0},
+        compiler_params=pltpu.CompilerParams(vmem_limit_bytes=VMEM_LIMIT),
+        name="last",
+    )(me, *[blocks[j] for j in FAR_ORDER], weight, info, far, table, held)
 
 
 def route(block, flip, back):
@@ -353,8 +399,7 @@
     far = pack(me, far_info, far_tokens, half, capacity, "pack_far", own_grads)
     far_grads = route(far_grad(far, backs, half, capacity), half + turn, 0)
     far = spread(far)
-    (d_hidden,) = expert(me, far, weight_t, half, capacity, turn, held=held)
-    grad_in = router(me, info, far, far_grads, w_router.T, tokens, half, capacity, turn)
+    d_hidden, grad_in = last(me, far, weight_t, info, far_grads, w_router.T, held, tokens, half, capacity, turn)
     return d_hidden.reshape(saved_hidden.shape), grad_in[None]
 
 

time: 49.1 us -> 48.1 us (0.980)
  Pallas kernels: 9.1 us -> 8.2 us
    pallas_call x2 -> x1, Pallas kernels: 3.37 us -> 1.79 us  [expert(): pl.pallas_call(functools.partial(expert_kernel, half, capacity, turn, gra...]
    pallas_call x1, Pallas kernels: 1.41 us -> 2.08 us  [last(): pl.pallas_call(functools.partial(last_kernel, half, capacity, turn), out_...]
  transfers between devices with their start and end apart: 14 -> 14, of which waited for: 8 -> 7; matrix products, arithmetic and copies ran while one was open for 0% -> 0% of each run, Pallas kernels for 16% -> 13%
where the time goes in v5:
time: 48.1 us; the launch traced here: 47.9 us
  starting transfers between devices  21.7 us (45%)
  waiting for transfers between devices  13.2 us (27%)
  Pallas kernels  8.2 us (17%)
  local copies, waits for them, and re-layouts  4.01 us (8%)
  between operations  0.7 us (1%)
    ppermute x14, starting transfers between devices, route(): return lax.ppermute(block, ('pipe', 'expert'), pairs)  21.7 us
    ppermute x14, waiting for transfers between devices, route(): return lax.ppermute(block, ('pipe', 'expert'), pairs)  13.2 us
    unnamed x14, local copies, waits for them, and re-layouts  4.01 us
    pallas_call x1, Pallas kernels, last(): pl.pallas_call(functools.partial(last_kernel, half, capacity, turn), out_...  2.08 us
    pallas_call x1, Pallas kernels, expert(): pl.pallas_call(functools.partial(expert_kernel, half, capacity, turn, gra...  1.79 us
    pallas_call x1, Pallas kernels, by_halves(): pl.pallas_call(info_kernel, out_shape=jax.ShapeDtypeStruct((8, LANES), F3...  1.31 us
  transfers between devices with their start and end apart: 14, of which 7 were waited for; matrix products, arithmetic and copies ran while one was open for 0% of the time, Pallas kernels for 13%

profile of v5, /device:TPU:0, one launch (start us, length us, event | category | flops | bytes accessed | tf_op | source)
XLA Modules:
  0.0 47.9 jit_solution(2738490861546029029)
XLA Ops:
  0.6 5.5 %collective-permute-start.1 = (bf16[128,2048]{1,0:T(8,128)(2,1)}, bf16[128,2048]{1,0:T(8,128)(2,1)S(1)}, u32[]{:S(2)}, u32[]{:S(2)}) collective-permute-start(bf16[128,2048]{1,0:T(8,128)(2,1)} %bitcast.17), channel_id=1, source_target_pairs={{0,30},{1,31},{2,28},{3,29},{4,26},{5,27},{6,24},{7,25},{8,6},{9,7... | collective-permute-start | bytes 1572872 | tf_op jit(solution)/shard_map/ppermute | solution.py:366
  6.1 1.3 %info.1.refs_5_ = f32[8,128]{1,0:T(8,128)} custom-call(s32[2,128]{1,0:T(2,128)} %bitcast.22, f32[8,128]{1,0:T(8,128)} %bitcast.21), custom_call_target="tpu_custom_call" | custom-call | tf_op jit(solution)/shard_map/info/pallas_call | solution.py:382
  7.4 0.0 copy-start.6
  7.4 0.0 collective-permute-start.2
  7.4 3.3 %collective-permute-done.2.info_ref = f32[8,128]{1,0:T(8,128)S(1)} collective-permute-done((f32[8,128]{1,0:T(8,128)}, f32[8,128]{1,0:T(8,128)S(1)}, u32[]{:S(2)}, u32[]{:S(2)}) %collective-permute-start.2) | collective-permute-done | bytes 4128 | tf_op jit(solution)/shard_map/ppermute | solution.py:366
  10.7 0.0 copy-start.4
  10.7 1.0 %copy-done.4 = bf16[1,128,2048]{2,1,0:T(8,128)(2,1)S(1)} copy-done((bf16[1,128,2048]{2,1,0:T(8,128)(2,1)S(1)}, bf16[1,128,2048]{2,1,0:T(8,128)(2,1)}, u32[]{:S(2)}) %copy-start.4) | copy-done | bytes 524312
  11.8 0.5 pack_own.1
  12.3 0.1 collective-permute-start.3
  12.3 1.5 %collective-permute-start.4 = (bf16[48,2176]{1,0:T(8,128)(2,1)S(1)}, bf16[48,2176]{1,0:T(8,128)(2,1)S(1)}, u32[]{:S(2)}, u32[]{:S(2)}) collective-permute-start(bf16[48,2176]{1,0:T(8,128)(2,1)S(1)} %get-tuple-element.31), channel_id=1, source_target_pairs={{0,25},{1,24},{2,27},{3,26},{4,29},{5,28},{6,31},{7,30},{8,1},{9,0... | collective-permute-start | bytes 626696 | tf_op jit(solution)/shard_map/ppermute | solution.py:366
  13.9 0.0 collective-permute-start.5
  13.9 2.7 %collective-permute-start.6 = (bf16[48,2176]{1,0:T(8,128)(2,1)S(1)}, bf16[48,2176]{1,0:T(8,128)(2,1)S(1)}, u32[]{:S(2)}, u32[]{:S(2)}) collective-permute-start(bf16[48,2176]{1,0:T(8,128)(2,1)S(1)} %get-tuple-element.33), channel_id=1, source_target_pairs={{0,27},{1,26},{2,25},{3,24},{4,31},{5,30},{6,29},{7,28},{8,3},{9,2... | collective-permute-start | bytes 626696 | tf_op jit(solution)/shard_map/ppermute | solution.py:366
  16.5 0.0 copy-start
  16.5 1.9 %copy-done = bf16[1,768,2048]{2,1,0:T(8,128)(2,1)S(1)} copy-done((bf16[1,768,2048]{2,1,0:T(8,128)(2,1)S(1)}, bf16[1,768,2048]{2,1,0:T(8,128)(2,1)}, u32[]{:S(2)}) %copy-start) | copy-done | bytes 3145752
  18.4 0.0 copy-start.2
  18.4 1.1 %copy-done.2 = bf16[1,384,768]{2,1,0:T(8,128)(2,1)S(1)} copy-done((bf16[1,384,768]{2,1,0:T(8,128)(2,1)S(1)}, bf16[1,384,768]{2,1,0:T(8,128)(2,1)}, u32[]{:S(2)}) %copy-start.2) | copy-done | bytes 589848
  19.5 0.0 copy-start.1
  19.5 0.9 %back.1 = (bf16[48,2048]{1,0:T(8,128)(2,1)S(1)}, bf16[48,2048]{1,0:T(8,128)(2,1)S(1)}, bf16[48,2048]{1,0:T(8,128)(2,1)S(1)}, bf16[48,2048]{1,0:T(8,128)(2,1)S(1)}) custom-call(s32[1]{0:T(128)} %bitcast.me_ref, bf16[2,2,96,768]{3,2,1,0:T(8,128)(2,1)S(1)} %bitcast.15, bf16[768,2048]{1,0:T(8,128)(2,1)S(1)} %bitcast.13), custom_call_target="tpu_custom_call" | custom-call | tf_op jit(solution)/shard_map/back/pallas_call | solution.py:124
  20.4 2.2 %collective-permute-done.3.refs_0_ = bf16[48,2176]{1,0:T(8,128)(2,1)S(1)} collective-permute-done((bf16[48,2176]{1,0:T(8,128)(2,1)S(1)}, bf16[48,2176]{1,0:T(8,128)(2,1)S(1)}, u32[]{:S(2)}, u32[]{:S(2)}) %collective-permute-start.3) | collective-permute-done | bytes 208928 | tf_op jit(solution)/shard_map/ppermute | solution.py:366
  22.6 0.0 copy-start.3
  22.6 0.0 collective-permute-start.10
  22.6 0.0 collective-permute-done.4.refs_1_
  22.6 0.0 copy-done.6
  22.6 0.8 %collective-permute-start = (f32[8,128]{1,0:T(8,128)S(1)}, f32[8,128]{1,0:T(8,128)S(1)}, u32[]{:S(2)}, u32[]{:S(2)}) collective-permute-start(f32[8,128]{1,0:T(8,128)S(1)} %copy-done.6), channel_id=1, source_target_pairs={{0,6},{1,7},{2,4},{3,5},{4,2},{5,3},{6,0},{7,1},{8,14},{9,15},{10,... | collective-permute-start | bytes 12296 | tf_op jit(solution)/shard_map/ppermute | solution.py:366
  23.4 0.0 copy-done.1
  23.4 0.9 %turned.1.refs_4_ = bf16[2048,768]{1,0:T(8,128)(2,1)S(1)} custom-call(bf16[768,2048]{1,0:T(8,128)(2,1)S(1)} %bitcast.14, bf16[48,2176]{1,0:T(8,128)(2,1)S(1)} %get-tuple-element.30.after_ref), custom_call_target="tpu_custom_call" | custom-call | tf_op jit(solution)/shard_map/turned/pallas_call | solution.py:150
  24.3 0.0 collective-permute-done.5.refs_2_
  24.3 3.0 %collective-permute-start.11 = (bf16[48,2048]{1,0:T(8,128)(2,1)S(1)}, bf16[48,2048]{1,0:T(8,128)(2,1)S(1)}, u32[]{:S(2)}, u32[]{:S(2)}) collective-permute-start(bf16[48,2048]{1,0:T(8,128)(2,1)S(1)} %get-tuple-element.45), channel_id=1, source_target_pairs={{0,2},{1,3},{2,0},{3,1},{4,6},{5,7},{6,4},{7,5},{8,10},{9,11},{10,... | collective-permute-start | bytes 589832 | tf_op jit(solution)/shard_map/ppermute | solution.py:366
  27.3 1.0 %collective-permute-done.6.refs_3_ = bf16[48,2176]{1,0:T(8,128)(2,1)S(1)} collective-permute-done((bf16[48,2176]{1,0:T(8,128)(2,1)S(1)}, bf16[48,2176]{1,0:T(8,128)(2,1)S(1)}, u32[]{:S(2)}, u32[]{:S(2)}) %collective-permute-start.6) | collective-permute-done | bytes 208928 | tf_op jit(solution)/shard_map/ppermute | solution.py:366
  28.3 0.0 copy-start.5
  28.3 0.8 %collective-permute-start.12 = (bf16[48,2048]{1,0:T(8,128)(2,1)S(1)}, bf16[48,2048]{1,0:T(8,128)(2,1)S(1)}, u32[]{:S(2)}, u32[]{:S(2)}) collective-permute-start(bf16[48,2048]{1,0:T(8,128)(2,1)S(1)} %get-tuple-element.46), channel_id=1, source_target_pairs={{0,1},{1,0},{2,3},{3,2},{4,5},{5,4},{6,7},{7,6},{8,9},{9,8},{10,11... | collective-permute-start | bytes 589832 | tf_op jit(solution)/shard_map/ppermute | solution.py:366
  29.2 0.0 copy-done.3
  29.2 1.8 %expert_own.1 = (bf16[2,2,96,768]{3,2,1,0:T(8,128)(2,1)}, bf16[48,128]{1,0:T(8,128)(2,1)S(1)}, bf16[48,128]{1,0:T(8,128)(2,1)S(1)}, bf16[48,128]{1,0:T(8,128)(2,1)S(1)}, bf16[48,128]{1,0:T(8,128)(2,1)S(1)}) custom-call(s32[1]{0:T(128)} %bitcast.me_ref, bf16[48,2176]{1,0:T(8,128)(2,1)S(1)} %collective-permute-done.3.refs_0_, ...), custom_call_target="tpu_custom_call" | custom-call | tf_op jit(solution)/shard_map/expert_own/pallas_call | solution.py:252
  31.0 1.0 %collective-permute-done.info_ref = f32[8,128]{1,0:T(8,128)S(1)} collective-permute-done((f32[8,128]{1,0:T(8,128)S(1)}, f32[8,128]{1,0:T(8,128)S(1)}, u32[]{:S(2)}, u32[]{:S(2)}) %collective-permute-start) | collective-permute-done | bytes 4128 | tf_op jit(solution)/shard_map/ppermute | solution.py:366
  32.0 0.0 collective-permute-done.1.token_ref
  32.0 0.5 pack_far.1
  32.5 0.5 %collective-permute-start.7 = (bf16[48,2176]{1,0:T(8,128)(2,1)S(1)}, bf16[48,2176]{1,0:T(8,128)(2,1)S(1)}, u32[]{:S(2)}, u32[]{:S(2)}) collective-permute-start(bf16[48,2176]{1,0:T(8,128)(2,1)S(1)} %get-tuple-element.40.refs_3_), channel_id=1, source_target_pairs={{0,3},{1,2},{2,1},{3,0},{4,7},{5,6},{6,5},{7,4},{8,11},{9,10},{10,... | collective-permute-start | bytes 626696 | tf_op jit(solution)/shard_map/ppermute | solution.py:366
  33.0 3.1 %collective-permute-start.8 = (bf16[48,2176]{1,0:T(8,128)(2,1)S(1)}, bf16[48,2176]{1,0:T(8,128)(2,1)S(1)}, u32[]{:S(2)}, u32[]{:S(2)}) collective-permute-start(bf16[48,2176]{1,0:T(8,128)(2,1)S(1)} %get-tuple-element.41.refs_2_), channel_id=1, source_target_pairs={{0,2},{1,3},{2,0},{3,1},{4,6},{5,7},{6,4},{7,5},{8,10},{9,11},{10,... | collective-permute-start | bytes 626696 | tf_op jit(solution)/shard_map/ppermute | solution.py:366
  36.1 0.0 collective-permute-done.10.refs_5_
  36.1 0.0 collective-permute-start.9
  36.1 0.0 collective-permute-done.11.refs_6_
  36.1 0.7 %collective-permute-done.12.refs_7_ = bf16[48,2048]{1,0:T(8,128)(2,1)S(1)} collective-permute-done((bf16[48,2048]{1,0:T(8,128)(2,1)S(1)}, bf16[48,2048]{1,0:T(8,128)(2,1)S(1)}, u32[]{:S(2)}, u32[]{:S(2)}) %collective-permute-start.12) | collective-permute-done | bytes 196640 | tf_op jit(solution)/shard_map/ppermute | solution.py:366
  36.8 0.3 far_grad.1
  37.1 3.7 %collective-permute-start.13 = (bf16[48,128]{1,0:T(8,128)(2,1)S(1)}, bf16[48,128]{1,0:T(8,128)(2,1)S(1)}, u32[]{:S(2)}, u32[]{:S(2)}) collective-permute-start(bf16[48,128]{1,0:T(8,128)(2,1)S(1)} %far_grad.1), channel_id=1, source_target_pairs={{0,6},{1,7},{2,4},{3,5},{4,2},{5,3},{6,0},{7,1},{8,14},{9,15},{10,... | collective-permute-start | bytes 36872 | tf_op jit(solution)/shard_map/ppermute | solution.py:366
  40.8 4.6 %collective-permute-done.13.refs_6_ = bf16[48,128]{1,0:T(8,128)(2,1)S(1)} collective-permute-done((bf16[48,128]{1,0:T(8,128)(2,1)S(1)}, bf16[48,128]{1,0:T(8,128)(2,1)S(1)}, u32[]{:S(2)}, u32[]{:S(2)}) %collective-permute-start.13) | collective-permute-done | bytes 12320 | tf_op jit(solution)/shard_map/ppermute | solution.py:366
  45.4 0.0 collective-permute-done.7.refs_1_
  45.4 0.0 collective-permute-done.8.refs_2_
  45.4 0.4 collective-permute-done.9.refs_3_
  45.8 0.0 copy-done.5
  45.8 2.1 %last.1 = (bf16[2,2,96,768]{3,2,1,0:T(8,128)(2,1)}, bf16[128,2048]{1,0:T(8,128)(2,1)}) custom-call(s32[1]{0:T(128)} %bitcast.me_ref, bf16[48,2176]{1,0:T(8,128)(2,1)S(1)} %get-tuple-element.39.refs_0_, bf16[48,2176]{1,0:T(8,128)(2,1)S(1)} %collective-permute-done.7.refs_1_, ...), custom_call_target="tpu_custom_call", output_to_operand_aliasing={{0}: (9, {})} | custom-call | tf_op jit(solution)/shard_map/last/pallas_call | solution.py:341
Async XLA Ops:
  0.6 31.4 %collective-permute-start.1 = (bf16[128,2048]{1,0:T(8,128)(2,1)}, bf16[128,2048]{1,0:T(8,128)(2,1)S(1)}, u32[]{:S(2)}, u32[]{:S(2)}) collective-permute-start(bf16[128,2048]{1,0:T(8,128)(2,1)} %bitcast.17), channel_id=1, source_target_pairs={{0,30},{1,31},{2,28},{3,29},{4,26},{5,27},{6,24},{7,25},{8,6},{9,7... | collective-permute-start | bytes 1572872 | tf_op jit(solution)/shard_map/ppermute | solution.py:366
  7.4 15.2 %copy-start.6 = (f32[8,128]{1,0:T(8,128)S(1)}, f32[8,128]{1,0:T(8,128)}, u32[]{:S(2)}) copy-start(f32[8,128]{1,0:T(8,128)} %info.1.refs_5_) | copy-start | bytes 12292
  7.4 3.3 %collective-permute-start.2 = (f32[8,128]{1,0:T(8,128)}, f32[8,128]{1,0:T(8,128)S(1)}, u32[]{:S(2)}, u32[]{:S(2)}) collective-permute-start(f32[8,128]{1,0:T(8,128)} %info.1.refs_5_), channel_id=1, source_target_pairs={{0,8},{1,9},{2,10},{3,11},{4,12},{5,13},{6,14},{7,15},{8,16},{9,17... | collective-permute-start | bytes 12296 | tf_op jit(solution)/shard_map/ppermute | solution.py:366
  10.7 1.0 %copy-start.4 = (bf16[1,128,2048]{2,1,0:T(8,128)(2,1)S(1)}, bf16[1,128,2048]{2,1,0:T(8,128)(2,1)}, u32[]{:S(2)}) copy-start(bf16[1,128,2048]{2,1,0:T(8,128)(2,1)} %param.6) | copy-start | bytes 1572868
  12.3 10.4 %collective-permute-start.3 = (bf16[48,2176]{1,0:T(8,128)(2,1)S(1)}, bf16[48,2176]{1,0:T(8,128)(2,1)S(1)}, u32[]{:S(2)}, u32[]{:S(2)}) collective-permute-start(bf16[48,2176]{1,0:T(8,128)(2,1)S(1)} %get-tuple-element.30.after_ref), channel_id=1, source_target_pairs={{0,24},{1,25},{2,26},{3,27},{4,28},{5,29},{6,30},{7,31},{8,0},{9,1... | collective-permute-start | bytes 626696 | tf_op jit(solution)/shard_map/ppermute | solution.py:366
  12.3 10.3 %collective-permute-start.4 = (bf16[48,2176]{1,0:T(8,128)(2,1)S(1)}, bf16[48,2176]{1,0:T(8,128)(2,1)S(1)}, u32[]{:S(2)}, u32[]{:S(2)}) collective-permute-start(bf16[48,2176]{1,0:T(8,128)(2,1)S(1)} %get-tuple-element.31), channel_id=1, source_target_pairs={{0,25},{1,24},{2,27},{3,26},{4,29},{5,28},{6,31},{7,30},{8,1},{9,0... | collective-permute-start | bytes 626696 | tf_op jit(solution)/shard_map/ppermute | solution.py:366
  13.9 10.4 %collective-permute-start.5 = (bf16[48,2176]{1,0:T(8,128)(2,1)S(1)}, bf16[48,2176]{1,0:T(8,128)(2,1)S(1)}, u32[]{:S(2)}, u32[]{:S(2)}) collective-permute-start(bf16[48,2176]{1,0:T(8,128)(2,1)S(1)} %get-tuple-element.32), channel_id=1, source_target_pairs={{0,26},{1,27},{2,24},{3,25},{4,30},{5,31},{6,28},{7,29},{8,2},{9,3... | collective-permute-start | bytes 626696 | tf_op jit(solution)/shard_map/ppermute | solution.py:366
  13.9 14.5 %collective-permute-start.6 = (bf16[48,2176]{1,0:T(8,128)(2,1)S(1)}, bf16[48,2176]{1,0:T(8,128)(2,1)S(1)}, u32[]{:S(2)}, u32[]{:S(2)}) collective-permute-start(bf16[48,2176]{1,0:T(8,128)(2,1)S(1)} %get-tuple-element.33), channel_id=1, source_target_pairs={{0,27},{1,26},{2,25},{3,24},{4,31},{5,30},{6,29},{7,28},{8,3},{9,2... | collective-permute-start | bytes 626696 | tf_op jit(solution)/shard_map/ppermute | solution.py:366
  16.5 1.9 %copy-start = (bf16[1,768,2048]{2,1,0:T(8,128)(2,1)S(1)}, bf16[1,768,2048]{2,1,0:T(8,128)(2,1)}, u32[]{:S(2)}) copy-start(bf16[1,768,2048]{2,1,0:T(8,128)(2,1)} %param.10) | copy-start | bytes 9437188
  18.4 1.1 %copy-start.2 = (bf16[1,384,768]{2,1,0:T(8,128)(2,1)S(1)}, bf16[1,384,768]{2,1,0:T(8,128)(2,1)}, u32[]{:S(2)}) copy-start(bf16[1,384,768]{2,1,0:T(8,128)(2,1)} %param.9) | copy-start | bytes 1769476
  19.5 3.9 %copy-start.1 = (bf16[1,768,2048]{2,1,0:T(8,128)(2,1)S(1)}, bf16[1,768,2048]{2,1,0:T(8,128)(2,1)}, u32[]{:S(2)}) copy-start(bf16[1,768,2048]{2,1,0:T(8,128)(2,1)} %param.10) | copy-start | bytes 9437188
  22.6 6.6 %copy-start.3 = (bf16[1,384,768]{2,1,0:T(8,128)(2,1)S(1)}, bf16[1,384,768]{2,1,0:T(8,128)(2,1)}, u32[]{:S(2)}) copy-start(bf16[1,384,768]{2,1,0:T(8,128)(2,1)} %param.9) | copy-start | bytes 1769476
  22.6 13.5 %collective-permute-start.10 = (bf16[48,2048]{1,0:T(8,128)(2,1)S(1)}, bf16[48,2048]{1,0:T(8,128)(2,1)S(1)}, u32[]{:S(2)}, u32[]{:S(2)}) collective-permute-start(bf16[48,2048]{1,0:T(8,128)(2,1)S(1)} %get-tuple-element.44), channel_id=1, source_target_pairs={{0,3},{1,2},{2,1},{3,0},{4,7},{5,6},{6,5},{7,4},{8,11},{9,10},{10,... | collective-permute-start | bytes 589832 | tf_op jit(solution)/shard_map/ppermute | solution.py:366
  22.6 9.3 %collective-permute-start = (f32[8,128]{1,0:T(8,128)S(1)}, f32[8,128]{1,0:T(8,128)S(1)}, u32[]{:S(2)}, u32[]{:S(2)}) collective-permute-start(f32[8,128]{1,0:T(8,128)S(1)} %copy-done.6), channel_id=1, source_target_pairs={{0,6},{1,7},{2,4},{3,5},{4,2},{5,3},{6,0},{7,1},{8,14},{9,15},{10,... | collective-permute-start | bytes 12296 | tf_op jit(solution)/shard_map/ppermute | solution.py:366
  24.3 11.8 %collective-permute-start.11 = (bf16[48,2048]{1,0:T(8,128)(2,1)S(1)}, bf16[48,2048]{1,0:T(8,128)(2,1)S(1)}, u32[]{:S(2)}, u32[]{:S(2)}) collective-permute-start(bf16[48,2048]{1,0:T(8,128)(2,1)S(1)} %get-tuple-element.45), channel_id=1, source_target_pairs={{0,2},{1,3},{2,0},{3,1},{4,6},{5,7},{6,4},{7,5},{8,10},{9,11},{10,... | collective-permute-start | bytes 589832 | tf_op jit(solution)/shard_map/ppermute | solution.py:366
  28.3 17.4 %copy-start.5 = (bf16[2048,8]{0,1:T(8,128)(2,1)S(1)}, bf16[2048,8]{0,1:T(8,128)(2,1)}, u32[]{:S(2)}) copy-start(bf16[2048,8]{0,1:T(8,128)(2,1)} %param.11) | copy-start | bytes 98308
  28.3 8.5 %collective-permute-start.12 = (bf16[48,2048]{1,0:T(8,128)(2,1)S(1)}, bf16[48,2048]{1,0:T(8,128)(2,1)S(1)}, u32[]{:S(2)}, u32[]{:S(2)}) collective-permute-start(bf16[48,2048]{1,0:T(8,128)(2,1)S(1)} %get-tuple-element.46), channel_id=1, source_target_pairs={{0,1},{1,0},{2,3},{3,2},{4,5},{5,4},{6,7},{7,6},{8,9},{9,8},{10,11... | collective-permute-start | bytes 589832 | tf_op jit(solution)/shard_map/ppermute | solution.py:366
  32.5 12.9 %collective-permute-start.7 = (bf16[48,2176]{1,0:T(8,128)(2,1)S(1)}, bf16[48,2176]{1,0:T(8,128)(2,1)S(1)}, u32[]{:S(2)}, u32[]{:S(2)}) collective-permute-start(bf16[48,2176]{1,0:T(8,128)(2,1)S(1)} %get-tuple-element.40.refs_3_), channel_id=1, source_target_pairs={{0,3},{1,2},{2,1},{3,0},{4,7},{5,6},{6,5},{7,4},{8,11},{9,10},{10,... | collective-permute-start | bytes 626696 | tf_op jit(solution)/shard_map/ppermute | solution.py:366
  33.0 12.4 %collective-permute-start.8 = (bf16[48,2176]{1,0:T(8,128)(2,1)S(1)}, bf16[48,2176]{1,0:T(8,128)(2,1)S(1)}, u32[]{:S(2)}, u32[]{:S(2)}) collective-permute-start(bf16[48,2176]{1,0:T(8,128)(2,1)S(1)} %get-tuple-element.41.refs_2_), channel_id=1, source_target_pairs={{0,2},{1,3},{2,0},{3,1},{4,6},{5,7},{6,4},{7,5},{8,10},{9,11},{10,... | collective-permute-start | bytes 626696 | tf_op jit(solution)/shard_map/ppermute | solution.py:366
  36.1 9.6 %collective-permute-start.9 = (bf16[48,2176]{1,0:T(8,128)(2,1)S(1)}, bf16[48,2176]{1,0:T(8,128)(2,1)S(1)}, u32[]{:S(2)}, u32[]{:S(2)}) collective-permute-start(bf16[48,2176]{1,0:T(8,128)(2,1)S(1)} %get-tuple-element.42.refs_1_), channel_id=1, source_target_pairs={{0,1},{1,0},{2,3},{3,2},{4,5},{5,4},{6,7},{7,6},{8,9},{9,8},{10,11... | collective-permute-start | bytes 626696 | tf_op jit(solution)/shard_map/ppermute | solution.py:366
  37.1 8.3 %collective-permute-start.13 = (bf16[48,128]{1,0:T(8,128)(2,1)S(1)}, bf16[48,128]{1,0:T(8,128)(2,1)S(1)}, u32[]{:S(2)}, u32[]{:S(2)}) collective-permute-start(bf16[48,128]{1,0:T(8,128)(2,1)S(1)} %far_grad.1), channel_id=1, source_target_pairs={{0,6},{1,7},{2,4},{3,5},{4,2},{5,3},{6,0},{7,1},{8,14},{9,15},{10,... | collective-permute-start | bytes 36872 | tf_op jit(solution)/shard_map/ppermute | solution.py:366

commit v6 on v5

--- a/solution.py
+++ b/solution.py
@@ -14,7 +14,7 @@
 F32, BF16 = jnp.float32, jnp.bfloat16
 VMEM_LIMIT = 16 * 1024 * 1024
 COLUMN = 256
-SCALE = 3
+SCALE = 4
 OWN_ORDER, BACK_ORDER, FAR_ORDER = (0, 1, 2, 3), (0, 3, 2, 1), (0, 3, 2, 1)
 
 
@@ -81,14 +81,13 @@
     lane = iota((size, LANES), 1)
     for j in range(half):
         outs[j][:, 0:width] = packed[j * size : (j + 1) * size]
-        tail = jnp.concatenate(scales[j * MICRO : (j + 1) * MICRO], axis=0)
         if grads:
-            tail = jnp.where(lane < SCALE, grads[j][...].astype(F32), tail)
-        outs[j][:, width:] = tail.astype(BF16)
+            tail = jnp.concatenate(scales[j * MICRO : (j + 1) * MICRO], axis=0)
+            outs[j][:, width:] = jnp.where(lane < SCALE, grads[j][...].astype(F32), tail).astype(BF16)
 
 
 def pack(me, info, tokens, half, capacity, name, grads=()):
-    block = jax.ShapeDtypeStruct((MICRO * capacity, tokens.shape[1] + LANES), BF16)
+    block = jax.ShapeDtypeStruct((MICRO * capacity, tokens.shape[1] + LANES * bool(grads)), BF16)
     vmem = pl.BlockSpec(memory_space=pltpu.VMEM)
     return pl.pallas_call(
         functools.partial(pack_kernel, half, capacity),
@@ -139,22 +138,30 @@
     )(me, saved, weight)
 
 
-def turn_kernel(w_ref, after_ref, out_ref):
+def turn_kernel(half, capacity, me_ref, w_ref, info_ref, after_ref, out_ref, scale_ref):
     del after_ref
     for columns in chunks(w_ref.shape[1]):
         out_ref[columns, :] = w_ref[:, columns].T
-
-
-def turned(weight, after):
+    rank, weight = ranks(info_ref[...], jnp.bitwise_xor(me_ref[0], iota((8, LANES), 0)))
+    for j in range(half):
+        for m in range(MICRO):
+            _, scale = pick(rank[j : j + 1, :], weight[j : j + 1, :], m, capacity)
+            scale_ref[j, m * capacity : (m + 1) * capacity, :] = scale
+
+
+def turned(me, weight, info, after, half, capacity):
     vmem = pl.BlockSpec(memory_space=pltpu.VMEM)
     return pl.pallas_call(
-        turn_kernel,
-        out_shape=jax.ShapeDtypeStruct(weight.shape[::-1], BF16),
-        in_specs=[vmem, pl.BlockSpec(memory_space=pl.ANY)],
-        out_specs=vmem,
+        functools.partial(turn_kernel, half, capacity),
+        out_shape=[
+            jax.ShapeDtypeStruct(weight.shape[::-1], BF16),
+            jax.ShapeDtypeStruct((half, MICRO * capacity, LANES), F32),
+        ],
+        in_specs=[pl.BlockSpec(memory_space=pltpu.SMEM), vmem, vmem, pl.BlockSpec(memory_space=pl.ANY)],
+        out_specs=[vmem, vmem],
         compiler_params=pltpu.CompilerParams(vmem_limit_bytes=VMEM_LIMIT),
         name="turned",
-    )(weight, after)
+    )(me, weight, info, after)
 
 
 def far_grad_kernel(half, capacity, *refs):
@@ -186,83 +193,53 @@
     )(*blocks, *[backs[j] for j in BACK_ORDER])
 
 
-def expert_kernel(half, capacity, turn, graded, me_ref, *refs):
-    order = OWN_ORDER if graded else FAR_ORDER
-    blocks, w_ref, refs = [refs[order.index(j)] for j in range(half)], refs[half], refs[half + 1 :]
-    if graded:
-        saved_ref, d_ref, *grads, lhs, product, scale, partial = refs
-    else:
-        _, d_ref, lhs, product, scale = refs
-    width, hidden_width = w_ref.shape
-    run = half * capacity
-    here = jnp.bitwise_xor(lax.rem(me_ref[0], half), turn)
+def own_kernel(half, capacity, me_ref, *refs):
+    blocks, refs = [refs[OWN_ORDER.index(j)] for j in range(half)], refs[half:]
+    w_ref, saved_ref, scale_ref, product, grads = refs[0], refs[1], refs[2], refs[3], refs[4 : 4 + half]
+    lhs, partial = refs[4 + half :]
+    hidden_width = w_ref.shape[1]
+    run, size = half * capacity, MICRO * capacity
+    me = me_ref[0]
+    here, side = lax.rem(me, half), me // half
     places = []
     for j in range(half):
+        lhs[j * size : (j + 1) * size, :] = blocks[j][...]
         for m in range(MICRO):
             slot = pl.multiple_of(m * run + jnp.bitwise_xor(here, j) * capacity, 8)
-            places.append((j, m * capacity, (j * MICRO + m) * capacity, slot))
-    for j in range(half):
-        lhs[j * MICRO * capacity : (j + 1) * MICRO * capacity, :] = blocks[j][:, 0:width]
-    for j, row, _, slot in places:
-        tail = blocks[j][row : row + capacity, width:].astype(F32)
-        scale[pl.ds(slot, capacity), :] = jnp.broadcast_to(tail[:, SCALE : SCALE + 1], tail.shape)
+            places.append((j, m * capacity, slot))
     for columns in chunks(hidden_width):
         got = jnp.dot(lhs[...], w_ref[:, columns], preferred_element_type=F32)
-        for _, _, begin, slot in places:
-            product[pl.ds(slot, capacity), columns] = got[begin : begin + capacity, :]
-    total = jnp.zeros((MICRO * run, LANES), F32)
-    for lane in range(0, hidden_width, LANES):
-        part = product[:, lane : lane + LANES]
-        scaled = (scale[...] * part).astype(BF16)
-        for m in range(MICRO):
-            d_ref[m, 0, :, lane : lane + LANES] = scaled[m * run : (m + 1) * run]
-        if graded:
-            held = jnp.concatenate([saved_ref[m, 0, :, lane : lane + LANES] for m in range(MICRO)], axis=0)
-            total = total + part * held.astype(F32)
-    if graded:
-        partial[...] = total
-        lane = iota((capacity, LANES), 1)
-        for j, row, _, slot in places:
-            parts = split(jnp.sum(partial[pl.ds(slot, capacity), :], axis=1, keepdims=True))
-            table = jnp.where(lane == 0, parts[0], jnp.where(lane == 1, parts[1], parts[2]))
-            grads[j][row : row + capacity, :] = table.astype(BF16)
-
-
-def expert(me, blocks, weight, half, capacity, turn, saved=None, held=None):
+        for j, row, slot in places:
+            product[pl.ds(slot, capacity), columns] = got[j * size + row : j * size + row + capacity, :]
+    for m in range(MICRO):
+        total = jnp.zeros((run, LANES), F32)
+        for lane in range(0, hidden_width, LANES):
+            held = saved_ref[m, side, :, lane : lane + LANES].astype(F32)
+            total = total + product[m * run : (m + 1) * run, lane : lane + LANES] * held
+        partial[m * run : (m + 1) * run, :] = total
+    lane = iota((capacity, LANES), 1)
+    for j, row, slot in places:
+        parts = split(jnp.sum(partial[pl.ds(slot, capacity), :], axis=1, keepdims=True))
+        table = scale_ref[j, row : row + capacity, :]
+        for i, part in enumerate(parts):
+            table = jnp.where(lane == i, part, table)
+        grads[j][row : row + capacity, :] = table.astype(BF16)
+
+
+def own_expert(me, blocks, weight, saved, scales, half, capacity):
     width, hidden_width = weight.shape
-    run, rows = half * capacity, MICRO * capacity
-    graded = held is None
-    anywhere = pl.BlockSpec(memory_space=pl.ANY)
-    side = (lambda me: me[0] // half) if graded else (lambda me: 1 - me[0] // half)
-    slots = pl.BlockSpec((MICRO, 1, run, hidden_width), lambda i, me: (0, side(me), 0, 0))
-    in_specs = [pl.BlockSpec(memory_space=pltpu.VMEM)] * (half + 1)
-    scratch = [
-        pltpu.VMEM((MICRO * run, width), BF16),
-        pltpu.VMEM((MICRO * run, hidden_width), F32),
-        pltpu.VMEM((MICRO * run, LANES), F32),
-    ]
-    if graded:
-        out_shape = [jax.ShapeDtypeStruct(saved.shape, BF16)] + [jax.ShapeDtypeStruct((rows, LANES), BF16)] * half
-        out_specs = [slots] + [pl.BlockSpec((rows, LANES), lambda i, me: (0, 0))] * half
-        scratch.append(pltpu.VMEM((MICRO * run, LANES), F32))
-        operands, in_specs, aliases = [saved], in_specs + [slots], {}
-    else:
-        out_shape, out_specs = [jax.ShapeDtypeStruct(held.shape, BF16)], [slots]
-        operands, in_specs, aliases = [held], in_specs + [anywhere], {half + 2: 0}
-    return pl.pallas_call(
-        functools.partial(expert_kernel, half, capacity, turn, graded),
-        grid_spec=pltpu.PrefetchScalarGridSpec(
-            num_scalar_prefetch=1,
-            grid=(1,),
-            in_specs=in_specs,
-            out_specs=out_specs,
-            scratch_shapes=scratch,
-        ),
-        out_shape=out_shape,
-        input_output_aliases=aliases,
-        compiler_params=pltpu.CompilerParams(vmem_limit_bytes=VMEM_LIMIT),
-        name="expert_own" if graded else "expert_far",
-    )(me, *[blocks[j] for j in (OWN_ORDER if graded else FAR_ORDER)], weight, *operands)
+    rows = MICRO * capacity
+    vmem = pl.BlockSpec(memory_space=pltpu.VMEM)
+    return pl.pallas_call(
+        functools.partial(own_kernel, half, capacity),
+        out_shape=[jax.ShapeDtypeStruct((half * rows, hidden_width), F32)]
+        + [jax.ShapeDtypeStruct((rows, LANES), BF16)] * half,
+        in_specs=[pl.BlockSpec(memory_space=pltpu.SMEM)] + [vmem] * (half + 3),
+        out_specs=[vmem] * (1 + half),
+        scratch_shapes=[pltpu.VMEM((half * rows, width), BF16), pltpu.VMEM((half * rows, LANES), F32)],
+        compiler_params=pltpu.CompilerParams(vmem_limit_bytes=VMEM_LIMIT),
+        name="own_expert",
+    )(me, *[blocks[j] for j in OWN_ORDER], weight, saved, scales)
 
 
 def router_rows(half, capacity, turn, me, info_ref, own, far_ref, router_ref):
@@ -298,64 +275,74 @@
 
 def last_kernel(half, capacity, turn, me_ref, *refs):
     blocks, refs = [refs[FAR_ORDER.index(j)] for j in range(half)], refs[half:]
-    w_ref, info_ref, far_ref, router_ref, _, d_ref, out_ref = refs[:7]
+    w_ref, own_ref, info_ref, far_ref, router_ref, d_ref, out_ref = refs[:7]
     lhs, product, scale, rows, hidden, row_sem, hidden_sem = refs[7:]
     width, hidden_width = w_ref.shape
     run, size = half * capacity, MICRO * capacity
     me = me_ref[0]
-    here = jnp.bitwise_xor(lax.rem(me, half), turn)
-    side = 1 - me // half
-    own = [block[:, width:] for block in blocks]
-    rows[...] = router_rows(half, capacity, turn, me, info_ref, own, far_ref, router_ref)
-    row_copy = pltpu.make_async_copy(rows, out_ref, row_sem)
-    row_copy.start()
-    places = []
+    side = me // half
+    tails = [block[:, width:] for block in blocks]
+    rows[...] = router_rows(half, capacity, turn, me, info_ref, tails, far_ref, router_ref)
+    copies = [pltpu.make_async_copy(rows, out_ref, row_sem)]
+    copies[0].start()
+    here = lax.rem(me, half)
+
+    def scaled(far, source, lane_of, slots):
+        for j in range(half):
+            for m in range(MICRO):
+                tail = tails[j][m * capacity : (m + 1) * capacity].astype(F32)
+                column = jnp.broadcast_to(tail[:, lane_of : lane_of + 1], tail.shape)
+                scale[pl.ds(slots[j][m], capacity), :] = column
+        for m in range(MICRO):
+            at = slice(m * run, (m + 1) * run)
+            for lane in range(0, hidden_width, LANES):
+                lanes = slice(lane, lane + LANES)
+                hidden[far, m, :, lanes] = (scale[at, :] * source[at, lanes]).astype(BF16)
+            to = d_ref.at[m, 1 - side if far else side]
+            copies.append(pltpu.make_async_copy(hidden.at[far, m], to, hidden_sem.at[far, m]))
+            copies[-1].start()
+
+    def slots_of(first):
+        return [
+            [pl.multiple_of(m * run + jnp.bitwise_xor(first, j) * capacity, 8) for m in range(MICRO)] for j in range(half)
+        ]
+
+    scaled(0, own_ref, SCALE - 1, slots_of(here))
+    far_slots = slots_of(jnp.bitwise_xor(here, turn))
     for j in range(half):
         lhs[j * size : (j + 1) * size, :] = blocks[j][:, 0:width]
-        for m in range(MICRO):
-            slot = pl.multiple_of(m * run + jnp.bitwise_xor(here, j) * capacity, 8)
-            places.append((j * size + m * capacity, slot))
-            tail = own[j][m * capacity : (m + 1) * capacity].astype(F32)
-            scale[pl.ds(slot, capacity), :] = jnp.broadcast_to(tail[:, SCALE : SCALE + 1], tail.shape)
     for columns in chunks(hidden_width):
         got = jnp.dot(lhs[...], w_ref[:, columns], preferred_element_type=F32)
-        for begin, slot in places:
-            product[pl.ds(slot, capacity), columns] = got[begin : begin + capacity, :]
-    copies = []
-    for m in range(MICRO):
-        at = slice(m * run, (m + 1) * run)
-        for lane in range(0, hidden_width, LANES):
-            lanes = slice(lane, lane + LANES)
-            hidden[m, :, lanes] = (scale[at, :] * product[at, lanes]).astype(BF16)
-        copies.append(pltpu.make_async_copy(hidden.at[m], d_ref.at[m, side], hidden_sem.at[m]))
-        copies[m].start()
+        for j in range(half):
+            for m in range(MICRO):
+                begin = j * size + m * capacity
+                product[pl.ds(far_slots[j][m], capacity), columns] = got[begin : begin + capacity, :]
+    scaled(1, product, SCALE, far_slots)
     for copy in copies:
         copy.wait()
-    row_copy.wait()
-
-
-def last(me, blocks, weight, info, far, table, held, tokens, half, capacity, turn):
+
+
+def last(me, blocks, weight, own, info, far, table, saved, tokens, half, capacity, turn):
     width, hidden_width = weight.shape
     run = half * capacity
     vmem, anywhere = pl.BlockSpec(memory_space=pltpu.VMEM), pl.BlockSpec(memory_space=pl.ANY)
     return pl.pallas_call(
         functools.partial(last_kernel, half, capacity, turn),
-        out_shape=[jax.ShapeDtypeStruct(held.shape, BF16), jax.ShapeDtypeStruct(tokens.shape, BF16)],
-        in_specs=[pl.BlockSpec(memory_space=pltpu.SMEM)] + [vmem] * (half + 4) + [anywhere],
+        out_shape=[jax.ShapeDtypeStruct(saved.shape, BF16), jax.ShapeDtypeStruct(tokens.shape, BF16)],
+        in_specs=[pl.BlockSpec(memory_space=pltpu.SMEM)] + [vmem] * (half + 5),
         out_specs=[anywhere, anywhere],
         scratch_shapes=[
             pltpu.VMEM((MICRO * run, width), BF16),
             pltpu.VMEM((MICRO * run, hidden_width), F32),
             pltpu.VMEM((MICRO * run, LANES), F32),
             pltpu.VMEM(tokens.shape, BF16),
-            pltpu.VMEM((MICRO, run, hidden_width), BF16),
+            pltpu.VMEM((2, MICRO, run, hidden_width), BF16),
             pltpu.SemaphoreType.DMA,
-            pltpu.SemaphoreType.DMA((MICRO,)),
+            pltpu.SemaphoreType.DMA((2, MICRO)),
         ],
-        input_output_aliases={half + 5: 0},
         compiler_params=pltpu.CompilerParams(vmem_limit_bytes=VMEM_LIMIT),
         name="last",
-    )(me, *[blocks[j] for j in FAR_ORDER], weight, info, far, table, held)
+    )(me, *[blocks[j] for j in FAR_ORDER], weight, own, info, far, table)
 
 
 def route(block, flip, back):
@@ -390,16 +377,18 @@
     far_info = route(info, half + turn, 0)
     far_tokens = route(tokens, half + turn, 1)
     packed = pack(me, next_info, tokens, half, capacity, "pack_own")
-    weight_t = turned(weight, packed[0])
+    weight_t, scales = turned(me, weight, info, packed[0], half, capacity)
     saved, packed = lax.optimization_barrier((saved, packed))
     backs = back(me, saved, weight, half, capacity, turn)
     own = [route(packed[j], j, 1) for j in range(half)]
     backs = spread(backs)
-    held, *own_grads = expert(me, own, weight_t, half, capacity, 0, saved=saved)
+    own_product, *own_grads = own_expert(me, own, weight_t, saved, scales, half, capacity)
     far = pack(me, far_info, far_tokens, half, capacity, "pack_far", own_grads)
     far_grads = route(far_grad(far, backs, half, capacity), half + turn, 0)
     far = spread(far)
-    d_hidden, grad_in = last(me, far, weight_t, info, far_grads, w_router.T, held, tokens, half, capacity, turn)
+    d_hidden, grad_in = last(
+        me, far, weight_t, own_product, info, far_grads, w_router.T, saved, tokens, half, capacity, turn
+    )
     return d_hidden.reshape(saved_hidden.shape), grad_in[None]
 
 

time: 48.1 us -> 47.7 us (level)
  Pallas kernels: 8.2 us -> 7.57 us
    pallas_call x2, Pallas kernels: 2.65 us -> 1.95 us  [the longest x1 1.01 us: own_expert(): pl.pallas_call(functools.partial(own_kernel, half, capacity), out_shape=[...]
  transfers between devices with their start and end apart: 14 -> 14, of which waited for: 7 -> 8; matrix products, arithmetic and copies ran while one was open for 0% -> 0% of each run, Pallas kernels for 13% -> 11%
where the time goes in v6:
time: 47.7 us; the launch traced here: 47.4 us
  starting transfers between devices  21.6 us (45%)
  waiting for transfers between devices  13.5 us (28%)
  Pallas kernels  7.57 us (16%)
  local copies, waits for them, and re-layouts  4.01 us (8%)
  between operations  0.71 us (1%)
    ppermute x14, starting transfers between devices, route(): return lax.ppermute(block, ('pipe', 'expert'), pairs)  21.6 us
    ppermute x14, waiting for transfers between devices, route(): return lax.ppermute(block, ('pipe', 'expert'), pairs)  13.5 us
    unnamed x14, local copies, waits for them, and re-layouts  4.01 us
    pallas_call x1, Pallas kernels, last(): pl.pallas_call(functools.partial(last_kernel, half, capacity, turn), out_...  2.14 us
    pallas_call x1, Pallas kernels, by_halves(): pl.pallas_call(info_kernel, out_shape=jax.ShapeDtypeStruct((8, LANES), F3...  1.31 us
    pallas_call x1, Pallas kernels, own_expert(): pl.pallas_call(functools.partial(own_kernel, half, capacity), out_shape=[...  1.01 us
    pallas_call x2, Pallas kernels, pack(): pl.pallas_call(functools.partial(pack_kernel, half, capacity), out_shape=...  0.97 us
  transfers between devices with their start and end apart: 14, of which 8 were waited for; matrix products, arithmetic and copies ran while one was open for 0% of the time, Pallas kernels for 11%

profile of v6, /device:TPU:0, one launch (start us, length us, event | category | flops | bytes accessed | tf_op | source)
XLA Modules:
  0.0 47.4 jit_solution(10100890543171951237)
XLA Ops:
  0.6 5.5 %collective-permute-start.1 = (bf16[128,2048]{1,0:T(8,128)(2,1)}, bf16[128,2048]{1,0:T(8,128)(2,1)S(1)}, u32[]{:S(2)}, u32[]{:S(2)}) collective-permute-start(bf16[128,2048]{1,0:T(8,128)(2,1)} %bitcast.17), channel_id=1, source_target_pairs={{0,30},{1,31},{2,28},{3,29},{4,26},{5,27},{6,24},{7,25},{8,6},{9,7... | collective-permute-start | bytes 1572872 | tf_op jit(solution)/shard_map/ppermute | solution.py:353
  6.1 1.3 %info.1.info_ref.refs_6_ = f32[8,128]{1,0:T(8,128)} custom-call(s32[2,128]{1,0:T(2,128)} %bitcast.21, f32[8,128]{1,0:T(8,128)} %bitcast.20), custom_call_target="tpu_custom_call" | custom-call | tf_op jit(solution)/shard_map/info/pallas_call | solution.py:369
  7.4 0.0 copy-start.5
  7.4 0.0 collective-permute-start.2
  7.4 3.3 %collective-permute-done.2.info_ref = f32[8,128]{1,0:T(8,128)S(1)} collective-permute-done((f32[8,128]{1,0:T(8,128)}, f32[8,128]{1,0:T(8,128)S(1)}, u32[]{:S(2)}, u32[]{:S(2)}) %collective-permute-start.2) | collective-permute-done | bytes 4128 | tf_op jit(solution)/shard_map/ppermute | solution.py:353
  10.7 0.0 copy-start.4
  10.7 1.0 %copy-done.4 = bf16[1,128,2048]{2,1,0:T(8,128)(2,1)S(1)} copy-done((bf16[1,128,2048]{2,1,0:T(8,128)(2,1)S(1)}, bf16[1,128,2048]{2,1,0:T(8,128)(2,1)}, u32[]{:S(2)}) %copy-start.4) | copy-done | bytes 524312
  11.8 0.5 %pack_own.1 = (bf16[48,2048]{1,0:T(8,128)(2,1)S(1)}, bf16[48,2048]{1,0:T(8,128)(2,1)S(1)}, bf16[48,2048]{1,0:T(8,128)(2,1)S(1)}, bf16[48,2048]{1,0:T(8,128)(2,1)S(1)}) custom-call(s32[1]{0:T(128)} %bitcast.me_ref, f32[8,128]{1,0:T(8,128)S(1)} %collective-permute-done.2.info_ref, bf16[128,2048]{1,0:T(8,128)(2,1)S(1)} %bitcast.18), custom_call_target="tpu_custom_call" | custom-call | tf_op jit(solution)/shard_map/pack_own/pallas_call | solution.py:92
  12.3 0.1 collective-permute-start.3
  12.3 1.5 %collective-permute-start.4 = (bf16[48,2048]{1,0:T(8,128)(2,1)S(1)}, bf16[48,2048]{1,0:T(8,128)(2,1)S(1)}, u32[]{:S(2)}, u32[]{:S(2)}) collective-permute-start(bf16[48,2048]{1,0:T(8,128)(2,1)S(1)} %get-tuple-element.33), channel_id=1, source_target_pairs={{0,25},{1,24},{2,27},{3,26},{4,29},{5,28},{6,31},{7,30},{8,1},{9,0... | collective-permute-start | bytes 589832 | tf_op jit(solution)/shard_map/ppermute | solution.py:353
  13.9 0.0 collective-permute-start.5
  13.9 2.7 %collective-permute-start.6 = (bf16[48,2048]{1,0:T(8,128)(2,1)S(1)}, bf16[48,2048]{1,0:T(8,128)(2,1)S(1)}, u32[]{:S(2)}, u32[]{:S(2)}) collective-permute-start(bf16[48,2048]{1,0:T(8,128)(2,1)S(1)} %get-tuple-element.35), channel_id=1, source_target_pairs={{0,27},{1,26},{2,25},{3,24},{4,31},{5,30},{6,29},{7,28},{8,3},{9,2... | collective-permute-start | bytes 589832 | tf_op jit(solution)/shard_map/ppermute | solution.py:353
  16.5 0.0 copy-start
  16.5 1.9 %copy-done = bf16[1,768,2048]{2,1,0:T(8,128)(2,1)S(1)} copy-done((bf16[1,768,2048]{2,1,0:T(8,128)(2,1)S(1)}, bf16[1,768,2048]{2,1,0:T(8,128)(2,1)}, u32[]{:S(2)}) %copy-start) | copy-done | bytes 3145752
  18.4 0.0 copy-start.2
  18.4 1.1 %copy-done.2 = bf16[1,384,768]{2,1,0:T(8,128)(2,1)S(1)} copy-done((bf16[1,384,768]{2,1,0:T(8,128)(2,1)S(1)}, bf16[1,384,768]{2,1,0:T(8,128)(2,1)}, u32[]{:S(2)}) %copy-start.2) | copy-done | bytes 589848
  19.5 0.0 copy-start.1
  19.5 0.0 copy-start.3
  19.5 0.9 %back.1 = (bf16[48,2048]{1,0:T(8,128)(2,1)S(1)}, bf16[48,2048]{1,0:T(8,128)(2,1)S(1)}, bf16[48,2048]{1,0:T(8,128)(2,1)S(1)}, bf16[48,2048]{1,0:T(8,128)(2,1)S(1)}) custom-call(s32[1]{0:T(128)} %bitcast.me_ref, bf16[2,2,96,768]{3,2,1,0:T(8,128)(2,1)S(1)} %bitcast.15, bf16[768,2048]{1,0:T(8,128)(2,1)S(1)} %bitcast.13), custom_call_target="tpu_custom_call" | custom-call | tf_op jit(solution)/shard_map/back/pallas_call | solution.py:123
  20.4 1.8 %collective-permute-done.3.refs_0_ = bf16[48,2048]{1,0:T(8,128)(2,1)S(1)} collective-permute-done((bf16[48,2048]{1,0:T(8,128)(2,1)S(1)}, bf16[48,2048]{1,0:T(8,128)(2,1)S(1)}, u32[]{:S(2)}, u32[]{:S(2)}) %collective-permute-start.3) | collective-permute-done | bytes 196640 | tf_op jit(solution)/shard_map/ppermute | solution.py:353
  22.2 0.0 collective-permute-start.10
  22.2 0.0 collective-permute-done.4.refs_1_
  22.2 0.0 copy-done.5
  22.2 0.6 %collective-permute-start = (f32[8,128]{1,0:T(8,128)S(1)}, f32[8,128]{1,0:T(8,128)S(1)}, u32[]{:S(2)}, u32[]{:S(2)}) collective-permute-start(f32[8,128]{1,0:T(8,128)S(1)} %copy-done.5), channel_id=1, source_target_pairs={{0,6},{1,7},{2,4},{3,5},{4,2},{5,3},{6,0},{7,1},{8,14},{9,15},{10,... | collective-permute-start | bytes 12296 | tf_op jit(solution)/shard_map/ppermute | solution.py:353
  22.9 0.0 copy-done.1
  22.9 0.9 %turned.1 = (bf16[2048,768]{1,0:T(8,128)(2,1)S(1)}, f32[4,48,128]{2,1,0:T(8,128)S(1)}) custom-call(s32[1]{0:T(128)} %bitcast.me_ref, bf16[768,2048]{1,0:T(8,128)(2,1)S(1)} %bitcast.14, f32[8,128]{1,0:T(8,128)S(1)} %copy-done.5, bf16[48,2048]{1,0:T(8,128)(2,1)S(1)} %get-tuple-element.32.after_ref), custom_call_target="tpu_custom_call" | custom-call | tf_op jit(solution)/shard_map/turned/pallas_call | solution.py:154
  23.8 0.0 collective-permute-done.5.refs_2_
  23.8 3.0 %collective-permute-start.11 = (bf16[48,2048]{1,0:T(8,128)(2,1)S(1)}, bf16[48,2048]{1,0:T(8,128)(2,1)S(1)}, u32[]{:S(2)}, u32[]{:S(2)}) collective-permute-start(bf16[48,2048]{1,0:T(8,128)(2,1)S(1)} %get-tuple-element.50), channel_id=1, source_target_pairs={{0,2},{1,3},{2,0},{3,1},{4,6},{5,7},{6,4},{7,5},{8,10},{9,11},{10,... | collective-permute-start | bytes 589832 | tf_op jit(solution)/shard_map/ppermute | solution.py:353
  26.9 0.9 %collective-permute-done.6.refs_3_ = bf16[48,2048]{1,0:T(8,128)(2,1)S(1)} collective-permute-done((bf16[48,2048]{1,0:T(8,128)(2,1)S(1)}, bf16[48,2048]{1,0:T(8,128)(2,1)S(1)}, u32[]{:S(2)}, u32[]{:S(2)}) %collective-permute-start.6) | collective-permute-done | bytes 196640 | tf_op jit(solution)/shard_map/ppermute | solution.py:353
  27.8 0.8 %collective-permute-start.12 = (bf16[48,2048]{1,0:T(8,128)(2,1)S(1)}, bf16[48,2048]{1,0:T(8,128)(2,1)S(1)}, u32[]{:S(2)}, u32[]{:S(2)}) collective-permute-start(bf16[48,2048]{1,0:T(8,128)(2,1)S(1)} %get-tuple-element.51), channel_id=1, source_target_pairs={{0,1},{1,0},{2,3},{3,2},{4,5},{5,4},{6,7},{7,6},{8,9},{9,8},{10,11... | collective-permute-start | bytes 589832 | tf_op jit(solution)/shard_map/ppermute | solution.py:353
  28.6 0.0 copy-done.3
  28.6 0.0 copy-start.6
  28.7 1.0 %own_expert.1 = (f32[192,768]{1,0:T(8,128)S(1)}, bf16[48,128]{1,0:T(8,128)(2,1)S(1)}, bf16[48,128]{1,0:T(8,128)(2,1)S(1)}, bf16[48,128]{1,0:T(8,128)(2,1)S(1)}, bf16[48,128]{1,0:T(8,128)(2,1)S(1)}) custom-call(s32[1]{0:T(128)} %bitcast.me_ref, bf16[48,2048]{1,0:T(8,128)(2,1)S(1)} %collective-permute-done.3.refs_0_, ...), custom_call_target="tpu_custom_call" | custom-call | tf_op jit(solution)/shard_map/own_expert/pallas_call | solution.py:233
  29.7 1.8 %collective-permute-done.info_ref = f32[8,128]{1,0:T(8,128)S(1)} collective-permute-done((f32[8,128]{1,0:T(8,128)S(1)}, f32[8,128]{1,0:T(8,128)S(1)}, u32[]{:S(2)}, u32[]{:S(2)}) %collective-permute-start) | collective-permute-done | bytes 4128 | tf_op jit(solution)/shard_map/ppermute | solution.py:353
  31.5 0.0 collective-permute-done.1.token_ref
  31.5 0.5 %pack_far.1 = (bf16[48,2176]{1,0:T(8,128)(2,1)S(1)}, bf16[48,2176]{1,0:T(8,128)(2,1)S(1)}, bf16[48,2176]{1,0:T(8,128)(2,1)S(1)}, bf16[48,2176]{1,0:T(8,128)(2,1)S(1)}) custom-call(s32[1]{0:T(128)} %bitcast.me_ref, f32[8,128]{1,0:T(8,128)S(1)} %collective-permute-done.info_ref, bf16[128,2048]{1,0:T(8,128)(2,1)S(1)} %collective-permute-done.1.token_ref, ...), custom_call_target="tpu_custom_call" | custom-call | tf_op jit(solution)/shard_map/pack_far/pallas_call | solution.py:92
  32.0 0.1 collective-permute-start.7
  32.0 3.6 %collective-permute-start.8 = (bf16[48,2176]{1,0:T(8,128)(2,1)S(1)}, bf16[48,2176]{1,0:T(8,128)(2,1)S(1)}, u32[]{:S(2)}, u32[]{:S(2)}) collective-permute-start(bf16[48,2176]{1,0:T(8,128)(2,1)S(1)} %get-tuple-element.45.refs_2_), channel_id=1, source_target_pairs={{0,2},{1,3},{2,0},{3,1},{4,6},{5,7},{6,4},{7,5},{8,10},{9,11},{10,... | collective-permute-start | bytes 626696 | tf_op jit(solution)/shard_map/ppermute | solution.py:353
  35.6 0.0 collective-permute-done.10.refs_5_
  35.6 0.0 collective-permute-start.9
  35.6 0.2 collective-permute-done.11.refs_6_
  35.8 0.5 %collective-permute-done.12.refs_7_ = bf16[48,2048]{1,0:T(8,128)(2,1)S(1)} collective-permute-done((bf16[48,2048]{1,0:T(8,128)(2,1)S(1)}, bf16[48,2048]{1,0:T(8,128)(2,1)S(1)}, u32[]{:S(2)}, u32[]{:S(2)}) %collective-permute-start.12) | collective-permute-done | bytes 196640 | tf_op jit(solution)/shard_map/ppermute | solution.py:353
  36.3 0.3 far_grad.1
  36.6 3.7 %collective-permute-start.13 = (bf16[48,128]{1,0:T(8,128)(2,1)S(1)}, bf16[48,128]{1,0:T(8,128)(2,1)S(1)}, u32[]{:S(2)}, u32[]{:S(2)}) collective-permute-start(bf16[48,128]{1,0:T(8,128)(2,1)S(1)} %far_grad.1), channel_id=1, source_target_pairs={{0,6},{1,7},{2,4},{3,5},{4,2},{5,3},{6,0},{7,1},{8,14},{9,15},{10,... | collective-permute-start | bytes 36872 | tf_op jit(solution)/shard_map/ppermute | solution.py:353
  40.3 4.2 %collective-permute-done.13.refs_7_ = bf16[48,128]{1,0:T(8,128)(2,1)S(1)} collective-permute-done((bf16[48,128]{1,0:T(8,128)(2,1)S(1)}, bf16[48,128]{1,0:T(8,128)(2,1)S(1)}, u32[]{:S(2)}, u32[]{:S(2)}) %collective-permute-start.13) | collective-permute-done | bytes 12320 | tf_op jit(solution)/shard_map/ppermute | solution.py:353
  44.4 0.0 collective-permute-done.7.refs_1_
  44.4 0.0 collective-permute-done.8.refs_2_
  44.4 0.8 %collective-permute-done.9.refs_3_ = bf16[48,2176]{1,0:T(8,128)(2,1)S(1)} collective-permute-done((bf16[48,2176]{1,0:T(8,128)(2,1)S(1)}, bf16[48,2176]{1,0:T(8,128)(2,1)S(1)}, u32[]{:S(2)}, u32[]{:S(2)}) %collective-permute-start.9) | collective-permute-done | bytes 208928 | tf_op jit(solution)/shard_map/ppermute | solution.py:353
  45.2 0.0 copy-done.6
  45.2 2.1 %last.1 = (bf16[2,2,96,768]{3,2,1,0:T(8,128)(2,1)}, bf16[128,2048]{1,0:T(8,128)(2,1)}) custom-call(s32[1]{0:T(128)} %bitcast.me_ref, bf16[48,2176]{1,0:T(8,128)(2,1)S(1)} %get-tuple-element.43.refs_0_, bf16[48,2176]{1,0:T(8,128)(2,1)S(1)} %collective-permute-done.7.refs_1_, bf16[48,2176]{1,0:T(8,128)(2,1)S(1)} %collective-permute-done.8.refs_2_, ...), custom_call_target="tpu_custom_call" | custom-call | tf_op jit(solution)/shard_map/last/pallas_call | solution.py:329
Async XLA Ops:
  0.6 30.8 %collective-permute-start.1 = (bf16[128,2048]{1,0:T(8,128)(2,1)}, bf16[128,2048]{1,0:T(8,128)(2,1)S(1)}, u32[]{:S(2)}, u32[]{:S(2)}) collective-permute-start(bf16[128,2048]{1,0:T(8,128)(2,1)} %bitcast.17), channel_id=1, source_target_pairs={{0,30},{1,31},{2,28},{3,29},{4,26},{5,27},{6,24},{7,25},{8,6},{9,7... | collective-permute-start | bytes 1572872 | tf_op jit(solution)/shard_map/ppermute | solution.py:353
  7.4 14.8 %copy-start.5 = (f32[8,128]{1,0:T(8,128)S(1)}, f32[8,128]{1,0:T(8,128)}, u32[]{:S(2)}) copy-start(f32[8,128]{1,0:T(8,128)} %info.1.info_ref.refs_6_) | copy-start | bytes 12292
  7.4 3.3 %collective-permute-start.2 = (f32[8,128]{1,0:T(8,128)}, f32[8,128]{1,0:T(8,128)S(1)}, u32[]{:S(2)}, u32[]{:S(2)}) collective-permute-start(f32[8,128]{1,0:T(8,128)} %info.1.info_ref.refs_6_), channel_id=1, source_target_pairs={{0,8},{1,9},{2,10},{3,11},{4,12},{5,13},{6,14},{7,15},{8,16},{9,17... | collective-permute-start | bytes 12296 | tf_op jit(solution)/shard_map/ppermute | solution.py:353
  10.7 1.0 %copy-start.4 = (bf16[1,128,2048]{2,1,0:T(8,128)(2,1)S(1)}, bf16[1,128,2048]{2,1,0:T(8,128)(2,1)}, u32[]{:S(2)}) copy-start(bf16[1,128,2048]{2,1,0:T(8,128)(2,1)} %param.6) | copy-start | bytes 1572868
  12.3 10.0 %collective-permute-start.3 = (bf16[48,2048]{1,0:T(8,128)(2,1)S(1)}, bf16[48,2048]{1,0:T(8,128)(2,1)S(1)}, u32[]{:S(2)}, u32[]{:S(2)}) collective-permute-start(bf16[48,2048]{1,0:T(8,128)(2,1)S(1)} %get-tuple-element.32.after_ref), channel_id=1, source_target_pairs={{0,24},{1,25},{2,26},{3,27},{4,28},{5,29},{6,30},{7,31},{8,0},{9,1... | collective-permute-start | bytes 589832 | tf_op jit(solution)/shard_map/ppermute | solution.py:353
  12.3 9.9 %collective-permute-start.4 = (bf16[48,2048]{1,0:T(8,128)(2,1)S(1)}, bf16[48,2048]{1,0:T(8,128)(2,1)S(1)}, u32[]{:S(2)}, u32[]{:S(2)}) collective-permute-start(bf16[48,2048]{1,0:T(8,128)(2,1)S(1)} %get-tuple-element.33), channel_id=1, source_target_pairs={{0,25},{1,24},{2,27},{3,26},{4,29},{5,28},{6,31},{7,30},{8,1},{9,0... | collective-permute-start | bytes 589832 | tf_op jit(solution)/shard_map/ppermute | solution.py:353
  13.9 10.0 %collective-permute-start.5 = (bf16[48,2048]{1,0:T(8,128)(2,1)S(1)}, bf16[48,2048]{1,0:T(8,128)(2,1)S(1)}, u32[]{:S(2)}, u32[]{:S(2)}) collective-permute-start(bf16[48,2048]{1,0:T(8,128)(2,1)S(1)} %get-tuple-element.34), channel_id=1, source_target_pairs={{0,26},{1,27},{2,24},{3,25},{4,30},{5,31},{6,28},{7,29},{8,2},{9,3... | collective-permute-start | bytes 589832 | tf_op jit(solution)/shard_map/ppermute | solution.py:353
  13.9 13.9 %collective-permute-start.6 = (bf16[48,2048]{1,0:T(8,128)(2,1)S(1)}, bf16[48,2048]{1,0:T(8,128)(2,1)S(1)}, u32[]{:S(2)}, u32[]{:S(2)}) collective-permute-start(bf16[48,2048]{1,0:T(8,128)(2,1)S(1)} %get-tuple-element.35), channel_id=1, source_target_pairs={{0,27},{1,26},{2,25},{3,24},{4,31},{5,30},{6,29},{7,28},{8,3},{9,2... | collective-permute-start | bytes 589832 | tf_op jit(solution)/shard_map/ppermute | solution.py:353
  16.5 1.9 %copy-start = (bf16[1,768,2048]{2,1,0:T(8,128)(2,1)S(1)}, bf16[1,768,2048]{2,1,0:T(8,128)(2,1)}, u32[]{:S(2)}) copy-start(bf16[1,768,2048]{2,1,0:T(8,128)(2,1)} %param.10) | copy-start | bytes 9437188
  18.4 1.1 %copy-start.2 = (bf16[1,384,768]{2,1,0:T(8,128)(2,1)S(1)}, bf16[1,384,768]{2,1,0:T(8,128)(2,1)}, u32[]{:S(2)}) copy-start(bf16[1,384,768]{2,1,0:T(8,128)(2,1)} %param.9) | copy-start | bytes 1769476
  19.5 3.4 %copy-start.1 = (bf16[1,768,2048]{2,1,0:T(8,128)(2,1)S(1)}, bf16[1,768,2048]{2,1,0:T(8,128)(2,1)}, u32[]{:S(2)}) copy-start(bf16[1,768,2048]{2,1,0:T(8,128)(2,1)} %param.10) | copy-start | bytes 9437188
  19.5 9.2 %copy-start.3 = (bf16[1,384,768]{2,1,0:T(8,128)(2,1)S(1)}, bf16[1,384,768]{2,1,0:T(8,128)(2,1)}, u32[]{:S(2)}) copy-start(bf16[1,384,768]{2,1,0:T(8,128)(2,1)} %param.9) | copy-start | bytes 1769476
  22.2 13.4 %collective-permute-start.10 = (bf16[48,2048]{1,0:T(8,128)(2,1)S(1)}, bf16[48,2048]{1,0:T(8,128)(2,1)S(1)}, u32[]{:S(2)}, u32[]{:S(2)}) collective-permute-start(bf16[48,2048]{1,0:T(8,128)(2,1)S(1)} %get-tuple-element.49), channel_id=1, source_target_pairs={{0,3},{1,2},{2,1},{3,0},{4,7},{5,6},{6,5},{7,4},{8,11},{9,10},{10,... | collective-permute-start | bytes 589832 | tf_op jit(solution)/shard_map/ppermute | solution.py:353
  22.2 9.2 %collective-permute-start = (f32[8,128]{1,0:T(8,128)S(1)}, f32[8,128]{1,0:T(8,128)S(1)}, u32[]{:S(2)}, u32[]{:S(2)}) collective-permute-start(f32[8,128]{1,0:T(8,128)S(1)} %copy-done.5), channel_id=1, source_target_pairs={{0,6},{1,7},{2,4},{3,5},{4,2},{5,3},{6,0},{7,1},{8,14},{9,15},{10,... | collective-permute-start | bytes 12296 | tf_op jit(solution)/shard_map/ppermute | solution.py:353
  23.8 12.0 %collective-permute-start.11 = (bf16[48,2048]{1,0:T(8,128)(2,1)S(1)}, bf16[48,2048]{1,0:T(8,128)(2,1)S(1)}, u32[]{:S(2)}, u32[]{:S(2)}) collective-permute-start(bf16[48,2048]{1,0:T(8,128)(2,1)S(1)} %get-tuple-element.50), channel_id=1, source_target_pairs={{0,2},{1,3},{2,0},{3,1},{4,6},{5,7},{6,4},{7,5},{8,10},{9,11},{10,... | collective-permute-start | bytes 589832 | tf_op jit(solution)/shard_map/ppermute | solution.py:353
  27.8 8.5 %collective-permute-start.12 = (bf16[48,2048]{1,0:T(8,128)(2,1)S(1)}, bf16[48,2048]{1,0:T(8,128)(2,1)S(1)}, u32[]{:S(2)}, u32[]{:S(2)}) collective-permute-start(bf16[48,2048]{1,0:T(8,128)(2,1)S(1)} %get-tuple-element.51), channel_id=1, source_target_pairs={{0,1},{1,0},{2,3},{3,2},{4,5},{5,4},{6,7},{7,6},{8,9},{9,8},{10,11... | collective-permute-start | bytes 589832 | tf_op jit(solution)/shard_map/ppermute | solution.py:353
  28.6 16.6 %copy-start.6 = (bf16[2048,8]{0,1:T(8,128)(2,1)S(1)}, bf16[2048,8]{0,1:T(8,128)(2,1)}, u32[]{:S(2)}) copy-start(bf16[2048,8]{0,1:T(8,128)(2,1)} %param.11) | copy-start | bytes 98308
  32.0 12.5 %collective-permute-start.7 = (bf16[48,2176]{1,0:T(8,128)(2,1)S(1)}, bf16[48,2176]{1,0:T(8,128)(2,1)S(1)}, u32[]{:S(2)}, u32[]{:S(2)}) collective-permute-start(bf16[48,2176]{1,0:T(8,128)(2,1)S(1)} %get-tuple-element.44.refs_3_), channel_id=1, source_target_pairs={{0,3},{1,2},{2,1},{3,0},{4,7},{5,6},{6,5},{7,4},{8,11},{9,10},{10,... | collective-permute-start | bytes 626696 | tf_op jit(solution)/shard_map/ppermute | solution.py:353
  32.0 12.4 %collective-permute-start.8 = (bf16[48,2176]{1,0:T(8,128)(2,1)S(1)}, bf16[48,2176]{1,0:T(8,128)(2,1)S(1)}, u32[]{:S(2)}, u32[]{:S(2)}) collective-permute-start(bf16[48,2176]{1,0:T(8,128)(2,1)S(1)} %get-tuple-element.45.refs_2_), channel_id=1, source_target_pairs={{0,2},{1,3},{2,0},{3,1},{4,6},{5,7},{6,4},{7,5},{8,10},{9,11},{10,... | collective-permute-start | bytes 626696 | tf_op jit(solution)/shard_map/ppermute | solution.py:353
  35.6 9.6 %collective-permute-start.9 = (bf16[48,2176]{1,0:T(8,128)(2,1)S(1)}, bf16[48,2176]{1,0:T(8,128)(2,1)S(1)}, u32[]{:S(2)}, u32[]{:S(2)}) collective-permute-start(bf16[48,2176]{1,0:T(8,128)(2,1)S(1)} %get-tuple-element.46.refs_1_), channel_id=1, source_target_pairs={{0,1},{1,0},{2,3},{3,2},{4,5},{5,4},{6,7},{7,6},{8,9},{9,8},{10,11... | collective-permute-start | bytes 626696 | tf_op jit(solution)/shard_map/ppermute | solution.py:353
  36.6 7.8 %collective-permute-start.13 = (bf16[48,128]{1,0:T(8,128)(2,1)S(1)}, bf16[48,128]{1,0:T(8,128)(2,1)S(1)}, u32[]{:S(2)}, u32[]{:S(2)}) collective-permute-start(bf16[48,128]{1,0:T(8,128)(2,1)S(1)} %far_grad.1), channel_id=1, source_target_pairs={{0,6},{1,7},{2,4},{3,5},{4,2},{5,3},{6,0},{7,1},{8,14},{9,15},{10,... | collective-permute-start | bytes 36872 | tf_op jit(solution)/shard_map/ppermute | solution.py:353

commit v7 on v6

--- a/solution.py
+++ b/solution.py
@@ -112,9 +112,9 @@
     for columns in chunks(w_ref.shape[1]):
         product[:, columns] = jnp.dot(saved, w_ref[:, columns], preferred_element_type=F32)
     for j in range(half):
-        for m in range(MICRO):
-            slot = pl.multiple_of(m * run + jnp.bitwise_xor(here, j) * capacity, 8)
-            outs[j][m * capacity : (m + 1) * capacity, :] = product[pl.ds(slot, capacity), :].astype(BF16)
+        slots = [pl.multiple_of(m * run + jnp.bitwise_xor(here, j) * capacity, 8) for m in range(MICRO)]
+        rows = jnp.concatenate([product[pl.ds(slot, capacity), :] for slot in slots], axis=0)
+        outs[j][...] = rows.astype(BF16)
 
 
 def back(me, saved, weight, half, capacity, turn):
@@ -138,30 +138,36 @@
     )(me, saved, weight)
 
 
-def turn_kernel(half, capacity, me_ref, w_ref, info_ref, after_ref, out_ref, scale_ref):
+def turn_kernel(half, capacity, me_ref, w_ref, info_ref, router_ref, after_ref, out_ref, scale_ref, rank_ref, table_ref):
     del after_ref
+    router = router_ref[...].astype(F32)
+    router = jnp.concatenate([router, router, router, jnp.zeros((LANES - 24, router.shape[1]), F32)], axis=0)
+    table_ref[...] = router.astype(BF16)
     for columns in chunks(w_ref.shape[1]):
         out_ref[columns, :] = w_ref[:, columns].T
     rank, weight = ranks(info_ref[...], jnp.bitwise_xor(me_ref[0], iota((8, LANES), 0)))
+    rank_ref[...] = rank
     for j in range(half):
         for m in range(MICRO):
             _, scale = pick(rank[j : j + 1, :], weight[j : j + 1, :], m, capacity)
             scale_ref[j, m * capacity : (m + 1) * capacity, :] = scale
 
 
-def turned(me, weight, info, after, half, capacity):
+def turned(me, weight, info, router, after, half, capacity):
     vmem = pl.BlockSpec(memory_space=pltpu.VMEM)
     return pl.pallas_call(
         functools.partial(turn_kernel, half, capacity),
         out_shape=[
             jax.ShapeDtypeStruct(weight.shape[::-1], BF16),
             jax.ShapeDtypeStruct((half, MICRO * capacity, LANES), F32),
+            jax.ShapeDtypeStruct((8, LANES), jnp.int32),
+            jax.ShapeDtypeStruct((LANES, router.shape[1]), BF16),
         ],
-        in_specs=[pl.BlockSpec(memory_space=pltpu.SMEM), vmem, vmem, pl.BlockSpec(memory_space=pl.ANY)],
-        out_specs=[vmem, vmem],
+        in_specs=[pl.BlockSpec(memory_space=pltpu.SMEM), vmem, vmem, vmem, pl.BlockSpec(memory_space=pl.ANY)],
+        out_specs=[vmem] * 4,
         compiler_params=pltpu.CompilerParams(vmem_limit_bytes=VMEM_LIMIT),
         name="turned",
-    )(me, weight, info, after)
+    )(me, weight, info, router, after)
 
 
 def far_grad_kernel(half, capacity, *refs):
@@ -217,13 +223,14 @@
             held = saved_ref[m, side, :, lane : lane + LANES].astype(F32)
             total = total + product[m * run : (m + 1) * run, lane : lane + LANES] * held
         partial[m * run : (m + 1) * run, :] = total
-    lane = iota((capacity, LANES), 1)
-    for j, row, slot in places:
-        parts = split(jnp.sum(partial[pl.ds(slot, capacity), :], axis=1, keepdims=True))
-        table = scale_ref[j, row : row + capacity, :]
-        for i, part in enumerate(parts):
+    lane = iota((size, LANES), 1)
+    for j in range(half):
+        slots = [slot for which, _, slot in places if which == j]
+        sums = jnp.concatenate([partial[pl.ds(slot, capacity), :] for slot in slots], axis=0)
+        table = scale_ref[j]
+        for i, part in enumerate(split(jnp.sum(sums, axis=1, keepdims=True))):
             table = jnp.where(lane == i, part, table)
-        grads[j][row : row + capacity, :] = table.astype(BF16)
+        grads[j][...] = table.astype(BF16)
 
 
 def own_expert(me, blocks, weight, saved, scales, half, capacity):
@@ -242,17 +249,16 @@
     )(me, *[blocks[j] for j in OWN_ORDER], weight, saved, scales)
 
 
-def router_rows(half, capacity, turn, me, info_ref, own, far_ref, router_ref):
+def router_rows(half, capacity, turn, me, info_ref, own, far_ref, rank, table_ref):
     info = info_ref[...]
     relative = jnp.bitwise_xor(me, iota((8, LANES), 0))
-    rank, _ = ranks(info, relative)
     slot = iota((capacity, LANES), 0)
     token = iota((capacity, LANES), 1)
     far = far_ref[...].astype(F32)
     rows = []
     for j in range(2 * half):
         if j < half:
-            table, lane = own[j].astype(F32), 0
+            table, lane = own[j], 0
         else:
             table, lane = far, 3 * ((j - half) ^ turn)
         column = table[:, lane : lane + 1] + table[:, lane + 1 : lane + 2] + table[:, lane + 2 : lane + 3]
@@ -268,38 +274,39 @@
     logit = jnp.where(expert_rows == first, w_first * (g_first - mean), 0.0)
     logit = logit + jnp.where(expert_rows == second, w_second * (g_second - mean), 0.0)
     parts = jnp.concatenate([*split(logit), jnp.zeros((LANES - 24, LANES), F32)], axis=0).T
-    router = router_ref[...].astype(F32)
-    router = jnp.concatenate([router, router, router, jnp.zeros((LANES - 24, router.shape[1]), F32)], axis=0)
-    return jnp.dot(parts.astype(BF16), router.astype(BF16), preferred_element_type=F32).astype(BF16)
+    return jnp.dot(parts.astype(BF16), table_ref[...], preferred_element_type=F32).astype(BF16)
 
 
 def last_kernel(half, capacity, turn, me_ref, *refs):
     blocks, refs = [refs[FAR_ORDER.index(j)] for j in range(half)], refs[half:]
-    w_ref, own_ref, info_ref, far_ref, router_ref, d_ref, out_ref = refs[:7]
-    lhs, product, scale, rows, hidden, row_sem, hidden_sem = refs[7:]
+    w_ref, own_ref, info_ref, far_ref, rank_ref, table_ref, d_ref, out_ref = refs[:8]
+    lhs, product, scale, rows, hidden, row_sem, hidden_sem = refs[8:]
     width, hidden_width = w_ref.shape
     run, size = half * capacity, MICRO * capacity
     me = me_ref[0]
     side = me // half
-    tails = [block[:, width:] for block in blocks]
-    rows[...] = router_rows(half, capacity, turn, me, info_ref, tails, far_ref, router_ref)
+    tails = [block[:, width:].astype(F32) for block in blocks]
+    rows[...] = router_rows(half, capacity, turn, me, info_ref, tails, far_ref, rank_ref[...], table_ref)
     copies = [pltpu.make_async_copy(rows, out_ref, row_sem)]
     copies[0].start()
     here = lax.rem(me, half)
 
-    def scaled(far, source, lane_of, slots):
+    def spread_scale(lane_of, slots):
         for j in range(half):
             for m in range(MICRO):
-                tail = tails[j][m * capacity : (m + 1) * capacity].astype(F32)
+                tail = tails[j][m * capacity : (m + 1) * capacity]
                 column = jnp.broadcast_to(tail[:, lane_of : lane_of + 1], tail.shape)
                 scale[pl.ds(slots[j][m], capacity), :] = column
+
+    def scaled(far, source, columns):
         for m in range(MICRO):
             at = slice(m * run, (m + 1) * run)
-            for lane in range(0, hidden_width, LANES):
+            for lane in range(columns.start, columns.start + columns.size, LANES):
                 lanes = slice(lane, lane + LANES)
                 hidden[far, m, :, lanes] = (scale[at, :] * source[at, lanes]).astype(BF16)
-            to = d_ref.at[m, 1 - side if far else side]
-            copies.append(pltpu.make_async_copy(hidden.at[far, m], to, hidden_sem.at[far, m]))
+            to = d_ref.at[m, 1 - side if far else side, :, columns]
+            part = columns.start // columns.size
+            copies.append(pltpu.make_async_copy(hidden.at[far, m, :, columns], to, hidden_sem.at[far, m, part]))
             copies[-1].start()
 
     def slots_of(first):
@@ -307,8 +314,10 @@
             [pl.multiple_of(m * run + jnp.bitwise_xor(first, j) * capacity, 8) for m in range(MICRO)] for j in range(half)
         ]
 
-    scaled(0, own_ref, SCALE - 1, slots_of(here))
+    spread_scale(SCALE - 1, slots_of(here))
+    scaled(0, own_ref, pl.ds(0, hidden_width))
     far_slots = slots_of(jnp.bitwise_xor(here, turn))
+    spread_scale(SCALE, far_slots)
     for j in range(half):
         lhs[j * size : (j + 1) * size, :] = blocks[j][:, 0:width]
     for columns in chunks(hidden_width):
@@ -317,19 +326,19 @@
             for m in range(MICRO):
                 begin = j * size + m * capacity
                 product[pl.ds(far_slots[j][m], capacity), columns] = got[begin : begin + capacity, :]
-    scaled(1, product, SCALE, far_slots)
+        scaled(1, product, columns)
     for copy in copies:
         copy.wait()
 
 
-def last(me, blocks, weight, own, info, far, table, saved, tokens, half, capacity, turn):
+def last(me, blocks, weight, own, info, far, rank, table, saved, tokens, half, capacity, turn):
     width, hidden_width = weight.shape
     run = half * capacity
     vmem, anywhere = pl.BlockSpec(memory_space=pltpu.VMEM), pl.BlockSpec(memory_space=pl.ANY)
     return pl.pallas_call(
         functools.partial(last_kernel, half, capacity, turn),
         out_shape=[jax.ShapeDtypeStruct(saved.shape, BF16), jax.ShapeDtypeStruct(tokens.shape, BF16)],
-        in_specs=[pl.BlockSpec(memory_space=pltpu.SMEM)] + [vmem] * (half + 5),
+        in_specs=[pl.BlockSpec(memory_space=pltpu.SMEM)] + [vmem] * (half + 6),
         out_specs=[anywhere, anywhere],
         scratch_shapes=[
             pltpu.VMEM((MICRO * run, width), BF16),
@@ -338,11 +347,11 @@
             pltpu.VMEM(tokens.shape, BF16),
             pltpu.VMEM((2, MICRO, run, hidden_width), BF16),
             pltpu.SemaphoreType.DMA,
-            pltpu.SemaphoreType.DMA((2, MICRO)),
+            pltpu.SemaphoreType.DMA((2, MICRO, len(chunks(hidden_width)))),
         ],
         compiler_params=pltpu.CompilerParams(vmem_limit_bytes=VMEM_LIMIT),
         name="last",
-    )(me, *[blocks[j] for j in FAR_ORDER], weight, own, info, far, table)
+    )(me, *[blocks[j] for j in FAR_ORDER], weight, own, info, far, rank, table)
 
 
 def route(block, flip, back):
@@ -377,7 +386,7 @@
     far_info = route(info, half + turn, 0)
     far_tokens = route(tokens, half + turn, 1)
     packed = pack(me, next_info, tokens, half, capacity, "pack_own")
-    weight_t, scales = turned(me, weight, info, packed[0], half, capacity)
+    weight_t, scales, rank, table = turned(me, weight, info, w_router.T, packed[0], half, capacity)
     saved, packed = lax.optimization_barrier((saved, packed))
     backs = back(me, saved, weight, half, capacity, turn)
     own = [route(packed[j], j, 1) for j in range(half)]
@@ -387,7 +396,7 @@
     far_grads = route(far_grad(far, backs, half, capacity), half + turn, 0)
     far = spread(far)
     d_hidden, grad_in = last(
-        me, far, weight_t, own_product, info, far_grads, w_router.T, saved, tokens, half, capacity, turn
+        me, far, weight_t, own_product, info, far_grads, rank, table, saved, tokens, half, capacity, turn
     )
     return d_hidden.reshape(saved_hidden.shape), grad_in[None]
 

time: 47.7 us -> 47.6 us (level)
  transfers between devices with their start and end apart: 14 -> 14, of which waited for: 8 -> 8; matrix products, arithmetic and copies ran while one was open for 0% -> 0% of each run, Pallas kernels for 11% -> 12%
where the time goes in v7:
time: 47.6 us; the launch traced here: 47.3 us
  starting transfers between devices  21.6 us (45%)
  waiting for transfers between devices  13.5 us (28%)
  Pallas kernels  7.53 us (16%)
  local copies, waits for them, and re-layouts  4.01 us (8%)
  between operations  0.71 us (1%)
    ppermute x14, starting transfers between devices, route(): return lax.ppermute(block, ('pipe', 'expert'), pairs)  21.6 us
    ppermute x14, waiting for transfers between devices, route(): return lax.ppermute(block, ('pipe', 'expert'), pairs)  13.5 us
    unnamed x14, local copies, waits for them, and re-layouts  4.01 us
    pallas_call x1, Pallas kernels, last(): pl.pallas_call(functools.partial(last_kernel, half, capacity, turn), out_...  2.05 us
    pallas_call x1, Pallas kernels, by_halves(): pl.pallas_call(info_kernel, out_shape=jax.ShapeDtypeStruct((8, LANES), F3...  1.31 us
    pallas_call x1, Pallas kernels, own_expert(): pl.pallas_call(functools.partial(own_kernel, half, capacity), out_shape=[...  1.01 us
    pallas_call x1, Pallas kernels, turned(): pl.pallas_call(functools.partial(turn_kernel, half, capacity), out_shape=...  0.98 us
    pallas_call x2, Pallas kernels, pack(): pl.pallas_call(functools.partial(pack_kernel, half, capacity), out_shape=...  0.97 us
  transfers between devices with their start and end apart: 14, of which 8 were waited for; matrix products, arithmetic and copies ran while one was open for 0% of the time, Pallas kernels for 12%

profile of v7, /device:TPU:0, one launch (start us, length us, event | category | flops | bytes accessed | tf_op | source)
XLA Modules:
  0.0 47.3 jit_solution(15088234383434956989)
XLA Ops:
  0.6 5.5 %collective-permute-start.1 = (bf16[128,2048]{1,0:T(8,128)(2,1)}, bf16[128,2048]{1,0:T(8,128)(2,1)S(1)}, u32[]{:S(2)}, u32[]{:S(2)}) collective-permute-start(bf16[128,2048]{1,0:T(8,128)(2,1)} %bitcast.17), channel_id=1, source_target_pairs={{0,30},{1,31},{2,28},{3,29},{4,26},{5,27},{6,24},{7,25},{8,6},{9,7... | collective-permute-start | bytes 1572872 | tf_op jit(solution)/shard_map/ppermute | solution.py:362
  6.1 1.3 %info.1.info_ref.refs_6_ = f32[8,128]{1,0:T(8,128)} custom-call(s32[2,128]{1,0:T(2,128)} %bitcast.21, f32[8,128]{1,0:T(8,128)} %bitcast.20), custom_call_target="tpu_custom_call" | custom-call | tf_op jit(solution)/shard_map/info/pallas_call | solution.py:378
  7.4 0.0 copy-start.5
  7.4 0.0 collective-permute-start.2
  7.4 3.3 %collective-permute-done.2.info_ref = f32[8,128]{1,0:T(8,128)S(1)} collective-permute-done((f32[8,128]{1,0:T(8,128)}, f32[8,128]{1,0:T(8,128)S(1)}, u32[]{:S(2)}, u32[]{:S(2)}) %collective-permute-start.2) | collective-permute-done | bytes 4128 | tf_op jit(solution)/shard_map/ppermute | solution.py:362
  10.7 0.0 copy-start.4
  10.7 1.0 %copy-done.4 = bf16[1,128,2048]{2,1,0:T(8,128)(2,1)S(1)} copy-done((bf16[1,128,2048]{2,1,0:T(8,128)(2,1)S(1)}, bf16[1,128,2048]{2,1,0:T(8,128)(2,1)}, u32[]{:S(2)}) %copy-start.4) | copy-done | bytes 524312
  11.8 0.0 copy-start.6
  11.8 0.5 %pack_own.1 = (bf16[48,2048]{1,0:T(8,128)(2,1)S(1)}, bf16[48,2048]{1,0:T(8,128)(2,1)S(1)}, bf16[48,2048]{1,0:T(8,128)(2,1)S(1)}, bf16[48,2048]{1,0:T(8,128)(2,1)S(1)}) custom-call(s32[1]{0:T(128)} %bitcast.me_ref, f32[8,128]{1,0:T(8,128)S(1)} %collective-permute-done.2.info_ref, bf16[128,2048]{1,0:T(8,128)(2,1)S(1)} %bitcast.18), custom_call_target="tpu_custom_call" | custom-call | tf_op jit(solution)/shard_map/pack_own/pallas_call | solution.py:92
  12.3 0.1 collective-permute-start.3
  12.3 1.5 %collective-permute-start.4 = (bf16[48,2048]{1,0:T(8,128)(2,1)S(1)}, bf16[48,2048]{1,0:T(8,128)(2,1)S(1)}, u32[]{:S(2)}, u32[]{:S(2)}) collective-permute-start(bf16[48,2048]{1,0:T(8,128)(2,1)S(1)} %get-tuple-element.35), channel_id=1, source_target_pairs={{0,25},{1,24},{2,27},{3,26},{4,29},{5,28},{6,31},{7,30},{8,1},{9,0... | collective-permute-start | bytes 589832 | tf_op jit(solution)/shard_map/ppermute | solution.py:362
  13.9 0.0 collective-permute-start.5
  13.9 2.7 %collective-permute-start.6 = (bf16[48,2048]{1,0:T(8,128)(2,1)S(1)}, bf16[48,2048]{1,0:T(8,128)(2,1)S(1)}, u32[]{:S(2)}, u32[]{:S(2)}) collective-permute-start(bf16[48,2048]{1,0:T(8,128)(2,1)S(1)} %get-tuple-element.37), channel_id=1, source_target_pairs={{0,27},{1,26},{2,25},{3,24},{4,31},{5,30},{6,29},{7,28},{8,3},{9,2... | collective-permute-start | bytes 589832 | tf_op jit(solution)/shard_map/ppermute | solution.py:362
  16.5 0.0 copy-start
  16.5 1.9 %copy-done = bf16[1,768,2048]{2,1,0:T(8,128)(2,1)S(1)} copy-done((bf16[1,768,2048]{2,1,0:T(8,128)(2,1)S(1)}, bf16[1,768,2048]{2,1,0:T(8,128)(2,1)}, u32[]{:S(2)}) %copy-start) | copy-done | bytes 3145752
  18.4 0.0 copy-start.2
  18.4 1.1 %copy-done.2 = bf16[1,384,768]{2,1,0:T(8,128)(2,1)S(1)} copy-done((bf16[1,384,768]{2,1,0:T(8,128)(2,1)S(1)}, bf16[1,384,768]{2,1,0:T(8,128)(2,1)}, u32[]{:S(2)}) %copy-start.2) | copy-done | bytes 589848
  19.5 0.0 copy-start.1
  19.5 0.0 copy-start.3
  19.5 0.9 %back.1 = (bf16[48,2048]{1,0:T(8,128)(2,1)S(1)}, bf16[48,2048]{1,0:T(8,128)(2,1)S(1)}, bf16[48,2048]{1,0:T(8,128)(2,1)S(1)}, bf16[48,2048]{1,0:T(8,128)(2,1)S(1)}) custom-call(s32[1]{0:T(128)} %bitcast.me_ref, bf16[2,2,96,768]{3,2,1,0:T(8,128)(2,1)S(1)} %bitcast.15, bf16[768,2048]{1,0:T(8,128)(2,1)S(1)} %bitcast.13), custom_call_target="tpu_custom_call" | custom-call | tf_op jit(solution)/shard_map/back/pallas_call | solution.py:123
  20.4 1.8 %collective-permute-done.3.refs_0_ = bf16[48,2048]{1,0:T(8,128)(2,1)S(1)} collective-permute-done((bf16[48,2048]{1,0:T(8,128)(2,1)S(1)}, bf16[48,2048]{1,0:T(8,128)(2,1)S(1)}, u32[]{:S(2)}, u32[]{:S(2)}) %collective-permute-start.3) | collective-permute-done | bytes 196640 | tf_op jit(solution)/shard_map/ppermute | solution.py:362
  22.2 0.0 collective-permute-start.10
  22.2 0.0 collective-permute-done.4.refs_1_
  22.2 0.0 copy-done.5
  22.2 0.6 %collective-permute-start = (f32[8,128]{1,0:T(8,128)S(1)}, f32[8,128]{1,0:T(8,128)S(1)}, u32[]{:S(2)}, u32[]{:S(2)}) collective-permute-start(f32[8,128]{1,0:T(8,128)S(1)} %copy-done.5), channel_id=1, source_target_pairs={{0,6},{1,7},{2,4},{3,5},{4,2},{5,3},{6,0},{7,1},{8,14},{9,15},{10,... | collective-permute-start | bytes 12296 | tf_op jit(solution)/shard_map/ppermute | solution.py:362
  22.9 0.0 copy-done.6
  22.9 0.0 copy-done.1
  22.9 1.0 %turned.1 = (bf16[2048,768]{1,0:T(8,128)(2,1)S(1)}, f32[4,48,128]{2,1,0:T(8,128)S(1)}, s32[8,128]{1,0:T(8,128)S(1)}, bf16[128,2048]{1,0:T(8,128)(2,1)S(1)}) custom-call(s32[1]{0:T(128)} %bitcast.me_ref, bf16[768,2048]{1,0:T(8,128)(2,1)S(1)} %bitcast.14, f32[8,128]{1,0:T(8,128)S(1)} %copy-done.5, bf16[8,2048]{1,0:T(8,128)(2,1)S(1)} %bitcast.19, ...), custom_call_target="tpu_custom_call" | custom-call | tf_op jit(solution)/shard_map/turned/pallas_call | solution.py:158
  23.9 0.0 collective-permute-done.5.refs_2_
  23.9 3.0 %collective-permute-start.11 = (bf16[48,2048]{1,0:T(8,128)(2,1)S(1)}, bf16[48,2048]{1,0:T(8,128)(2,1)S(1)}, u32[]{:S(2)}, u32[]{:S(2)}) collective-permute-start(bf16[48,2048]{1,0:T(8,128)(2,1)S(1)} %get-tuple-element.52), channel_id=1, source_target_pairs={{0,2},{1,3},{2,0},{3,1},{4,6},{5,7},{6,4},{7,5},{8,10},{9,11},{10,... | collective-permute-start | bytes 589832 | tf_op jit(solution)/shard_map/ppermute | solution.py:362
  26.9 0.9 %collective-permute-done.6.refs_3_ = bf16[48,2048]{1,0:T(8,128)(2,1)S(1)} collective-permute-done((bf16[48,2048]{1,0:T(8,128)(2,1)S(1)}, bf16[48,2048]{1,0:T(8,128)(2,1)S(1)}, u32[]{:S(2)}, u32[]{:S(2)}) %collective-permute-start.6) | collective-permute-done | bytes 196640 | tf_op jit(solution)/shard_map/ppermute | solution.py:362
  27.8 0.8 %collective-permute-start.12 = (bf16[48,2048]{1,0:T(8,128)(2,1)S(1)}, bf16[48,2048]{1,0:T(8,128)(2,1)S(1)}, u32[]{:S(2)}, u32[]{:S(2)}) collective-permute-start(bf16[48,2048]{1,0:T(8,128)(2,1)S(1)} %get-tuple-element.53), channel_id=1, source_target_pairs={{0,1},{1,0},{2,3},{3,2},{4,5},{5,4},{6,7},{7,6},{8,9},{9,8},{10,11... | collective-permute-start | bytes 589832 | tf_op jit(solution)/shard_map/ppermute | solution.py:362
  28.6 0.0 copy-done.3
  28.6 1.0 %own_expert.1 = (f32[192,768]{1,0:T(8,128)S(1)}, bf16[48,128]{1,0:T(8,128)(2,1)S(1)}, bf16[48,128]{1,0:T(8,128)(2,1)S(1)}, bf16[48,128]{1,0:T(8,128)(2,1)S(1)}, bf16[48,128]{1,0:T(8,128)(2,1)S(1)}) custom-call(s32[1]{0:T(128)} %bitcast.me_ref, bf16[48,2048]{1,0:T(8,128)(2,1)S(1)} %collective-permute-done.3.refs_0_, ...), custom_call_target="tpu_custom_call" | custom-call | tf_op jit(solution)/shard_map/own_expert/pallas_call | solution.py:240
  29.7 1.8 %collective-permute-done.info_ref = f32[8,128]{1,0:T(8,128)S(1)} collective-permute-done((f32[8,128]{1,0:T(8,128)S(1)}, f32[8,128]{1,0:T(8,128)S(1)}, u32[]{:S(2)}, u32[]{:S(2)}) %collective-permute-start) | collective-permute-done | bytes 4128 | tf_op jit(solution)/shard_map/ppermute | solution.py:362
  31.5 0.0 collective-permute-done.1.token_ref
  31.5 0.5 %pack_far.1 = (bf16[48,2176]{1,0:T(8,128)(2,1)S(1)}, bf16[48,2176]{1,0:T(8,128)(2,1)S(1)}, bf16[48,2176]{1,0:T(8,128)(2,1)S(1)}, bf16[48,2176]{1,0:T(8,128)(2,1)S(1)}) custom-call(s32[1]{0:T(128)} %bitcast.me_ref, f32[8,128]{1,0:T(8,128)S(1)} %collective-permute-done.info_ref, bf16[128,2048]{1,0:T(8,128)(2,1)S(1)} %collective-permute-done.1.token_ref, ...), custom_call_target="tpu_custom_call" | custom-call | tf_op jit(solution)/shard_map/pack_far/pallas_call | solution.py:92
  32.0 0.1 collective-permute-start.7
  32.0 3.6 %collective-permute-start.8 = (bf16[48,2176]{1,0:T(8,128)(2,1)S(1)}, bf16[48,2176]{1,0:T(8,128)(2,1)S(1)}, u32[]{:S(2)}, u32[]{:S(2)}) collective-permute-start(bf16[48,2176]{1,0:T(8,128)(2,1)S(1)} %get-tuple-element.47.refs_2_), channel_id=1, source_target_pairs={{0,2},{1,3},{2,0},{3,1},{4,6},{5,7},{6,4},{7,5},{8,10},{9,11},{10,... | collective-permute-start | bytes 626696 | tf_op jit(solution)/shard_map/ppermute | solution.py:362
  35.6 0.0 collective-permute-done.10.refs_5_
  35.6 0.0 collective-permute-start.9
  35.6 0.2 collective-permute-done.11.refs_6_
  35.8 0.5 %collective-permute-done.12.refs_7_ = bf16[48,2048]{1,0:T(8,128)(2,1)S(1)} collective-permute-done((bf16[48,2048]{1,0:T(8,128)(2,1)S(1)}, bf16[48,2048]{1,0:T(8,128)(2,1)S(1)}, u32[]{:S(2)}, u32[]{:S(2)}) %collective-permute-start.12) | collective-permute-done | bytes 196640 | tf_op jit(solution)/shard_map/ppermute | solution.py:362
  36.3 0.3 far_grad.1
  36.6 3.7 %collective-permute-start.13 = (bf16[48,128]{1,0:T(8,128)(2,1)S(1)}, bf16[48,128]{1,0:T(8,128)(2,1)S(1)}, u32[]{:S(2)}, u32[]{:S(2)}) collective-permute-start(bf16[48,128]{1,0:T(8,128)(2,1)S(1)} %far_grad.1), channel_id=1, source_target_pairs={{0,6},{1,7},{2,4},{3,5},{4,2},{5,3},{6,0},{7,1},{8,14},{9,15},{10,... | collective-permute-start | bytes 36872 | tf_op jit(solution)/shard_map/ppermute | solution.py:362
  40.3 4.2 %collective-permute-done.13.refs_7_ = bf16[48,128]{1,0:T(8,128)(2,1)S(1)} collective-permute-done((bf16[48,128]{1,0:T(8,128)(2,1)S(1)}, bf16[48,128]{1,0:T(8,128)(2,1)S(1)}, u32[]{:S(2)}, u32[]{:S(2)}) %collective-permute-start.13) | collective-permute-done | bytes 12320 | tf_op jit(solution)/shard_map/ppermute | solution.py:362
  44.4 0.0 collective-permute-done.7.refs_1_
  44.4 0.0 collective-permute-done.8.refs_2_
  44.4 0.8 %collective-permute-done.9.refs_3_ = bf16[48,2176]{1,0:T(8,128)(2,1)S(1)} collective-permute-done((bf16[48,2176]{1,0:T(8,128)(2,1)S(1)}, bf16[48,2176]{1,0:T(8,128)(2,1)S(1)}, u32[]{:S(2)}, u32[]{:S(2)}) %collective-permute-start.9) | collective-permute-done | bytes 208928 | tf_op jit(solution)/shard_map/ppermute | solution.py:362
  45.2 2.1 %last.1 = (bf16[2,2,96,768]{3,2,1,0:T(8,128)(2,1)}, bf16[128,2048]{1,0:T(8,128)(2,1)}) custom-call(s32[1]{0:T(128)} %bitcast.me_ref, bf16[48,2176]{1,0:T(8,128)(2,1)S(1)} %get-tuple-element.45.refs_0_, bf16[48,2176]{1,0:T(8,128)(2,1)S(1)} %collective-permute-done.7.refs_1_, bf16[48,2176]{1,0:T(8,128)(2,1)S(1)} %collective-permute-done.8.refs_2_, ...), custom_call_target="tpu_custom_call" | custom-call | tf_op jit(solution)/shard_map/last/pallas_call | solution.py:338
Async XLA Ops:
  0.6 30.8 %collective-permute-start.1 = (bf16[128,2048]{1,0:T(8,128)(2,1)}, bf16[128,2048]{1,0:T(8,128)(2,1)S(1)}, u32[]{:S(2)}, u32[]{:S(2)}) collective-permute-start(bf16[128,2048]{1,0:T(8,128)(2,1)} %bitcast.17), channel_id=1, source_target_pairs={{0,30},{1,31},{2,28},{3,29},{4,26},{5,27},{6,24},{7,25},{8,6},{9,7... | collective-permute-start | bytes 1572872 | tf_op jit(solution)/shard_map/ppermute | solution.py:362
  7.4 14.8 %copy-start.5 = (f32[8,128]{1,0:T(8,128)S(1)}, f32[8,128]{1,0:T(8,128)}, u32[]{:S(2)}) copy-start(f32[8,128]{1,0:T(8,128)} %info.1.info_ref.refs_6_) | copy-start | bytes 12292
  7.4 3.3 %collective-permute-start.2 = (f32[8,128]{1,0:T(8,128)}, f32[8,128]{1,0:T(8,128)S(1)}, u32[]{:S(2)}, u32[]{:S(2)}) collective-permute-start(f32[8,128]{1,0:T(8,128)} %info.1.info_ref.refs_6_), channel_id=1, source_target_pairs={{0,8},{1,9},{2,10},{3,11},{4,12},{5,13},{6,14},{7,15},{8,16},{9,17... | collective-permute-start | bytes 12296 | tf_op jit(solution)/shard_map/ppermute | solution.py:362
  10.7 1.0 %copy-start.4 = (bf16[1,128,2048]{2,1,0:T(8,128)(2,1)S(1)}, bf16[1,128,2048]{2,1,0:T(8,128)(2,1)}, u32[]{:S(2)}) copy-start(bf16[1,128,2048]{2,1,0:T(8,128)(2,1)} %param.6) | copy-start | bytes 1572868
  11.8 11.1 %copy-start.6 = (bf16[2048,8]{0,1:T(8,128)(2,1)S(1)}, bf16[2048,8]{0,1:T(8,128)(2,1)}, u32[]{:S(2)}) copy-start(bf16[2048,8]{0,1:T(8,128)(2,1)} %param.11) | copy-start | bytes 98308
  12.3 10.0 %collective-permute-start.3 = (bf16[48,2048]{1,0:T(8,128)(2,1)S(1)}, bf16[48,2048]{1,0:T(8,128)(2,1)S(1)}, u32[]{:S(2)}, u32[]{:S(2)}) collective-permute-start(bf16[48,2048]{1,0:T(8,128)(2,1)S(1)} %get-tuple-element.34.after_ref), channel_id=1, source_target_pairs={{0,24},{1,25},{2,26},{3,27},{4,28},{5,29},{6,30},{7,31},{8,0},{9,1... | collective-permute-start | bytes 589832 | tf_op jit(solution)/shard_map/ppermute | solution.py:362
  12.3 9.9 %collective-permute-start.4 = (bf16[48,2048]{1,0:T(8,128)(2,1)S(1)}, bf16[48,2048]{1,0:T(8,128)(2,1)S(1)}, u32[]{:S(2)}, u32[]{:S(2)}) collective-permute-start(bf16[48,2048]{1,0:T(8,128)(2,1)S(1)} %get-tuple-element.35), channel_id=1, source_target_pairs={{0,25},{1,24},{2,27},{3,26},{4,29},{5,28},{6,31},{7,30},{8,1},{9,0... | collective-permute-start | bytes 589832 | tf_op jit(solution)/shard_map/ppermute | solution.py:362
  13.9 10.0 %collective-permute-start.5 = (bf16[48,2048]{1,0:T(8,128)(2,1)S(1)}, bf16[48,2048]{1,0:T(8,128)(2,1)S(1)}, u32[]{:S(2)}, u32[]{:S(2)}) collective-permute-start(bf16[48,2048]{1,0:T(8,128)(2,1)S(1)} %get-tuple-element.36), channel_id=1, source_target_pairs={{0,26},{1,27},{2,24},{3,25},{4,30},{5,31},{6,28},{7,29},{8,2},{9,3... | collective-permute-start | bytes 589832 | tf_op jit(solution)/shard_map/ppermute | solution.py:362
  13.9 13.9 %collective-permute-start.6 = (bf16[48,2048]{1,0:T(8,128)(2,1)S(1)}, bf16[48,2048]{1,0:T(8,128)(2,1)S(1)}, u32[]{:S(2)}, u32[]{:S(2)}) collective-permute-start(bf16[48,2048]{1,0:T(8,128)(2,1)S(1)} %get-tuple-element.37), channel_id=1, source_target_pairs={{0,27},{1,26},{2,25},{3,24},{4,31},{5,30},{6,29},{7,28},{8,3},{9,2... | collective-permute-start | bytes 589832 | tf_op jit(solution)/shard_map/ppermute | solution.py:362
  16.5 1.9 %copy-start = (bf16[1,768,2048]{2,1,0:T(8,128)(2,1)S(1)}, bf16[1,768,2048]{2,1,0:T(8,128)(2,1)}, u32[]{:S(2)}) copy-start(bf16[1,768,2048]{2,1,0:T(8,128)(2,1)} %param.10) | copy-start | bytes 9437188
  18.4 1.1 %copy-start.2 = (bf16[1,384,768]{2,1,0:T(8,128)(2,1)S(1)}, bf16[1,384,768]{2,1,0:T(8,128)(2,1)}, u32[]{:S(2)}) copy-start(bf16[1,384,768]{2,1,0:T(8,128)(2,1)} %param.9) | copy-start | bytes 1769476
  19.5 3.4 %copy-start.1 = (bf16[1,768,2048]{2,1,0:T(8,128)(2,1)S(1)}, bf16[1,768,2048]{2,1,0:T(8,128)(2,1)}, u32[]{:S(2)}) copy-start(bf16[1,768,2048]{2,1,0:T(8,128)(2,1)} %param.10) | copy-start | bytes 9437188
  19.5 9.2 %copy-start.3 = (bf16[1,384,768]{2,1,0:T(8,128)(2,1)S(1)}, bf16[1,384,768]{2,1,0:T(8,128)(2,1)}, u32[]{:S(2)}) copy-start(bf16[1,384,768]{2,1,0:T(8,128)(2,1)} %param.9) | copy-start | bytes 1769476
  22.2 13.4 %collective-permute-start.10 = (bf16[48,2048]{1,0:T(8,128)(2,1)S(1)}, bf16[48,2048]{1,0:T(8,128)(2,1)S(1)}, u32[]{:S(2)}, u32[]{:S(2)}) collective-permute-start(bf16[48,2048]{1,0:T(8,128)(2,1)S(1)} %get-tuple-element.51), channel_id=1, source_target_pairs={{0,3},{1,2},{2,1},{3,0},{4,7},{5,6},{6,5},{7,4},{8,11},{9,10},{10,... | collective-permute-start | bytes 589832 | tf_op jit(solution)/shard_map/ppermute | solution.py:362
  22.2 9.2 %collective-permute-start = (f32[8,128]{1,0:T(8,128)S(1)}, f32[8,128]{1,0:T(8,128)S(1)}, u32[]{:S(2)}, u32[]{:S(2)}) collective-permute-start(f32[8,128]{1,0:T(8,128)S(1)} %copy-done.5), channel_id=1, source_target_pairs={{0,6},{1,7},{2,4},{3,5},{4,2},{5,3},{6,0},{7,1},{8,14},{9,15},{10,... | collective-permute-start | bytes 12296 | tf_op jit(solution)/shard_map/ppermute | solution.py:362
  23.9 11.9 %collective-permute-start.11 = (bf16[48,2048]{1,0:T(8,128)(2,1)S(1)}, bf16[48,2048]{1,0:T(8,128)(2,1)S(1)}, u32[]{:S(2)}, u32[]{:S(2)}) collective-permute-start(bf16[48,2048]{1,0:T(8,128)(2,1)S(1)} %get-tuple-element.52), channel_id=1, source_target_pairs={{0,2},{1,3},{2,0},{3,1},{4,6},{5,7},{6,4},{7,5},{8,10},{9,11},{10,... | collective-permute-start | bytes 589832 | tf_op jit(solution)/shard_map/ppermute | solution.py:362
  27.8 8.5 %collective-permute-start.12 = (bf16[48,2048]{1,0:T(8,128)(2,1)S(1)}, bf16[48,2048]{1,0:T(8,128)(2,1)S(1)}, u32[]{:S(2)}, u32[]{:S(2)}) collective-permute-start(bf16[48,2048]{1,0:T(8,128)(2,1)S(1)} %get-tuple-element.53), channel_id=1, source_target_pairs={{0,1},{1,0},{2,3},{3,2},{4,5},{5,4},{6,7},{7,6},{8,9},{9,8},{10,11... | collective-permute-start | bytes 589832 | tf_op jit(solution)/shard_map/ppermute | solution.py:362
  32.0 12.5 %collective-permute-start.7 = (bf16[48,2176]{1,0:T(8,128)(2,1)S(1)}, bf16[48,2176]{1,0:T(8,128)(2,1)S(1)}, u32[]{:S(2)}, u32[]{:S(2)}) collective-permute-start(bf16[48,2176]{1,0:T(8,128)(2,1)S(1)} %get-tuple-element.46.refs_3_), channel_id=1, source_target_pairs={{0,3},{1,2},{2,1},{3,0},{4,7},{5,6},{6,5},{7,4},{8,11},{9,10},{10,... | collective-permute-start | bytes 626696 | tf_op jit(solution)/shard_map/ppermute | solution.py:362
  32.0 12.4 %collective-permute-start.8 = (bf16[48,2176]{1,0:T(8,128)(2,1)S(1)}, bf16[48,2176]{1,0:T(8,128)(2,1)S(1)}, u32[]{:S(2)}, u32[]{:S(2)}) collective-permute-start(bf16[48,2176]{1,0:T(8,128)(2,1)S(1)} %get-tuple-element.47.refs_2_), channel_id=1, source_target_pairs={{0,2},{1,3},{2,0},{3,1},{4,6},{5,7},{6,4},{7,5},{8,10},{9,11},{10,... | collective-permute-start | bytes 626696 | tf_op jit(solution)/shard_map/ppermute | solution.py:362
  35.6 9.6 %collective-permute-start.9 = (bf16[48,2176]{1,0:T(8,128)(2,1)S(1)}, bf16[48,2176]{1,0:T(8,128)(2,1)S(1)}, u32[]{:S(2)}, u32[]{:S(2)}) collective-permute-start(bf16[48,2176]{1,0:T(8,128)(2,1)S(1)} %get-tuple-element.48.refs_1_), channel_id=1, source_target_pairs={{0,1},{1,0},{2,3},{3,2},{4,5},{5,4},{6,7},{7,6},{8,9},{9,8},{10,11... | collective-permute-start | bytes 626696 | tf_op jit(solution)/shard_map/ppermute | solution.py:362
  36.6 7.8 %collective-permute-start.13 = (bf16[48,128]{1,0:T(8,128)(2,1)S(1)}, bf16[48,128]{1,0:T(8,128)(2,1)S(1)}, u32[]{:S(2)}, u32[]{:S(2)}) collective-permute-start(bf16[48,128]{1,0:T(8,128)(2,1)S(1)} %far_grad.1), channel_id=1, source_target_pairs={{0,6},{1,7},{2,4},{3,5},{4,2},{5,3},{6,0},{7,1},{8,14},{9,15},{10,... | collective-permute-start | bytes 36872 | tf_op jit(solution)/shard_map/ppermute | solution.py:362

commit v8 on v7

--- a/solution.py
+++ b/solution.py
@@ -202,19 +202,19 @@
 def own_kernel(half, capacity, me_ref, *refs):
     blocks, refs = [refs[OWN_ORDER.index(j)] for j in range(half)], refs[half:]
     w_ref, saved_ref, scale_ref, product, grads = refs[0], refs[1], refs[2], refs[3], refs[4 : 4 + half]
-    lhs, partial = refs[4 + half :]
+    (partial,) = refs[4 + half :]
     hidden_width = w_ref.shape[1]
     run, size = half * capacity, MICRO * capacity
     me = me_ref[0]
     here, side = lax.rem(me, half), me // half
     places = []
     for j in range(half):
-        lhs[j * size : (j + 1) * size, :] = blocks[j][...]
         for m in range(MICRO):
             slot = pl.multiple_of(m * run + jnp.bitwise_xor(here, j) * capacity, 8)
             places.append((j, m * capacity, slot))
+    sent = jnp.concatenate([block[...] for block in blocks], axis=0)
     for columns in chunks(hidden_width):
-        got = jnp.dot(lhs[...], w_ref[:, columns], preferred_element_type=F32)
+        got = jnp.dot(sent, w_ref[:, columns], preferred_element_type=F32)
         for j, row, slot in places:
             product[pl.ds(slot, capacity), columns] = got[j * size + row : j * size + row + capacity, :]
     for m in range(MICRO):
@@ -234,7 +234,7 @@
 
 
 def own_expert(me, blocks, weight, saved, scales, half, capacity):
-    width, hidden_width = weight.shape
+    hidden_width = weight.shape[1]
     rows = MICRO * capacity
     vmem = pl.BlockSpec(memory_space=pltpu.VMEM)
     return pl.pallas_call(
@@ -243,7 +243,7 @@
         + [jax.ShapeDtypeStruct((rows, LANES), BF16)] * half,
         in_specs=[pl.BlockSpec(memory_space=pltpu.SMEM)] + [vmem] * (half + 3),
         out_specs=[vmem] * (1 + half),
-        scratch_shapes=[pltpu.VMEM((half * rows, width), BF16), pltpu.VMEM((half * rows, LANES), F32)],
+        scratch_shapes=[pltpu.VMEM((half * rows, LANES), F32)],
         compiler_params=pltpu.CompilerParams(vmem_limit_bytes=VMEM_LIMIT),
         name="own_expert",
     )(me, *[blocks[j] for j in OWN_ORDER], weight, saved, scales)
@@ -280,7 +280,7 @@
 def last_kernel(half, capacity, turn, me_ref, *refs):
     blocks, refs = [refs[FAR_ORDER.index(j)] for j in range(half)], refs[half:]
     w_ref, own_ref, info_ref, far_ref, rank_ref, table_ref, d_ref, out_ref = refs[:8]
-    lhs, product, scale, rows, hidden, row_sem, hidden_sem = refs[8:]
+    product, scale, rows, hidden, row_sem, hidden_sem = refs[8:]
     width, hidden_width = w_ref.shape
     run, size = half * capacity, MICRO * capacity
     me = me_ref[0]
@@ -318,10 +318,9 @@
     scaled(0, own_ref, pl.ds(0, hidden_width))
     far_slots = slots_of(jnp.bitwise_xor(here, turn))
     spread_scale(SCALE, far_slots)
-    for j in range(half):
-        lhs[j * size : (j + 1) * size, :] = blocks[j][:, 0:width]
+    sent = jnp.concatenate([block[:, 0:width] for block in blocks], axis=0)
     for columns in chunks(hidden_width):
-        got = jnp.dot(lhs[...], w_ref[:, columns], preferred_element_type=F32)
+        got = jnp.dot(sent, w_ref[:, columns], preferred_element_type=F32)
         for j in range(half):
             for m in range(MICRO):
                 begin = j * size + m * capacity
@@ -332,7 +331,7 @@
 
 
 def last(me, blocks, weight, own, info, far, rank, table, saved, tokens, half, capacity, turn):
-    width, hidden_width = weight.shape
+    hidden_width = weight.shape[1]
     run = half * capacity
     vmem, anywhere = pl.BlockSpec(memory_space=pltpu.VMEM), pl.BlockSpec(memory_space=pl.ANY)
     return pl.pallas_call(
@@ -341,7 +340,6 @@
         in_specs=[pl.BlockSpec(memory_space=pltpu.SMEM)] + [vmem] * (half + 6),
         out_specs=[anywhere, anywhere],
         scratch_shapes=[
-            pltpu.VMEM((MICRO * run, width), BF16),
             pltpu.VMEM((MICRO * run, hidden_width), F32),
             pltpu.VMEM((MICRO * run, LANES), F32),
             pltpu.VMEM(tokens.shape, BF16),
@@ -390,6 +388,7 @@
     saved, packed = lax.optimization_barrier((saved, packed))
     backs = back(me, saved, weight, half, capacity, turn)
     own = [route(packed[j], j, 1) for j in range(half)]
+    backs, weight_t = lax.optimization_barrier((backs, weight_t))
     backs = spread(backs)
     own_product, *own_grads = own_expert(me, own, weight_t, saved, scales, half, capacity)
     far = pack(me, far_info, far_tokens, half, capacity, "pack_far", own_grads)

time: 47.6 us -> 47.6 us (level)
  local copies, waits for them, and re-layouts: 4.01 us -> 4.97 us
  waiting for transfers between devices: 13.5 us -> 12.7 us
    unnamed x14, local copies, waits for them, and re-layouts: 4.01 us -> 4.97 us
    ppermute x14, waiting for transfers between devices: 13.5 us -> 12.7 us  [route(): return lax.ppermute(block, ('pipe', 'expert'), pairs)]
  transfers between devices with their start and end apart: 14 -> 14, of which waited for: 8 -> 6; matrix products, arithmetic and copies ran while one was open for 0% -> 0% of each run, Pallas kernels for 12% -> 12%
where the time goes in v8:
time: 47.6 us; the launch traced here: 47.3 us
  starting transfers between devices  21.3 us (45%)
  waiting for transfers between devices  12.7 us (27%)
  Pallas kernels  7.53 us (16%)
  local copies, waits for them, and re-layouts  4.97 us (10%)
  between operations  0.72 us (2%)
    ppermute x14, starting transfers between devices, route(): return lax.ppermute(block, ('pipe', 'expert'), pairs)  21.3 us
    ppermute x14, waiting for transfers between devices, route(): return lax.ppermute(block, ('pipe', 'expert'), pairs)  12.7 us
    unnamed x14, local copies, waits for them, and re-layouts  4.97 us
    pallas_call x1, Pallas kernels, last(): pl.pallas_call(functools.partial(last_kernel, half, capacity, turn), out_...  2.05 us
    pallas_call x1, Pallas kernels, by_halves(): pl.pallas_call(info_kernel, out_shape=jax.ShapeDtypeStruct((8, LANES), F3...  1.31 us
    pallas_call x1, Pallas kernels, own_expert(): pl.pallas_call(functools.partial(own_kernel, half, capacity), out_shape=[...  1.01 us
    pallas_call x1, Pallas kernels, turned(): pl.pallas_call(functools.partial(turn_kernel, half, capacity), out_shape=...  0.98 us
    pallas_call x2, Pallas kernels, pack(): pl.pallas_call(functools.partial(pack_kernel, half, capacity), out_shape=...  0.97 us
  transfers between devices with their start and end apart: 14, of which 6 were waited for; matrix products, arithmetic and copies ran while one was open for 0% of the time, Pallas kernels for 12%

profile of v8, /device:TPU:0, one launch (start us, length us, event | category | flops | bytes accessed | tf_op | source)
XLA Modules:
  0.0 47.3 jit_solution(4197714410036328516)
XLA Ops:
  0.6 5.5 %collective-permute-start.1 = (bf16[128,2048]{1,0:T(8,128)(2,1)}, bf16[128,2048]{1,0:T(8,128)(2,1)S(1)}, u32[]{:S(2)}, u32[]{:S(2)}) collective-permute-start(bf16[128,2048]{1,0:T(8,128)(2,1)} %bitcast.17), channel_id=1, source_target_pairs={{0,30},{1,31},{2,28},{3,29},{4,26},{5,27},{6,24},{7,25},{8,6},{9,7... | collective-permute-start | bytes 1572872 | tf_op jit(solution)/shard_map/ppermute | solution.py:360
  6.1 1.3 %info.1.info_ref.refs_6_ = f32[8,128]{1,0:T(8,128)} custom-call(s32[2,128]{1,0:T(2,128)} %bitcast.21, f32[8,128]{1,0:T(8,128)} %bitcast.20), custom_call_target="tpu_custom_call" | custom-call | tf_op jit(solution)/shard_map/info/pallas_call | solution.py:376
  7.4 0.0 copy-start.5
  7.4 0.0 collective-permute-start.2
  7.4 3.3 %collective-permute-done.2.info_ref = f32[8,128]{1,0:T(8,128)S(1)} collective-permute-done((f32[8,128]{1,0:T(8,128)}, f32[8,128]{1,0:T(8,128)S(1)}, u32[]{:S(2)}, u32[]{:S(2)}) %collective-permute-start.2) | collective-permute-done | bytes 4128 | tf_op jit(solution)/shard_map/ppermute | solution.py:360
  10.7 0.0 copy-start.4
  10.7 1.0 %copy-done.4 = bf16[1,128,2048]{2,1,0:T(8,128)(2,1)S(1)} copy-done((bf16[1,128,2048]{2,1,0:T(8,128)(2,1)S(1)}, bf16[1,128,2048]{2,1,0:T(8,128)(2,1)}, u32[]{:S(2)}) %copy-start.4) | copy-done | bytes 524312
  11.8 0.0 copy-start.6
  11.8 0.5 %pack_own.1 = (bf16[48,2048]{1,0:T(8,128)(2,1)S(1)}, bf16[48,2048]{1,0:T(8,128)(2,1)S(1)}, bf16[48,2048]{1,0:T(8,128)(2,1)S(1)}, bf16[48,2048]{1,0:T(8,128)(2,1)S(1)}) custom-call(s32[1]{0:T(128)} %bitcast.me_ref, f32[8,128]{1,0:T(8,128)S(1)} %collective-permute-done.2.info_ref, bf16[128,2048]{1,0:T(8,128)(2,1)S(1)} %bitcast.18), custom_call_target="tpu_custom_call" | custom-call | tf_op jit(solution)/shard_map/pack_own/pallas_call | solution.py:92
  12.3 0.1 collective-permute-start.3
  12.3 1.5 %collective-permute-start.4 = (bf16[48,2048]{1,0:T(8,128)(2,1)S(1)}, bf16[48,2048]{1,0:T(8,128)(2,1)S(1)}, u32[]{:S(2)}, u32[]{:S(2)}) collective-permute-start(bf16[48,2048]{1,0:T(8,128)(2,1)S(1)} %get-tuple-element.40), channel_id=1, source_target_pairs={{0,25},{1,24},{2,27},{3,26},{4,29},{5,28},{6,31},{7,30},{8,1},{9,0... | collective-permute-start | bytes 589832 | tf_op jit(solution)/shard_map/ppermute | solution.py:360
  13.9 0.0 collective-permute-start.5
  13.9 2.7 %collective-permute-start.6 = (bf16[48,2048]{1,0:T(8,128)(2,1)S(1)}, bf16[48,2048]{1,0:T(8,128)(2,1)S(1)}, u32[]{:S(2)}, u32[]{:S(2)}) collective-permute-start(bf16[48,2048]{1,0:T(8,128)(2,1)S(1)} %get-tuple-element.42), channel_id=1, source_target_pairs={{0,27},{1,26},{2,25},{3,24},{4,31},{5,30},{6,29},{7,28},{8,3},{9,2... | collective-permute-start | bytes 589832 | tf_op jit(solution)/shard_map/ppermute | solution.py:360
  16.5 0.0 copy-start
  16.5 1.9 %copy-done = bf16[1,768,2048]{2,1,0:T(8,128)(2,1)S(1)} copy-done((bf16[1,768,2048]{2,1,0:T(8,128)(2,1)S(1)}, bf16[1,768,2048]{2,1,0:T(8,128)(2,1)}, u32[]{:S(2)}) %copy-start) | copy-done | bytes 3145752
  18.4 0.0 copy-start.2
  18.4 1.1 %copy-done.2 = bf16[1,384,768]{2,1,0:T(8,128)(2,1)S(1)} copy-done((bf16[1,384,768]{2,1,0:T(8,128)(2,1)S(1)}, bf16[1,384,768]{2,1,0:T(8,128)(2,1)}, u32[]{:S(2)}) %copy-start.2) | copy-done | bytes 589848
  19.5 0.0 copy-start.1
  19.5 0.0 copy-start.3
  19.5 0.9 %back.1 = (bf16[48,2048]{1,0:T(8,128)(2,1)S(1)}, bf16[48,2048]{1,0:T(8,128)(2,1)S(1)}, bf16[48,2048]{1,0:T(8,128)(2,1)S(1)}, bf16[48,2048]{1,0:T(8,128)(2,1)S(1)}) custom-call(s32[1]{0:T(128)} %bitcast.me_ref, bf16[2,2,96,768]{3,2,1,0:T(8,128)(2,1)S(1)} %bitcast.15, bf16[768,2048]{1,0:T(8,128)(2,1)S(1)} %bitcast.13), custom_call_target="tpu_custom_call" | custom-call | tf_op jit(solution)/shard_map/back/pallas_call | solution.py:123
  20.4 0.0 copy-done.5
  20.4 0.0 copy-done.6
  20.4 1.0 %copy-done.1 = bf16[1,768,2048]{2,1,0:T(8,128)(2,1)S(1)} copy-done((bf16[1,768,2048]{2,1,0:T(8,128)(2,1)S(1)}, bf16[1,768,2048]{2,1,0:T(8,128)(2,1)}, u32[]{:S(2)}) %copy-start.1) | copy-done | bytes 3145752
  21.4 1.0 %turned.1 = (bf16[2048,768]{1,0:T(8,128)(2,1)S(1)}, f32[4,48,128]{2,1,0:T(8,128)S(1)}, s32[8,128]{1,0:T(8,128)S(1)}, bf16[128,2048]{1,0:T(8,128)(2,1)S(1)}) custom-call(s32[1]{0:T(128)} %bitcast.me_ref, bf16[768,2048]{1,0:T(8,128)(2,1)S(1)} %bitcast.14, f32[8,128]{1,0:T(8,128)S(1)} %copy-done.5, bf16[8,2048]{1,0:T(8,128)(2,1)S(1)} %bitcast.19, ...), custom_call_target="tpu_custom_call" | custom-call | tf_op jit(solution)/shard_map/turned/pallas_call | solution.py:158
  22.4 0.0 collective-permute-done.3.refs_0_
  22.4 0.5 %collective-permute-start.10 = (bf16[48,2048]{1,0:T(8,128)(2,1)S(1)}, bf16[48,2048]{1,0:T(8,128)(2,1)S(1)}, u32[]{:S(2)}, u32[]{:S(2)}) collective-permute-start(bf16[48,2048]{1,0:T(8,128)(2,1)S(1)} %get-tuple-element.61), channel_id=1, source_target_pairs={{0,3},{1,2},{2,1},{3,0},{4,7},{5,6},{6,5},{7,4},{8,11},{9,10},{10,... | collective-permute-start | bytes 589832 | tf_op jit(solution)/shard_map/ppermute | solution.py:360
  22.9 0.0 collective-permute-done.4.refs_1_
  22.9 1.4 %collective-permute-start = (f32[8,128]{1,0:T(8,128)S(1)}, f32[8,128]{1,0:T(8,128)S(1)}, u32[]{:S(2)}, u32[]{:S(2)}) collective-permute-start(f32[8,128]{1,0:T(8,128)S(1)} %copy-done.5), channel_id=1, source_target_pairs={{0,6},{1,7},{2,4},{3,5},{4,2},{5,3},{6,0},{7,1},{8,14},{9,15},{10,... | collective-permute-start | bytes 12296 | tf_op jit(solution)/shard_map/ppermute | solution.py:360
  24.3 0.0 collective-permute-done.5.refs_2_
  24.3 1.6 %collective-permute-start.11 = (bf16[48,2048]{1,0:T(8,128)(2,1)S(1)}, bf16[48,2048]{1,0:T(8,128)(2,1)S(1)}, u32[]{:S(2)}, u32[]{:S(2)}) collective-permute-start(bf16[48,2048]{1,0:T(8,128)(2,1)S(1)} %get-tuple-element.62), channel_id=1, source_target_pairs={{0,2},{1,3},{2,0},{3,1},{4,6},{5,7},{6,4},{7,5},{8,10},{9,11},{10,... | collective-permute-start | bytes 589832 | tf_op jit(solution)/shard_map/ppermute | solution.py:360
  25.9 1.9 %collective-permute-done.6.refs_3_ = bf16[48,2048]{1,0:T(8,128)(2,1)S(1)} collective-permute-done((bf16[48,2048]{1,0:T(8,128)(2,1)S(1)}, bf16[48,2048]{1,0:T(8,128)(2,1)S(1)}, u32[]{:S(2)}, u32[]{:S(2)}) %collective-permute-start.6) | collective-permute-done | bytes 196640 | tf_op jit(solution)/shard_map/ppermute | solution.py:360
  27.8 0.8 %collective-permute-start.12 = (bf16[48,2048]{1,0:T(8,128)(2,1)S(1)}, bf16[48,2048]{1,0:T(8,128)(2,1)S(1)}, u32[]{:S(2)}, u32[]{:S(2)}) collective-permute-start(bf16[48,2048]{1,0:T(8,128)(2,1)S(1)} %get-tuple-element.63), channel_id=1, source_target_pairs={{0,1},{1,0},{2,3},{3,2},{4,5},{5,4},{6,7},{7,6},{8,9},{9,8},{10,11... | collective-permute-start | bytes 589832 | tf_op jit(solution)/shard_map/ppermute | solution.py:360
  28.6 0.0 copy-done.3
  28.6 1.0 %own_expert.1 = (f32[192,768]{1,0:T(8,128)S(1)}, bf16[48,128]{1,0:T(8,128)(2,1)S(1)}, bf16[48,128]{1,0:T(8,128)(2,1)S(1)}, bf16[48,128]{1,0:T(8,128)(2,1)S(1)}, bf16[48,128]{1,0:T(8,128)(2,1)S(1)}) custom-call(s32[1]{0:T(128)} %bitcast.me_ref, bf16[48,2048]{1,0:T(8,128)(2,1)S(1)} %collective-permute-done.3.refs_0_, ...), custom_call_target="tpu_custom_call" | custom-call | tf_op jit(solution)/shard_map/own_expert/pallas_call | solution.py:240
  29.7 2.5 %collective-permute-done.info_ref = f32[8,128]{1,0:T(8,128)S(1)} collective-permute-done((f32[8,128]{1,0:T(8,128)S(1)}, f32[8,128]{1,0:T(8,128)S(1)}, u32[]{:S(2)}, u32[]{:S(2)}) %collective-permute-start) | collective-permute-done | bytes 4128 | tf_op jit(solution)/shard_map/ppermute | solution.py:360
  32.1 0.0 collective-permute-done.1.token_ref
  32.1 0.5 %pack_far.1 = (bf16[48,2176]{1,0:T(8,128)(2,1)S(1)}, bf16[48,2176]{1,0:T(8,128)(2,1)S(1)}, bf16[48,2176]{1,0:T(8,128)(2,1)S(1)}, bf16[48,2176]{1,0:T(8,128)(2,1)S(1)}) custom-call(s32[1]{0:T(128)} %bitcast.me_ref, f32[8,128]{1,0:T(8,128)S(1)} %collective-permute-done.info_ref, bf16[128,2048]{1,0:T(8,128)(2,1)S(1)} %collective-permute-done.1.token_ref, ...), custom_call_target="tpu_custom_call" | custom-call | tf_op jit(solution)/shard_map/pack_far/pallas_call | solution.py:92
  32.6 0.1 collective-permute-start.7
  32.7 2.9 %collective-permute-start.8 = (bf16[48,2176]{1,0:T(8,128)(2,1)S(1)}, bf16[48,2176]{1,0:T(8,128)(2,1)S(1)}, u32[]{:S(2)}, u32[]{:S(2)}) collective-permute-start(bf16[48,2176]{1,0:T(8,128)(2,1)S(1)} %get-tuple-element.57.refs_2_), channel_id=1, source_target_pairs={{0,2},{1,3},{2,0},{3,1},{4,6},{5,7},{6,4},{7,5},{8,10},{9,11},{10,... | collective-permute-start | bytes 626696 | tf_op jit(solution)/shard_map/ppermute | solution.py:360
  35.6 0.0 collective-permute-done.10.refs_5_
  35.6 0.6 %collective-permute-start.9 = (bf16[48,2176]{1,0:T(8,128)(2,1)S(1)}, bf16[48,2176]{1,0:T(8,128)(2,1)S(1)}, u32[]{:S(2)}, u32[]{:S(2)}) collective-permute-start(bf16[48,2176]{1,0:T(8,128)(2,1)S(1)} %get-tuple-element.58.refs_1_), channel_id=1, source_target_pairs={{0,1},{1,0},{2,3},{3,2},{4,5},{5,4},{6,7},{7,6},{8,9},{9,8},{10,11... | collective-permute-start | bytes 626696 | tf_op jit(solution)/shard_map/ppermute | solution.py:360
  36.2 0.0 collective-permute-done.11.refs_6_
  36.2 0.1 collective-permute-done.12.refs_7_
  36.3 0.3 far_grad.1
  36.6 3.7 %collective-permute-start.13 = (bf16[48,128]{1,0:T(8,128)(2,1)S(1)}, bf16[48,128]{1,0:T(8,128)(2,1)S(1)}, u32[]{:S(2)}, u32[]{:S(2)}) collective-permute-start(bf16[48,128]{1,0:T(8,128)(2,1)S(1)} %far_grad.1), channel_id=1, source_target_pairs={{0,6},{1,7},{2,4},{3,5},{4,2},{5,3},{6,0},{7,1},{8,14},{9,15},{10,... | collective-permute-start | bytes 36872 | tf_op jit(solution)/shard_map/ppermute | solution.py:360
  40.3 4.2 %collective-permute-done.13.refs_7_ = bf16[48,128]{1,0:T(8,128)(2,1)S(1)} collective-permute-done((bf16[48,128]{1,0:T(8,128)(2,1)S(1)}, bf16[48,128]{1,0:T(8,128)(2,1)S(1)}, u32[]{:S(2)}, u32[]{:S(2)}) %collective-permute-start.13) | collective-permute-done | bytes 12320 | tf_op jit(solution)/shard_map/ppermute | solution.py:360
  44.4 0.0 collective-permute-done.7.refs_1_
  44.4 0.0 collective-permute-done.8.refs_2_
  44.4 0.8 %collective-permute-done.9.refs_3_ = bf16[48,2176]{1,0:T(8,128)(2,1)S(1)} collective-permute-done((bf16[48,2176]{1,0:T(8,128)(2,1)S(1)}, bf16[48,2176]{1,0:T(8,128)(2,1)S(1)}, u32[]{:S(2)}, u32[]{:S(2)}) %collective-permute-start.9) | collective-permute-done | bytes 208928 | tf_op jit(solution)/shard_map/ppermute | solution.py:360
  45.2 2.1 %last.1 = (bf16[2,2,96,768]{3,2,1,0:T(8,128)(2,1)}, bf16[128,2048]{1,0:T(8,128)(2,1)}) custom-call(s32[1]{0:T(128)} %bitcast.me_ref, bf16[48,2176]{1,0:T(8,128)(2,1)S(1)} %get-tuple-element.55.refs_0_, bf16[48,2176]{1,0:T(8,128)(2,1)S(1)} %collective-permute-done.7.refs_1_, bf16[48,2176]{1,0:T(8,128)(2,1)S(1)} %collective-permute-done.8.refs_2_, ...), custom_call_target="tpu_custom_call" | custom-call | tf_op jit(solution)/shard_map/last/pallas_call | solution.py:337
Async XLA Ops:
  0.6 31.5 %collective-permute-start.1 = (bf16[128,2048]{1,0:T(8,128)(2,1)}, bf16[128,2048]{1,0:T(8,128)(2,1)S(1)}, u32[]{:S(2)}, u32[]{:S(2)}) collective-permute-start(bf16[128,2048]{1,0:T(8,128)(2,1)} %bitcast.17), channel_id=1, source_target_pairs={{0,30},{1,31},{2,28},{3,29},{4,26},{5,27},{6,24},{7,25},{8,6},{9,7... | collective-permute-start | bytes 1572872 | tf_op jit(solution)/shard_map/ppermute | solution.py:360
  7.4 13.0 %copy-start.5 = (f32[8,128]{1,0:T(8,128)S(1)}, f32[8,128]{1,0:T(8,128)}, u32[]{:S(2)}) copy-start(f32[8,128]{1,0:T(8,128)} %info.1.info_ref.refs_6_) | copy-start | bytes 12292
  7.4 3.3 %collective-permute-start.2 = (f32[8,128]{1,0:T(8,128)}, f32[8,128]{1,0:T(8,128)S(1)}, u32[]{:S(2)}, u32[]{:S(2)}) collective-permute-start(f32[8,128]{1,0:T(8,128)} %info.1.info_ref.refs_6_), channel_id=1, source_target_pairs={{0,8},{1,9},{2,10},{3,11},{4,12},{5,13},{6,14},{7,15},{8,16},{9,17... | collective-permute-start | bytes 12296 | tf_op jit(solution)/shard_map/ppermute | solution.py:360
  10.7 1.0 %copy-start.4 = (bf16[1,128,2048]{2,1,0:T(8,128)(2,1)S(1)}, bf16[1,128,2048]{2,1,0:T(8,128)(2,1)}, u32[]{:S(2)}) copy-start(bf16[1,128,2048]{2,1,0:T(8,128)(2,1)} %param.6) | copy-start | bytes 1572868
  11.8 8.6 %copy-start.6 = (bf16[2048,8]{0,1:T(8,128)(2,1)S(1)}, bf16[2048,8]{0,1:T(8,128)(2,1)}, u32[]{:S(2)}) copy-start(bf16[2048,8]{0,1:T(8,128)(2,1)} %param.11) | copy-start | bytes 98308
  12.3 10.1 %collective-permute-start.3 = (bf16[48,2048]{1,0:T(8,128)(2,1)S(1)}, bf16[48,2048]{1,0:T(8,128)(2,1)S(1)}, u32[]{:S(2)}, u32[]{:S(2)}) collective-permute-start(bf16[48,2048]{1,0:T(8,128)(2,1)S(1)} %get-tuple-element.39.after_ref), channel_id=1, source_target_pairs={{0,24},{1,25},{2,26},{3,27},{4,28},{5,29},{6,30},{7,31},{8,0},{9,1... | collective-permute-start | bytes 589832 | tf_op jit(solution)/shard_map/ppermute | solution.py:360
  12.3 10.6 %collective-permute-start.4 = (bf16[48,2048]{1,0:T(8,128)(2,1)S(1)}, bf16[48,2048]{1,0:T(8,128)(2,1)S(1)}, u32[]{:S(2)}, u32[]{:S(2)}) collective-permute-start(bf16[48,2048]{1,0:T(8,128)(2,1)S(1)} %get-tuple-element.40), channel_id=1, source_target_pairs={{0,25},{1,24},{2,27},{3,26},{4,29},{5,28},{6,31},{7,30},{8,1},{9,0... | collective-permute-start | bytes 589832 | tf_op jit(solution)/shard_map/ppermute | solution.py:360
  13.9 10.4 %collective-permute-start.5 = (bf16[48,2048]{1,0:T(8,128)(2,1)S(1)}, bf16[48,2048]{1,0:T(8,128)(2,1)S(1)}, u32[]{:S(2)}, u32[]{:S(2)}) collective-permute-start(bf16[48,2048]{1,0:T(8,128)(2,1)S(1)} %get-tuple-element.41), channel_id=1, source_target_pairs={{0,26},{1,27},{2,24},{3,25},{4,30},{5,31},{6,28},{7,29},{8,2},{9,3... | collective-permute-start | bytes 589832 | tf_op jit(solution)/shard_map/ppermute | solution.py:360
  13.9 13.9 %collective-permute-start.6 = (bf16[48,2048]{1,0:T(8,128)(2,1)S(1)}, bf16[48,2048]{1,0:T(8,128)(2,1)S(1)}, u32[]{:S(2)}, u32[]{:S(2)}) collective-permute-start(bf16[48,2048]{1,0:T(8,128)(2,1)S(1)} %get-tuple-element.42), channel_id=1, source_target_pairs={{0,27},{1,26},{2,25},{3,24},{4,31},{5,30},{6,29},{7,28},{8,3},{9,2... | collective-permute-start | bytes 589832 | tf_op jit(solution)/shard_map/ppermute | solution.py:360
  16.5 1.9 %copy-start = (bf16[1,768,2048]{2,1,0:T(8,128)(2,1)S(1)}, bf16[1,768,2048]{2,1,0:T(8,128)(2,1)}, u32[]{:S(2)}) copy-start(bf16[1,768,2048]{2,1,0:T(8,128)(2,1)} %param.10) | copy-start | bytes 9437188
  18.4 1.1 %copy-start.2 = (bf16[1,384,768]{2,1,0:T(8,128)(2,1)S(1)}, bf16[1,384,768]{2,1,0:T(8,128)(2,1)}, u32[]{:S(2)}) copy-start(bf16[1,384,768]{2,1,0:T(8,128)(2,1)} %param.9) | copy-start | bytes 1769476
  19.5 1.9 %copy-start.1 = (bf16[1,768,2048]{2,1,0:T(8,128)(2,1)S(1)}, bf16[1,768,2048]{2,1,0:T(8,128)(2,1)}, u32[]{:S(2)}) copy-start(bf16[1,768,2048]{2,1,0:T(8,128)(2,1)} %param.10) | copy-start | bytes 9437188
  19.5 9.2 %copy-start.3 = (bf16[1,384,768]{2,1,0:T(8,128)(2,1)S(1)}, bf16[1,384,768]{2,1,0:T(8,128)(2,1)}, u32[]{:S(2)}) copy-start(bf16[1,384,768]{2,1,0:T(8,128)(2,1)} %param.9) | copy-start | bytes 1769476
  22.4 13.2 %collective-permute-start.10 = (bf16[48,2048]{1,0:T(8,128)(2,1)S(1)}, bf16[48,2048]{1,0:T(8,128)(2,1)S(1)}, u32[]{:S(2)}, u32[]{:S(2)}) collective-permute-start(bf16[48,2048]{1,0:T(8,128)(2,1)S(1)} %get-tuple-element.61), channel_id=1, source_target_pairs={{0,3},{1,2},{2,1},{3,0},{4,7},{5,6},{6,5},{7,4},{8,11},{9,10},{10,... | collective-permute-start | bytes 589832 | tf_op jit(solution)/shard_map/ppermute | solution.py:360
  22.9 9.2 %collective-permute-start = (f32[8,128]{1,0:T(8,128)S(1)}, f32[8,128]{1,0:T(8,128)S(1)}, u32[]{:S(2)}, u32[]{:S(2)}) collective-permute-start(f32[8,128]{1,0:T(8,128)S(1)} %copy-done.5), channel_id=1, source_target_pairs={{0,6},{1,7},{2,4},{3,5},{4,2},{5,3},{6,0},{7,1},{8,14},{9,15},{10,... | collective-permute-start | bytes 12296 | tf_op jit(solution)/shard_map/ppermute | solution.py:360
  24.3 11.9 %collective-permute-start.11 = (bf16[48,2048]{1,0:T(8,128)(2,1)S(1)}, bf16[48,2048]{1,0:T(8,128)(2,1)S(1)}, u32[]{:S(2)}, u32[]{:S(2)}) collective-permute-start(bf16[48,2048]{1,0:T(8,128)(2,1)S(1)} %get-tuple-element.62), channel_id=1, source_target_pairs={{0,2},{1,3},{2,0},{3,1},{4,6},{5,7},{6,4},{7,5},{8,10},{9,11},{10,... | collective-permute-start | bytes 589832 | tf_op jit(solution)/shard_map/ppermute | solution.py:360
  27.8 8.5 %collective-permute-start.12 = (bf16[48,2048]{1,0:T(8,128)(2,1)S(1)}, bf16[48,2048]{1,0:T(8,128)(2,1)S(1)}, u32[]{:S(2)}, u32[]{:S(2)}) collective-permute-start(bf16[48,2048]{1,0:T(8,128)(2,1)S(1)} %get-tuple-element.63), channel_id=1, source_target_pairs={{0,1},{1,0},{2,3},{3,2},{4,5},{5,4},{6,7},{7,6},{8,9},{9,8},{10,11... | collective-permute-start | bytes 589832 | tf_op jit(solution)/shard_map/ppermute | solution.py:360
  32.6 11.8 %collective-permute-start.7 = (bf16[48,2176]{1,0:T(8,128)(2,1)S(1)}, bf16[48,2176]{1,0:T(8,128)(2,1)S(1)}, u32[]{:S(2)}, u32[]{:S(2)}) collective-permute-start(bf16[48,2176]{1,0:T(8,128)(2,1)S(1)} %get-tuple-element.56.refs_3_), channel_id=1, source_target_pairs={{0,3},{1,2},{2,1},{3,0},{4,7},{5,6},{6,5},{7,4},{8,11},{9,10},{10,... | collective-permute-start | bytes 626696 | tf_op jit(solution)/shard_map/ppermute | solution.py:360
  32.7 11.8 %collective-permute-start.8 = (bf16[48,2176]{1,0:T(8,128)(2,1)S(1)}, bf16[48,2176]{1,0:T(8,128)(2,1)S(1)}, u32[]{:S(2)}, u32[]{:S(2)}) collective-permute-start(bf16[48,2176]{1,0:T(8,128)(2,1)S(1)} %get-tuple-element.57.refs_2_), channel_id=1, source_target_pairs={{0,2},{1,3},{2,0},{3,1},{4,6},{5,7},{6,4},{7,5},{8,10},{9,11},{10,... | collective-permute-start | bytes 626696 | tf_op jit(solution)/shard_map/ppermute | solution.py:360
  35.6 9.6 %collective-permute-start.9 = (bf16[48,2176]{1,0:T(8,128)(2,1)S(1)}, bf16[48,2176]{1,0:T(8,128)(2,1)S(1)}, u32[]{:S(2)}, u32[]{:S(2)}) collective-permute-start(bf16[48,2176]{1,0:T(8,128)(2,1)S(1)} %get-tuple-element.58.refs_1_), channel_id=1, source_target_pairs={{0,1},{1,0},{2,3},{3,2},{4,5},{5,4},{6,7},{7,6},{8,9},{9,8},{10,11... | collective-permute-start | bytes 626696 | tf_op jit(solution)/shard_map/ppermute | solution.py:360
  36.6 7.8 %collective-permute-start.13 = (bf16[48,128]{1,0:T(8,128)(2,1)S(1)}, bf16[48,128]{1,0:T(8,128)(2,1)S(1)}, u32[]{:S(2)}, u32[]{:S(2)}) collective-permute-start(bf16[48,128]{1,0:T(8,128)(2,1)S(1)} %far_grad.1), channel_id=1, source_target_pairs={{0,6},{1,7},{2,4},{3,5},{4,2},{5,3},{6,0},{7,1},{8,14},{9,15},{10,... | collective-permute-start | bytes 36872 | tf_op jit(solution)/shard_map/ppermute | solution.py:360

commit v9 on v7

--- a/solution.py
+++ b/solution.py
@@ -286,9 +286,7 @@
     me = me_ref[0]
     side = me // half
     tails = [block[:, width:].astype(F32) for block in blocks]
-    rows[...] = router_rows(half, capacity, turn, me, info_ref, tails, far_ref, rank_ref[...], table_ref)
-    copies = [pltpu.make_async_copy(rows, out_ref, row_sem)]
-    copies[0].start()
+    copies = []
     here = lax.rem(me, half)
 
     def spread_scale(lane_of, slots):
@@ -316,6 +314,12 @@
 
     spread_scale(SCALE - 1, slots_of(here))
     scaled(0, own_ref, pl.ds(0, hidden_width))
+    rows[...] = router_rows(half, capacity, turn, me, info_ref, tails, far_ref, rank_ref[...], table_ref)
+    cut = out_ref.shape[1] // 2
+    for i in range(2):
+        columns = pl.ds(i * cut, cut)
+        copies.append(pltpu.make_async_copy(rows.at[:, columns], out_ref.at[:, columns], row_sem.at[i]))
+        copies[-1].start()
     far_slots = slots_of(jnp.bitwise_xor(here, turn))
     spread_scale(SCALE, far_slots)
     for j in range(half):
@@ -346,7 +350,7 @@
             pltpu.VMEM((MICRO * run, LANES), F32),
             pltpu.VMEM(tokens.shape, BF16),
             pltpu.VMEM((2, MICRO, run, hidden_width), BF16),
-            pltpu.SemaphoreType.DMA,
+            pltpu.SemaphoreType.DMA((2,)),
             pltpu.SemaphoreType.DMA((2, MICRO, len(chunks(hidden_width)))),
         ],
         compiler_params=pltpu.CompilerParams(vmem_limit_bytes=VMEM_LIMIT),

time: 47.6 us -> 47.6 us (level)
  no operation moved by 1% of the time
where the time goes in v9:
time: 47.6 us; the launch traced here: 47.3 us
  starting transfers between devices  21.6 us (45%)
  waiting for transfers between devices  13.5 us (28%)
  Pallas kernels  7.54 us (16%)
  local copies, waits for them, and re-layouts  4.01 us (8%)
  between operations  0.71 us (1%)
    ppermute x14, starting transfers between devices, route(): return lax.ppermute(block, ('pipe', 'expert'), pairs)  21.6 us
    ppermute x14, waiting for transfers between devices, route(): return lax.ppermute(block, ('pipe', 'expert'), pairs)  13.5 us
    unnamed x14, local copies, waits for them, and re-layouts  4.01 us
    pallas_call x1, Pallas kernels, last(): pl.pallas_call(functools.partial(last_kernel, half, capacity, turn), out_...  2.06 us
    pallas_call x1, Pallas kernels, by_halves(): pl.pallas_call(info_kernel, out_shape=jax.ShapeDtypeStruct((8, LANES), F3...  1.31 us
    pallas_call x1, Pallas kernels, own_expert(): pl.pallas_call(functools.partial(own_kernel, half, capacity), out_shape=[...  1.01 us
    pallas_call x1, Pallas kernels, turned(): pl.pallas_call(functools.partial(turn_kernel, half, capacity), out_shape=...  0.98 us
    pallas_call x2, Pallas kernels, pack(): pl.pallas_call(functools.partial(pack_kernel, half, capacity), out_shape=...  0.97 us
  transfers between devices with their start and end apart: 14, of which 8 were waited for; matrix products, arithmetic and copies ran while one was open for 0% of the time, Pallas kernels for 12%

profile of v9, /device:TPU:0, one launch (start us, length us, event | category | flops | bytes accessed | tf_op | source)
XLA Modules:
  0.0 47.3 jit_solution(16367265424122910598)
XLA Ops:
  0.6 5.5 %collective-permute-start.1 = (bf16[128,2048]{1,0:T(8,128)(2,1)}, bf16[128,2048]{1,0:T(8,128)(2,1)S(1)}, u32[]{:S(2)}, u32[]{:S(2)}) collective-permute-start(bf16[128,2048]{1,0:T(8,128)(2,1)} %bitcast.17), channel_id=1, source_target_pairs={{0,30},{1,31},{2,28},{3,29},{4,26},{5,27},{6,24},{7,25},{8,6},{9,7... | collective-permute-start | bytes 1572872 | tf_op jit(solution)/shard_map/ppermute | solution.py:366
  6.1 1.3 %info.1.info_ref.refs_6_ = f32[8,128]{1,0:T(8,128)} custom-call(s32[2,128]{1,0:T(2,128)} %bitcast.21, f32[8,128]{1,0:T(8,128)} %bitcast.20), custom_call_target="tpu_custom_call" | custom-call | tf_op jit(solution)/shard_map/info/pallas_call | solution.py:382
  7.4 0.0 copy-start.5
  7.4 0.0 collective-permute-start.2
  7.4 3.3 %collective-permute-done.2.info_ref = f32[8,128]{1,0:T(8,128)S(1)} collective-permute-done((f32[8,128]{1,0:T(8,128)}, f32[8,128]{1,0:T(8,128)S(1)}, u32[]{:S(2)}, u32[]{:S(2)}) %collective-permute-start.2) | collective-permute-done | bytes 4128 | tf_op jit(solution)/shard_map/ppermute | solution.py:366
  10.7 0.0 copy-start.4
  10.7 1.0 %copy-done.4 = bf16[1,128,2048]{2,1,0:T(8,128)(2,1)S(1)} copy-done((bf16[1,128,2048]{2,1,0:T(8,128)(2,1)S(1)}, bf16[1,128,2048]{2,1,0:T(8,128)(2,1)}, u32[]{:S(2)}) %copy-start.4) | copy-done | bytes 524312
  11.8 0.0 copy-start.6
  11.8 0.5 %pack_own.1 = (bf16[48,2048]{1,0:T(8,128)(2,1)S(1)}, bf16[48,2048]{1,0:T(8,128)(2,1)S(1)}, bf16[48,2048]{1,0:T(8,128)(2,1)S(1)}, bf16[48,2048]{1,0:T(8,128)(2,1)S(1)}) custom-call(s32[1]{0:T(128)} %bitcast.me_ref, f32[8,128]{1,0:T(8,128)S(1)} %collective-permute-done.2.info_ref, bf16[128,2048]{1,0:T(8,128)(2,1)S(1)} %bitcast.18), custom_call_target="tpu_custom_call" | custom-call | tf_op jit(solution)/shard_map/pack_own/pallas_call | solution.py:92
  12.3 0.1 collective-permute-start.3
  12.3 1.5 %collective-permute-start.4 = (bf16[48,2048]{1,0:T(8,128)(2,1)S(1)}, bf16[48,2048]{1,0:T(8,128)(2,1)S(1)}, u32[]{:S(2)}, u32[]{:S(2)}) collective-permute-start(bf16[48,2048]{1,0:T(8,128)(2,1)S(1)} %get-tuple-element.35), channel_id=1, source_target_pairs={{0,25},{1,24},{2,27},{3,26},{4,29},{5,28},{6,31},{7,30},{8,1},{9,0... | collective-permute-start | bytes 589832 | tf_op jit(solution)/shard_map/ppermute | solution.py:366
  13.9 0.0 collective-permute-start.5
  13.9 2.7 %collective-permute-start.6 = (bf16[48,2048]{1,0:T(8,128)(2,1)S(1)}, bf16[48,2048]{1,0:T(8,128)(2,1)S(1)}, u32[]{:S(2)}, u32[]{:S(2)}) collective-permute-start(bf16[48,2048]{1,0:T(8,128)(2,1)S(1)} %get-tuple-element.37), channel_id=1, source_target_pairs={{0,27},{1,26},{2,25},{3,24},{4,31},{5,30},{6,29},{7,28},{8,3},{9,2... | collective-permute-start | bytes 589832 | tf_op jit(solution)/shard_map/ppermute | solution.py:366
  16.5 0.0 copy-start
  16.5 1.9 %copy-done = bf16[1,768,2048]{2,1,0:T(8,128)(2,1)S(1)} copy-done((bf16[1,768,2048]{2,1,0:T(8,128)(2,1)S(1)}, bf16[1,768,2048]{2,1,0:T(8,128)(2,1)}, u32[]{:S(2)}) %copy-start) | copy-done | bytes 3145752
  18.4 0.0 copy-start.2
  18.4 1.1 %copy-done.2 = bf16[1,384,768]{2,1,0:T(8,128)(2,1)S(1)} copy-done((bf16[1,384,768]{2,1,0:T(8,128)(2,1)S(1)}, bf16[1,384,768]{2,1,0:T(8,128)(2,1)}, u32[]{:S(2)}) %copy-start.2) | copy-done | bytes 589848
  19.5 0.0 copy-start.1
  19.5 0.0 copy-start.3
  19.5 0.9 %back.1 = (bf16[48,2048]{1,0:T(8,128)(2,1)S(1)}, bf16[48,2048]{1,0:T(8,128)(2,1)S(1)}, bf16[48,2048]{1,0:T(8,128)(2,1)S(1)}, bf16[48,2048]{1,0:T(8,128)(2,1)S(1)}) custom-call(s32[1]{0:T(128)} %bitcast.me_ref, bf16[2,2,96,768]{3,2,1,0:T(8,128)(2,1)S(1)} %bitcast.15, bf16[768,2048]{1,0:T(8,128)(2,1)S(1)} %bitcast.13), custom_call_target="tpu_custom_call" | custom-call | tf_op jit(solution)/shard_map/back/pallas_call | solution.py:123
  20.4 1.8 %collective-permute-done.3.refs_0_ = bf16[48,2048]{1,0:T(8,128)(2,1)S(1)} collective-permute-done((bf16[48,2048]{1,0:T(8,128)(2,1)S(1)}, bf16[48,2048]{1,0:T(8,128)(2,1)S(1)}, u32[]{:S(2)}, u32[]{:S(2)}) %collective-permute-start.3) | collective-permute-done | bytes 196640 | tf_op jit(solution)/shard_map/ppermute | solution.py:366
  22.2 0.0 collective-permute-start.10
  22.2 0.0 collective-permute-done.4.refs_1_
  22.2 0.0 copy-done.5
  22.2 0.6 %collective-permute-start = (f32[8,128]{1,0:T(8,128)S(1)}, f32[8,128]{1,0:T(8,128)S(1)}, u32[]{:S(2)}, u32[]{:S(2)}) collective-permute-start(f32[8,128]{1,0:T(8,128)S(1)} %copy-done.5), channel_id=1, source_target_pairs={{0,6},{1,7},{2,4},{3,5},{4,2},{5,3},{6,0},{7,1},{8,14},{9,15},{10,... | collective-permute-start | bytes 12296 | tf_op jit(solution)/shard_map/ppermute | solution.py:366
  22.9 0.0 copy-done.6
  22.9 0.0 copy-done.1
  22.9 1.0 %turned.1 = (bf16[2048,768]{1,0:T(8,128)(2,1)S(1)}, f32[4,48,128]{2,1,0:T(8,128)S(1)}, s32[8,128]{1,0:T(8,128)S(1)}, bf16[128,2048]{1,0:T(8,128)(2,1)S(1)}) custom-call(s32[1]{0:T(128)} %bitcast.me_ref, bf16[768,2048]{1,0:T(8,128)(2,1)S(1)} %bitcast.14, f32[8,128]{1,0:T(8,128)S(1)} %copy-done.5, bf16[8,2048]{1,0:T(8,128)(2,1)S(1)} %bitcast.19, ...), custom_call_target="tpu_custom_call" | custom-call | tf_op jit(solution)/shard_map/turned/pallas_call | solution.py:158
  23.9 0.0 collective-permute-done.5.refs_2_
  23.9 3.0 %collective-permute-start.11 = (bf16[48,2048]{1,0:T(8,128)(2,1)S(1)}, bf16[48,2048]{1,0:T(8,128)(2,1)S(1)}, u32[]{:S(2)}, u32[]{:S(2)}) collective-permute-start(bf16[48,2048]{1,0:T(8,128)(2,1)S(1)} %get-tuple-element.52), channel_id=1, source_target_pairs={{0,2},{1,3},{2,0},{3,1},{4,6},{5,7},{6,4},{7,5},{8,10},{9,11},{10,... | collective-permute-start | bytes 589832 | tf_op jit(solution)/shard_map/ppermute | solution.py:366
  26.9 0.9 %collective-permute-done.6.refs_3_ = bf16[48,2048]{1,0:T(8,128)(2,1)S(1)} collective-permute-done((bf16[48,2048]{1,0:T(8,128)(2,1)S(1)}, bf16[48,2048]{1,0:T(8,128)(2,1)S(1)}, u32[]{:S(2)}, u32[]{:S(2)}) %collective-permute-start.6) | collective-permute-done | bytes 196640 | tf_op jit(solution)/shard_map/ppermute | solution.py:366
  27.8 0.8 %collective-permute-start.12 = (bf16[48,2048]{1,0:T(8,128)(2,1)S(1)}, bf16[48,2048]{1,0:T(8,128)(2,1)S(1)}, u32[]{:S(2)}, u32[]{:S(2)}) collective-permute-start(bf16[48,2048]{1,0:T(8,128)(2,1)S(1)} %get-tuple-element.53), channel_id=1, source_target_pairs={{0,1},{1,0},{2,3},{3,2},{4,5},{5,4},{6,7},{7,6},{8,9},{9,8},{10,11... | collective-permute-start | bytes 589832 | tf_op jit(solution)/shard_map/ppermute | solution.py:366
  28.6 0.0 copy-done.3
  28.6 1.0 %own_expert.1 = (f32[192,768]{1,0:T(8,128)S(1)}, bf16[48,128]{1,0:T(8,128)(2,1)S(1)}, bf16[48,128]{1,0:T(8,128)(2,1)S(1)}, bf16[48,128]{1,0:T(8,128)(2,1)S(1)}, bf16[48,128]{1,0:T(8,128)(2,1)S(1)}) custom-call(s32[1]{0:T(128)} %bitcast.me_ref, bf16[48,2048]{1,0:T(8,128)(2,1)S(1)} %collective-permute-done.3.refs_0_, ...), custom_call_target="tpu_custom_call" | custom-call | tf_op jit(solution)/shard_map/own_expert/pallas_call | solution.py:240
  29.7 1.8 %collective-permute-done.info_ref = f32[8,128]{1,0:T(8,128)S(1)} collective-permute-done((f32[8,128]{1,0:T(8,128)S(1)}, f32[8,128]{1,0:T(8,128)S(1)}, u32[]{:S(2)}, u32[]{:S(2)}) %collective-permute-start) | collective-permute-done | bytes 4128 | tf_op jit(solution)/shard_map/ppermute | solution.py:366
  31.5 0.0 collective-permute-done.1.token_ref
  31.5 0.5 %pack_far.1 = (bf16[48,2176]{1,0:T(8,128)(2,1)S(1)}, bf16[48,2176]{1,0:T(8,128)(2,1)S(1)}, bf16[48,2176]{1,0:T(8,128)(2,1)S(1)}, bf16[48,2176]{1,0:T(8,128)(2,1)S(1)}) custom-call(s32[1]{0:T(128)} %bitcast.me_ref, f32[8,128]{1,0:T(8,128)S(1)} %collective-permute-done.info_ref, bf16[128,2048]{1,0:T(8,128)(2,1)S(1)} %collective-permute-done.1.token_ref, ...), custom_call_target="tpu_custom_call" | custom-call | tf_op jit(solution)/shard_map/pack_far/pallas_call | solution.py:92
  32.0 0.1 collective-permute-start.7
  32.0 3.6 %collective-permute-start.8 = (bf16[48,2176]{1,0:T(8,128)(2,1)S(1)}, bf16[48,2176]{1,0:T(8,128)(2,1)S(1)}, u32[]{:S(2)}, u32[]{:S(2)}) collective-permute-start(bf16[48,2176]{1,0:T(8,128)(2,1)S(1)} %get-tuple-element.47.refs_2_), channel_id=1, source_target_pairs={{0,2},{1,3},{2,0},{3,1},{4,6},{5,7},{6,4},{7,5},{8,10},{9,11},{10,... | collective-permute-start | bytes 626696 | tf_op jit(solution)/shard_map/ppermute | solution.py:366
  35.6 0.0 collective-permute-done.10.refs_5_
  35.6 0.0 collective-permute-start.9
  35.6 0.2 collective-permute-done.11.refs_6_
  35.8 0.5 %collective-permute-done.12.refs_7_ = bf16[48,2048]{1,0:T(8,128)(2,1)S(1)} collective-permute-done((bf16[48,2048]{1,0:T(8,128)(2,1)S(1)}, bf16[48,2048]{1,0:T(8,128)(2,1)S(1)}, u32[]{:S(2)}, u32[]{:S(2)}) %collective-permute-start.12) | collective-permute-done | bytes 196640 | tf_op jit(solution)/shard_map/ppermute | solution.py:366
  36.3 0.3 far_grad.1
  36.6 3.7 %collective-permute-start.13 = (bf16[48,128]{1,0:T(8,128)(2,1)S(1)}, bf16[48,128]{1,0:T(8,128)(2,1)S(1)}, u32[]{:S(2)}, u32[]{:S(2)}) collective-permute-start(bf16[48,128]{1,0:T(8,128)(2,1)S(1)} %far_grad.1), channel_id=1, source_target_pairs={{0,6},{1,7},{2,4},{3,5},{4,2},{5,3},{6,0},{7,1},{8,14},{9,15},{10,... | collective-permute-start | bytes 36872 | tf_op jit(solution)/shard_map/ppermute | solution.py:366
  40.3 4.2 %collective-permute-done.13.refs_7_ = bf16[48,128]{1,0:T(8,128)(2,1)S(1)} collective-permute-done((bf16[48,128]{1,0:T(8,128)(2,1)S(1)}, bf16[48,128]{1,0:T(8,128)(2,1)S(1)}, u32[]{:S(2)}, u32[]{:S(2)}) %collective-permute-start.13) | collective-permute-done | bytes 12320 | tf_op jit(solution)/shard_map/ppermute | solution.py:366
  44.4 0.0 collective-permute-done.7.refs_1_
  44.4 0.0 collective-permute-done.8.refs_2_
  44.4 0.8 %collective-permute-done.9.refs_3_ = bf16[48,2176]{1,0:T(8,128)(2,1)S(1)} collective-permute-done((bf16[48,2176]{1,0:T(8,128)(2,1)S(1)}, bf16[48,2176]{1,0:T(8,128)(2,1)S(1)}, u32[]{:S(2)}, u32[]{:S(2)}) %collective-permute-start.9) | collective-permute-done | bytes 208928 | tf_op jit(solution)/shard_map/ppermute | solution.py:366
  45.2 2.1 %last.1 = (bf16[2,2,96,768]{3,2,1,0:T(8,128)(2,1)}, bf16[128,2048]{1,0:T(8,128)(2,1)}) custom-call(s32[1]{0:T(128)} %bitcast.me_ref, bf16[48,2176]{1,0:T(8,128)(2,1)S(1)} %get-tuple-element.45.refs_0_, bf16[48,2176]{1,0:T(8,128)(2,1)S(1)} %collective-permute-done.7.refs_1_, bf16[48,2176]{1,0:T(8,128)(2,1)S(1)} %collective-permute-done.8.refs_2_, ...), custom_call_target="tpu_custom_call" | custom-call | tf_op jit(solution)/shard_map/last/pallas_call | solution.py:342
Async XLA Ops:
  0.6 30.8 %collective-permute-start.1 = (bf16[128,2048]{1,0:T(8,128)(2,1)}, bf16[128,2048]{1,0:T(8,128)(2,1)S(1)}, u32[]{:S(2)}, u32[]{:S(2)}) collective-permute-start(bf16[128,2048]{1,0:T(8,128)(2,1)} %bitcast.17), channel_id=1, source_target_pairs={{0,30},{1,31},{2,28},{3,29},{4,26},{5,27},{6,24},{7,25},{8,6},{9,7... | collective-permute-start | bytes 1572872 | tf_op jit(solution)/shard_map/ppermute | solution.py:366
  7.4 14.8 %copy-start.5 = (f32[8,128]{1,0:T(8,128)S(1)}, f32[8,128]{1,0:T(8,128)}, u32[]{:S(2)}) copy-start(f32[8,128]{1,0:T(8,128)} %info.1.info_ref.refs_6_) | copy-start | bytes 12292
  7.4 3.3 %collective-permute-start.2 = (f32[8,128]{1,0:T(8,128)}, f32[8,128]{1,0:T(8,128)S(1)}, u32[]{:S(2)}, u32[]{:S(2)}) collective-permute-start(f32[8,128]{1,0:T(8,128)} %info.1.info_ref.refs_6_), channel_id=1, source_target_pairs={{0,8},{1,9},{2,10},{3,11},{4,12},{5,13},{6,14},{7,15},{8,16},{9,17... | collective-permute-start | bytes 12296 | tf_op jit(solution)/shard_map/ppermute | solution.py:366
  10.7 1.0 %copy-start.4 = (bf16[1,128,2048]{2,1,0:T(8,128)(2,1)S(1)}, bf16[1,128,2048]{2,1,0:T(8,128)(2,1)}, u32[]{:S(2)}) copy-start(bf16[1,128,2048]{2,1,0:T(8,128)(2,1)} %param.6) | copy-start | bytes 1572868
  11.8 11.1 %copy-start.6 = (bf16[2048,8]{0,1:T(8,128)(2,1)S(1)}, bf16[2048,8]{0,1:T(8,128)(2,1)}, u32[]{:S(2)}) copy-start(bf16[2048,8]{0,1:T(8,128)(2,1)} %param.11) | copy-start | bytes 98308
  12.3 10.0 %collective-permute-start.3 = (bf16[48,2048]{1,0:T(8,128)(2,1)S(1)}, bf16[48,2048]{1,0:T(8,128)(2,1)S(1)}, u32[]{:S(2)}, u32[]{:S(2)}) collective-permute-start(bf16[48,2048]{1,0:T(8,128)(2,1)S(1)} %get-tuple-element.34.after_ref), channel_id=1, source_target_pairs={{0,24},{1,25},{2,26},{3,27},{4,28},{5,29},{6,30},{7,31},{8,0},{9,1... | collective-permute-start | bytes 589832 | tf_op jit(solution)/shard_map/ppermute | solution.py:366
  12.3 9.9 %collective-permute-start.4 = (bf16[48,2048]{1,0:T(8,128)(2,1)S(1)}, bf16[48,2048]{1,0:T(8,128)(2,1)S(1)}, u32[]{:S(2)}, u32[]{:S(2)}) collective-permute-start(bf16[48,2048]{1,0:T(8,128)(2,1)S(1)} %get-tuple-element.35), channel_id=1, source_target_pairs={{0,25},{1,24},{2,27},{3,26},{4,29},{5,28},{6,31},{7,30},{8,1},{9,0... | collective-permute-start | bytes 589832 | tf_op jit(solution)/shard_map/ppermute | solution.py:366
  13.9 10.0 %collective-permute-start.5 = (bf16[48,2048]{1,0:T(8,128)(2,1)S(1)}, bf16[48,2048]{1,0:T(8,128)(2,1)S(1)}, u32[]{:S(2)}, u32[]{:S(2)}) collective-permute-start(bf16[48,2048]{1,0:T(8,128)(2,1)S(1)} %get-tuple-element.36), channel_id=1, source_target_pairs={{0,26},{1,27},{2,24},{3,25},{4,30},{5,31},{6,28},{7,29},{8,2},{9,3... | collective-permute-start | bytes 589832 | tf_op jit(solution)/shard_map/ppermute | solution.py:366
  13.9 13.9 %collective-permute-start.6 = (bf16[48,2048]{1,0:T(8,128)(2,1)S(1)}, bf16[48,2048]{1,0:T(8,128)(2,1)S(1)}, u32[]{:S(2)}, u32[]{:S(2)}) collective-permute-start(bf16[48,2048]{1,0:T(8,128)(2,1)S(1)} %get-tuple-element.37), channel_id=1, source_target_pairs={{0,27},{1,26},{2,25},{3,24},{4,31},{5,30},{6,29},{7,28},{8,3},{9,2... | collective-permute-start | bytes 589832 | tf_op jit(solution)/shard_map/ppermute | solution.py:366
  16.5 1.9 %copy-start = (bf16[1,768,2048]{2,1,0:T(8,128)(2,1)S(1)}, bf16[1,768,2048]{2,1,0:T(8,128)(2,1)}, u32[]{:S(2)}) copy-start(bf16[1,768,2048]{2,1,0:T(8,128)(2,1)} %param.10) | copy-start | bytes 9437188
  18.4 1.1 %copy-start.2 = (bf16[1,384,768]{2,1,0:T(8,128)(2,1)S(1)}, bf16[1,384,768]{2,1,0:T(8,128)(2,1)}, u32[]{:S(2)}) copy-start(bf16[1,384,768]{2,1,0:T(8,128)(2,1)} %param.9) | copy-start | bytes 1769476
  19.5 3.4 %copy-start.1 = (bf16[1,768,2048]{2,1,0:T(8,128)(2,1)S(1)}, bf16[1,768,2048]{2,1,0:T(8,128)(2,1)}, u32[]{:S(2)}) copy-start(bf16[1,768,2048]{2,1,0:T(8,128)(2,1)} %param.10) | copy-start | bytes 9437188
  19.5 9.2 %copy-start.3 = (bf16[1,384,768]{2,1,0:T(8,128)(2,1)S(1)}, bf16[1,384,768]{2,1,0:T(8,128)(2,1)}, u32[]{:S(2)}) copy-start(bf16[1,384,768]{2,1,0:T(8,128)(2,1)} %param.9) | copy-start | bytes 1769476
  22.2 13.4 %collective-permute-start.10 = (bf16[48,2048]{1,0:T(8,128)(2,1)S(1)}, bf16[48,2048]{1,0:T(8,128)(2,1)S(1)}, u32[]{:S(2)}, u32[]{:S(2)}) collective-permute-start(bf16[48,2048]{1,0:T(8,128)(2,1)S(1)} %get-tuple-element.51), channel_id=1, source_target_pairs={{0,3},{1,2},{2,1},{3,0},{4,7},{5,6},{6,5},{7,4},{8,11},{9,10},{10,... | collective-permute-start | bytes 589832 | tf_op jit(solution)/shard_map/ppermute | solution.py:366
  22.2 9.2 %collective-permute-start = (f32[8,128]{1,0:T(8,128)S(1)}, f32[8,128]{1,0:T(8,128)S(1)}, u32[]{:S(2)}, u32[]{:S(2)}) collective-permute-start(f32[8,128]{1,0:T(8,128)S(1)} %copy-done.5), channel_id=1, source_target_pairs={{0,6},{1,7},{2,4},{3,5},{4,2},{5,3},{6,0},{7,1},{8,14},{9,15},{10,... | collective-permute-start | bytes 12296 | tf_op jit(solution)/shard_map/ppermute | solution.py:366
  23.9 11.9 %collective-permute-start.11 = (bf16[48,2048]{1,0:T(8,128)(2,1)S(1)}, bf16[48,2048]{1,0:T(8,128)(2,1)S(1)}, u32[]{:S(2)}, u32[]{:S(2)}) collective-permute-start(bf16[48,2048]{1,0:T(8,128)(2,1)S(1)} %get-tuple-element.52), channel_id=1, source_target_pairs={{0,2},{1,3},{2,0},{3,1},{4,6},{5,7},{6,4},{7,5},{8,10},{9,11},{10,... | collective-permute-start | bytes 589832 | tf_op jit(solution)/shard_map/ppermute | solution.py:366
  27.8 8.5 %collective-permute-start.12 = (bf16[48,2048]{1,0:T(8,128)(2,1)S(1)}, bf16[48,2048]{1,0:T(8,128)(2,1)S(1)}, u32[]{:S(2)}, u32[]{:S(2)}) collective-permute-start(bf16[48,2048]{1,0:T(8,128)(2,1)S(1)} %get-tuple-element.53), channel_id=1, source_target_pairs={{0,1},{1,0},{2,3},{3,2},{4,5},{5,4},{6,7},{7,6},{8,9},{9,8},{10,11... | collective-permute-start | bytes 589832 | tf_op jit(solution)/shard_map/ppermute | solution.py:366
  32.0 12.5 %collective-permute-start.7 = (bf16[48,2176]{1,0:T(8,128)(2,1)S(1)}, bf16[48,2176]{1,0:T(8,128)(2,1)S(1)}, u32[]{:S(2)}, u32[]{:S(2)}) collective-permute-start(bf16[48,2176]{1,0:T(8,128)(2,1)S(1)} %get-tuple-element.46.refs_3_), channel_id=1, source_target_pairs={{0,3},{1,2},{2,1},{3,0},{4,7},{5,6},{6,5},{7,4},{8,11},{9,10},{10,... | collective-permute-start | bytes 626696 | tf_op jit(solution)/shard_map/ppermute | solution.py:366
  32.0 12.4 %collective-permute-start.8 = (bf16[48,2176]{1,0:T(8,128)(2,1)S(1)}, bf16[48,2176]{1,0:T(8,128)(2,1)S(1)}, u32[]{:S(2)}, u32[]{:S(2)}) collective-permute-start(bf16[48,2176]{1,0:T(8,128)(2,1)S(1)} %get-tuple-element.47.refs_2_), channel_id=1, source_target_pairs={{0,2},{1,3},{2,0},{3,1},{4,6},{5,7},{6,4},{7,5},{8,10},{9,11},{10,... | collective-permute-start | bytes 626696 | tf_op jit(solution)/shard_map/ppermute | solution.py:366
  35.6 9.6 %collective-permute-start.9 = (bf16[48,2176]{1,0:T(8,128)(2,1)S(1)}, bf16[48,2176]{1,0:T(8,128)(2,1)S(1)}, u32[]{:S(2)}, u32[]{:S(2)}) collective-permute-start(bf16[48,2176]{1,0:T(8,128)(2,1)S(1)} %get-tuple-element.48.refs_1_), channel_id=1, source_target_pairs={{0,1},{1,0},{2,3},{3,2},{4,5},{5,4},{6,7},{7,6},{8,9},{9,8},{10,11... | collective-permute-start | bytes 626696 | tf_op jit(solution)/shard_map/ppermute | solution.py:366
  36.6 7.8 %collective-permute-start.13 = (bf16[48,128]{1,0:T(8,128)(2,1)S(1)}, bf16[48,128]{1,0:T(8,128)(2,1)S(1)}, u32[]{:S(2)}, u32[]{:S(2)}) collective-permute-start(bf16[48,128]{1,0:T(8,128)(2,1)S(1)} %far_grad.1), channel_id=1, source_target_pairs={{0,6},{1,7},{2,4},{3,5},{4,2},{5,3},{6,0},{7,1},{8,14},{9,15},{10,... | collective-permute-start | bytes 36872 | tf_op jit(solution)/shard_map/ppermute | solution.py:366
